TPU v7x, 32 devices: a whole 2x2x4 slice. The times are simulated.
32 devices in a mesh: dp: 8 (over z, core), space: 4 (over y, x).
Axes of the slice: x: 2, y: 2, z: 4, core: 2. Of those that a mesh axis runs over, the one named last changes fastest.
Arguments:
- features: bfloat16 [8, 40, 37, 1024], P('dp', 'space'), may hold values from -6 to 6
- weights: bfloat16 [3, 9, 1024, 128], P(None, None, 'space'), may hold values from -0.0625 to 0.0625
- bias: float32 [3, 128], replicated, may hold values from -3 to 3
- grad_out: bfloat16 [8, 40, 37, 384], P('dp', 'space'), may hold values from -6 to 6
Outputs:
- activations: bfloat16 [8, 40, 37, 384], P('dp', 'space')
- input_grad: bfloat16 [8, 40, 37, 1024], P('dp', 'space')
- weight_grad: float32 [3, 9, 1024, 128], P(None, None, 'space')
- bias_grad: float32 [3, 128], replicated
All inputs are finite; a program needn't handle non-finite values.
Results may differ from a plain program's by a relative error of at most 0.0049.
Values may be sent and summed in bfloat16 or wider, within the bound.
No kernel may reach another device: no remote copies, remote signals or barrier semaphores. Data moves between devices by JAX's collectives and lax.ppermute only.
A program may use at most 128 MiB of HBM per device.

v0:
```python
import jax
import jax.numpy as jnp
from jax import lax
from jax.sharding import PartitionSpec as P

dilations = (12, 24, 36)
offsets = tuple(((row_shift, col_shift) for row_shift in (-1, 0, 1) for col_shift in (-1, 0, 1)))
margin = 36


def shifted_windows(padded, spacing, sign, all_rows, columns):
    pieces = []
    for shift_y, shift_x in offsets:
        row_start = margin + sign * shift_y * spacing
        col_start = margin + sign * shift_x * spacing
        pieces.append(
            padded[:, row_start : row_start + all_rows, col_start : col_start + columns, :]
        )
    return jnp.concatenate(pieces, axis=3)


def per_device(features, weights, bias, grad_out):
    images, row_count, columns, _ = features.shape
    outputs = weights.shape[3]
    spread = lax.all_to_all(features, "space", split_axis=3, concat_axis=1, tiled=True)
    all_rows = spread.shape[1]
    channels = spread.shape[3]
    padded_in = jnp.pad(spread, ((0, 0), (margin, margin), (margin, margin), (0, 0)))
    stacked = [shifted_windows(padded_in, spacing, 1, all_rows, columns) for spacing in dilations]

    def branch_partial(branch):
        kernel = weights[branch].reshape(9 * channels, outputs)
        return jnp.einsum(
            "bhwc,co->bhwo", stacked[branch], kernel, preferred_element_type=jnp.float32
        )

    joined = jnp.concatenate([branch_partial(branch) for branch in range(3)], axis=3)
    summed = lax.psum_scatter(joined, "space", scatter_dimension=1, tiled=True)
    pre_act = summed + bias.reshape(-1)
    squash = jax.nn.sigmoid(pre_act)
    active = (pre_act * squash).astype(jnp.bfloat16)
    slope_terms = squash * (1.0 + pre_act * (1.0 - squash))
    grad_local = (grad_out.astype(jnp.float32) * slope_terms).astype(jnp.bfloat16)
    grad_full = lax.all_gather(grad_local, "space", axis=1, tiled=True)
    weight_scale = 1.0 / (images * lax.axis_size("dp"))
    weight_terms = []
    bias_terms = []
    for branch in range(3):
        first_col = branch * outputs
        branch_grad = grad_full[:, :, :, first_col : first_col + outputs]
        weight_part = jnp.einsum(
            "bhwc,bhwo->co", stacked[branch], branch_grad, preferred_element_type=jnp.float32
        ).reshape(9, channels, outputs)
        bias_part = jnp.sum(branch_grad.astype(jnp.float32), axis=(0, 1, 2))
        weight_terms.append(weight_part)
        bias_terms.append(bias_part)
    padded_grad = jnp.pad(grad_full, ((0, 0), (margin, margin), (margin, margin), (0, 0)))
    grad_stack = jnp.concatenate(
        [
            shifted_windows(
                padded_grad[:, :, :, branch * outputs : (branch + 1) * outputs],
                spacing,
                -1,
                all_rows,
                columns,
            )
            for branch, spacing in enumerate(dilations)
        ],
        axis=3,
    )
    kernel_back = jnp.transpose(weights, (0, 1, 3, 2)).reshape(27 * outputs, channels)
    input_sum = jnp.einsum(
        "bhwo,oc->bhwc", grad_stack, kernel_back, preferred_element_type=jnp.float32
    )
    weight_sum = jnp.stack(weight_terms)
    bias_sum = jnp.stack(bias_terms)
    weight_sum, bias_sum = lax.psum((weight_sum, bias_sum), "dp")
    input_grad = lax.all_to_all(
        input_sum.astype(jnp.bfloat16), "space", split_axis=1, concat_axis=3, tiled=True
    )
    return (active, input_grad, weight_sum * weight_scale, bias_sum * weight_scale)


def solution(mesh):
    placed = (
        P("dp", "space", None, None),
        P(None, None, "space", None),
        P(),
        P("dp", "space", None, None),
    )
    return jax.shard_map(
        per_device,
        mesh=mesh,
        in_specs=placed,
        out_specs=(
            P("dp", "space", None, None),
            P("dp", "space", None, None),
            P(None, None, "space", None),
            P(),
        ),
        check_vma=False,
    )
```

profile of v0, /device:TPU:0, one launch (start us, length us, event | category | flops | bytes accessed | tf_op | source)
XLA Modules:
  0.0 275.7 jit_solution(17523752401133420368)
XLA Ops:
  7.2 6.1 %copy.40 = bf16[1,10,37,1024]{2,1,0,3:T(8,128)(2,1)} copy(bf16[1,10,37,1024]{3,2,1,0:T(8,128)(2,1)} %param.4) | data formatting | bytes 1515520 | tf_op args[0]
  13.3 6.5 %reshape.83 = bf16[4,2,47360]{2,1,0:T(2,128)(2,1)} reshape(bf16[1024,1,10,37]{3,2,1,0:T(8,128)(2,1)} %bitcast.115) | data formatting | bytes 1515520
  19.8 5.2 %all-to-all-start = ((bf16[4,2,47360]{2,1,0:T(2,128)(2,1)}), bf16[4,2,47360]{2,1,0:T(2,128)(2,1)S(1)}, u32[]{:S(2)}, u32[]{:S(2)}) async-start(bf16[4,2,47360]{2,1,0:T(2,128)(2,1)} %reshape.83), calls=%async_computation | async-start | bytes 1515520 | tf_op jit(solution)/shard_map/all_to_all | solution.py:25
  26.1 9.3 %all-to-all-done = bf16[4,2,47360]{2,1,0:T(2,128)(2,1)S(1)} async-done(((bf16[4,2,47360]{2,1,0:T(2,128)(2,1)}), bf16[4,2,47360]{2,1,0:T(2,128)(2,1)S(1)}, u32[]{:S(2)}, u32[]{:S(2)}) %all-to-all-start) | async-done | bytes 757792 | tf_op jit(solution)/shard_map/all_to_all | solution.py:25
  35.5 5.5 %reshape.84 = bf16[1024,1,10,37]{3,2,1,0:T(8,128)(2,1)} reshape(bf16[4,2,47360]{2,1,0:T(2,128)(2,1)S(1)} %all-to-all-done) | data formatting | bytes 1515520
  40.9 4.9 %copy.41 = bf16[1,10,37,4,256]{4,2,1,3,0:T(8,128)(2,1)S(1)} copy(bf16[1,10,37,4,256]{2,1,4,3,0:T(8,128)(2,1)} %bitcast.114) | data formatting | bytes 1515520 | tf_op jit(solution)/shard_map/all_to_all | solution.py:25
  49.5 2.0 fusion.38
  53.1 2.1 fusion.35
  55.1 2.1 fusion.32
  57.4 3.7 %copy.46 = f32[1,40,37,384]{3,0,2,1:T(1,128)} copy(f32[1,40,37,384]{3,1,2,0:T(8,128)S(1)} %pad_maximum_fusion.1) | data formatting | bytes 4546560 | tf_op jit(solution)/shard_map/concatenate | solution.py:37
  62.4 71.8 %all-reduce.8.cloned.1.call-done = f32[1,40,37,384]{3,0,2,1:T(1,128)} async-done(((f32[1,40,37,384]{3,0,2,1:T(1,128)}), f32[1,40,37,384]{3,0,2,1:T(1,128)}) %all-reduce.8.cloned.1.call-update) | async-done | bytes 2273296
  134.3 2.8 %fusion.66 = (bf16[1,10,37,384]{3,0,2,1:T(2,128)(2,1)S(1)}, f32[1,10,37,384]{3,0,2,1:T(1,128)S(1)}) fusion(bf16[1,10,37,384]{3,2,1,0:T(8,128)(2,1)S(1)} %copy-done.4, f32[384]{0:T(512)S(1)} %bitcast.128, f32[1,40,37,384]{3,0,2,1:T(1,128)} %all-reduce.8.cloned.1.call-done, u32[]{:T(128)S(6)} %multiply.1), kind=kLoop, calls=%fused_computation.106 | loop fusion | flops 1562880 | bytes 1706500 | tf_op jit(solution)/shard_map/convert_element_type | solution.py:43
  137.9 2.4 copy.53
  140.3 26.0 %all-gather.2.cloned.1.call-done = bf16[1,40,37,384]{3,2,0,1:T(8,128)(2,1)} async-done(((bf16[1,10,37,384]{3,2,0,1:T(8,128)(2,1)}), bf16[1,40,37,384]{3,2,0,1:T(8,128)(2,1)}) %all-gather.2.cloned.1.call-update) | async-done | bytes 1136656 | tf_op jit(solution)/shard_map/all_gather | solution.py:44
  168.7 5.6 %fusion.23 = f32[1,9,256,128]{3,2,1,0:T(8,128)S(1)} fusion(bf16[37,5,9,8,256]{4,3,2,1,0:T(8,128)(2,1)} %bitcast.121, bf16[1,40,37,384]{3,1,2,0:T(8,128)(2,1)S(1)} %copy.49), kind=kOutput, calls=%fused_computation.70 | convolution fusion | flops 872939520 | bytes 8378368 | tf_op jit(solution)/shard_map/bhwc,bhwo->co/dot_general | solution.py:51
  174.3 2.1 fusion.20
  176.4 2.2 fusion.17
  178.6 2.0 pad_maximum_fusion
  202.9 7.0 %fusion.29 = bf16[1,40,37,256]{3,1,2,0:T(8,128)(2,1)S(1)} fusion(bf16[3456,256,1]{1,0,2:T(8,128)(2,1)S(1)} %bitcast.117, bf16[1,40,37,3456]{3,1,2,0:T(8,128)(2,1)} %fusion.90), kind=kOutput, calls=%fused_computation.72 | convolution fusion | flops 2619197440 | bytes 12756992 | tf_op jit(solution)/shard_map/bhwo,oc->bhwc/dot_general | solution.py:72
  211.0 3.5 %all-to-all-start.1 = ((bf16[1,40,37,256]{3,2,0,1:T(8,128)(2,1)}), bf16[1,40,37,256]{3,2,0,1:T(8,128)(2,1)S(1)}, u32[]{:S(2)}, u32[]{:S(2)}) async-start(bf16[1,40,37,256]{3,2,0,1:T(8,128)(2,1)} %copy.54), calls=%async_computation.1 | async-start | bytes 1638400 | tf_op jit(solution)/shard_map/all_to_all | solution.py:78
  214.5 1.7 multiply_convert_fusion
  217.1 16.5 %psum.15 = f32[3,128]{1,0:T(4,128)S(1)} all-reduce(f32[3,128]{1,0:T(4,128)S(1)} %pad_maximum_fusion.2), channel_id=1, replica_groups=mesh['dp'=8,'space'=4] {'dp'}, use_global_device_ids=true, to_apply=%region_5.6 | all-reduce | flops 384 | bytes 3072 | tf_op jit(solution)/shard_map/psum | solution.py:77
  235.9 29.1 %all-reduce.6.cloned.1.call-done = f32[3,9,256,128]{3,2,1,0:T(8,128)} async-done(((f32[3,9,256,128]{3,2,1,0:T(8,128)}), f32[3,9,256,128]{3,2,1,0:T(8,128)}) %all-reduce.6.cloned.1.call-update) | async-done | bytes 3538960 | tf_op jit(solution)/shard_map/psum | solution.py:77
  265.0 4.2 %broadcast_multiply_fusion = f32[3,9,256,128]{3,2,1,0:T(8,128)} fusion(f32[3,9,256,128]{3,2,1,0:T(8,128)} %all-reduce.6.cloned.1.call-done), kind=kLoop, calls=%fused_computation.67 | loop fusion | flops 884736 | bytes 7077888 | tf_op jit(solution)/shard_map/mul | solution.py:81
  (101 shorter events, 36.8 us)
Async XLA Ops:
  7.2 17.8 %copy-start = (bf16[3,9,256,128]{3,2,1,0:T(8,128)(2,1)S(1)}, bf16[3,9,256,128]{3,2,1,0:T(8,128)(2,1)}, u32[]{:S(2)}) copy-start(bf16[3,9,256,128]{3,2,1,0:T(8,128)(2,1)} %param.5) | copy-start | bytes 5308420
  19.8 15.7 %all-to-all-start = ((bf16[4,2,47360]{2,1,0:T(2,128)(2,1)}), bf16[4,2,47360]{2,1,0:T(2,128)(2,1)S(1)}, u32[]{:S(2)}, u32[]{:S(2)}) async-start(bf16[4,2,47360]{2,1,0:T(2,128)(2,1)} %reshape.83), calls=%async_computation | async-start | bytes 1515520 | tf_op jit(solution)/shard_map/all_to_all | solution.py:25
  24.9 109.3 %all-reduce.8.cloned.1.call-start = ((), (), s32[]{:S(2)}) async-start(), calls=%async_computation.4 | async-start | bytes 4546560
  47.5 7.6 %copy-start.7 = (bf16[1,40,37,2304]{3,1,2,0:T(8,128)(2,1)}, bf16[1,40,37,2304]{3,1,2,0:T(8,128)(2,1)S(1)}, u32[]{:S(2)}) copy-start(bf16[1,40,37,2304]{3,1,2,0:T(8,128)(2,1)S(1)} %get-tuple-element.28) | copy-start | bytes 20459524
  48.0 1.5 copy-start.3
  48.1 4.9 %copy-start.6 = (bf16[1,40,37,2304]{3,1,2,0:T(8,128)(2,1)}, bf16[1,40,37,2304]{3,1,2,0:T(8,128)(2,1)S(1)}, u32[]{:S(2)}) copy-start(bf16[1,40,37,2304]{3,1,2,0:T(8,128)(2,1)S(1)} %get-tuple-element.31) | copy-start | bytes 20459524
  48.7 3.3 %copy-start.5 = (bf16[1,40,37,2304]{3,1,2,0:T(8,128)(2,1)}, bf16[1,40,37,2304]{3,1,2,0:T(8,128)(2,1)S(1)}, u32[]{:S(2)}) copy-start(bf16[1,40,37,2304]{3,1,2,0:T(8,128)(2,1)S(1)} %fusion.64) | copy-start | bytes 20459524
  49.5 3.6 %copy-start.2 = (bf16[1,9,256,128]{3,2,1,0:T(8,128)(2,1)S(1)}, bf16[1,9,256,128]{3,2,1,0:T(8,128)(2,1)}, u32[]{:S(2)}) copy-start(bf16[1,9,256,128]{3,2,1,0:T(8,128)(2,1)} %get-tuple-element.26) | copy-start | bytes 1769476
  57.2 4.0 %copy-start.9 = (u32[32]{0:T(128)S(1)}, u32[32]{0:T(128)}, u32[]{:S(2)}) copy-start(u32[32]{0:T(128)} %constant.18) | copy-start | bytes 388
  57.2 77.0 %copy-start.4 = (bf16[1,10,37,384]{3,2,1,0:T(8,128)(2,1)S(1)}, bf16[1,10,37,384]{3,2,1,0:T(8,128)(2,1)}, u32[]{:S(2)}) copy-start(bf16[1,10,37,384]{3,2,1,0:T(8,128)(2,1)} %param.7) | copy-start | bytes 852484
  57.2 77.0 %copy-start.8 = (f32[3,128]{1,0:T(4,128)S(1)}, f32[3,128]{1,0:T(4,128)}, u32[]{:S(2)}) copy-start(f32[3,128]{1,0:T(4,128)} %param.6) | copy-start | bytes 4612
  61.1 105.2 %all-gather.2.cloned.1.call-start = ((), (), s32[]{:S(2)}) async-start(), calls=%async_computation.2 | async-start | bytes 1536000 | tf_op jit(solution)/shard_map/all_gather | solution.py:44
  137.8 127.2 %all-reduce.6.cloned.1.call-start = ((), (), s32[]{:S(2)}) async-start(), calls=%async_computation.3 | async-start | bytes 7077888 | tf_op jit(solution)/shard_map/psum | solution.py:77
  167.8 6.5 %slice-start = ((s8[6819840]{0:T(1024)(128)(4,1)}), s8[4194304]{0:T(1024)(128)(4,1)S(1)}, s32[]{:S(2)}) async-start(s8[6819840]{0:T(1024)(128)(4,1)} %bitcast.122), calls=%async_computation.5 | async-start | bytes 8388608
  168.7 5.6 %slice-start.1 = ((s8[6819840]{0:T(1024)(128)(4,1)}), s8[2625536]{0:T(1024)(128)(4,1)S(1)}, s32[]{:S(2)}) async-start(s8[6819840]{0:T(1024)(128)(4,1)} %bitcast.122), calls=%async_computation.6 | async-start | bytes 5251072
  168.7 7.7 %slice-start.2 = ((s8[6819840]{0:T(1024)(128)(4,1)}), s8[4194304]{0:T(1024)(128)(4,1)S(1)}, s32[]{:S(2)}) async-start(s8[6819840]{0:T(1024)(128)(4,1)} %bitcast.125), calls=%async_computation.7 | async-start | bytes 8388608
  174.3 2.1 slice-start.3
  195.3 7.6 %copy-start.1 = (bf16[3,9,256,128]{2,3,1,0:T(8,128)(2,1)S(1)}, bf16[3,9,256,128]{2,3,1,0:T(8,128)(2,1)}, u32[]{:S(2)}) copy-start(bf16[3,9,256,128]{2,3,1,0:T(8,128)(2,1)} %copy.53) | copy-start | bytes 5308420
  211.0 23.2 %all-to-all-start.1 = ((bf16[1,40,37,256]{3,2,0,1:T(8,128)(2,1)}), bf16[1,40,37,256]{3,2,0,1:T(8,128)(2,1)S(1)}, u32[]{:S(2)}, u32[]{:S(2)}) async-start(bf16[1,40,37,256]{3,2,0,1:T(8,128)(2,1)} %copy.54), calls=%async_computation.1 | async-start | bytes 1638400 | tf_op jit(solution)/shard_map/all_to_all | solution.py:78
Sparse Core Ops, SparseCore 0:
  61.3 72.9 all-reduce.7
  137.9 28.3 all-gather.1
  180.8 84.1 all-reduce.5
where the time goes:
time: 276 us
  waiting for transfers between devices  136 us (49%)
  local copies, waits for them, and re-layouts  64.8 us (23%)
  matrix products  23 us (8%)
  blocking collectives  16.5 us (6%)
  between operations  14.8 us (5%)
  other arithmetic  11.6 us (4%)
  starting transfers between devices  8.75 us (3%)
    unnamed x4, waiting for transfers between devices  71.8 us
    unnamed x81, local copies, waits for them, and re-layouts  48.6 us
    psum x1, waiting for transfers between devices, per_device(): weight_sum, bias_sum = lax.psum((weight_sum, bias_sum), 'dp')  29.1 us
    all_gather x1, waiting for transfers between devices, per_device(): grad_full = lax.all_gather(grad_local, 'space', axis=1, tiled=True)  26 us
    psum x1, blocking collectives, per_device(): weight_sum, bias_sum = lax.psum((weight_sum, bias_sum), 'dp')  16.5 us
    dot_general x3, matrix products, per_device(): jnp.einsum('bhwc,bhwo->co', stacked[branch], branch_grad, preferred_eleme...  9.89 us
    all_to_all x1, waiting for transfers between devices, per_device(): lax.all_to_all(features, 'space', split_axis=3, concat_axis=1, tiled=True)  9.34 us
    dot_general x1, matrix products, per_device(): jnp.einsum('bhwo,oc->bhwc', grad_stack, kernel_back, preferred_element_ty...  6.98 us
  transfers between devices with their start and end apart: 5, of which 4 were waited for; matrix products, arithmetic and copies ran while one was open for 14% of the time, Pallas kernels for 0%

commit v1 on v0

v1 whole, which is shorter than its diff:
```python
import functools

import jax
import jax.numpy as jnp
from jax import lax
from jax.experimental import pallas as pl
from jax.experimental.pallas import tpu as pltpu
from jax.sharding import PartitionSpec as P

dilations = (12, 24, 36)
BF = jnp.bfloat16
F32 = jnp.float32
EXTRA = 16


def stride_of(columns):
    return -(-columns // 8) * 8


def call(kernel, ins, outs, scratch, name, flops=0, in_specs=None):
    nbytes = sum(x.size * x.dtype.itemsize for x in ins) + sum(
        x.size * x.dtype.itemsize for x in outs
    )
    vmem = pl.BlockSpec(memory_space=pltpu.VMEM)
    return pl.pallas_call(
        kernel,
        grid=(1,),
        out_shape=tuple(outs),
        in_specs=in_specs or [vmem] * len(ins),
        out_specs=tuple(vmem for _ in outs),
        scratch_shapes=scratch,
        name=name,
        compiler_params=pltpu.CompilerParams(vmem_limit_bytes=48 * 1024 * 1024),
        cost_estimate=pl.CostEstimate(flops=flops, bytes_accessed=nbytes, transcendentals=0),
    )(*ins)


def shape(dims, kind):
    return jax.ShapeDtypeStruct(dims, kind)


def flatten_rows(src, scr, rows, columns, stride):
    for r in range(rows):
        scr[stride * r : stride * r + columns] = src[0, r].astype(F32)
        if stride > columns:
            scr[stride * r + columns : stride * (r + 1)] = jnp.zeros(
                (stride - columns, scr.shape[1]), F32
            )


def split_kernel(dims, x_ref, *refs):
    rows, columns, stride, parts = dims
    outs, scr = refs[:parts], refs[parts]
    me = lax.axis_index("space")
    flatten_rows(x_ref, scr, rows, columns, stride)
    width = outs[0].shape[1]
    for b in range(parts):
        at = pl.multiple_of((me ^ b) * width, width)
        outs[b][...] = scr[:, pl.ds(at, width)].astype(BF)


def shifted_copies(pad_scr, half_scr, out, columns, stride, shifts):
    total, n = out.shape[0], pad_scr.shape[1]
    pad = (pad_scr.shape[0] - total) // 2
    limit = pad_scr.shape[0] - 8
    half_scr[0:limit] = pad_scr[4 : limit + 4]
    step = 2 * stride
    col = lax.broadcasted_iota(jnp.int32, (step, n), 0)
    col = jnp.where(col >= stride, col - stride, col)

    @pl.loop(0, total // step)
    def _(p):
        base = pl.multiple_of(p * step, step)
        for j, shift in enumerate(shifts):
            off = pad + shift
            if off % 8 == 0:
                v = pad_scr[pl.ds(pl.multiple_of(base + off, 8), step)]
            else:
                v = half_scr[pl.ds(pl.multiple_of(base + off - 4, 8), step)]
            if shift:
                ok = (col + shift >= 0) & (col + shift < columns)
                v = jnp.where(ok, v, 0.0)
            out[pl.ds(base, step), j * n : (j + 1) * n] = v.astype(BF)


def gather_blocks(blocks, pad_scr, pad):
    me = lax.axis_index("space")
    size, n = blocks[0].shape
    total = size * len(blocks)
    pad_scr[0:pad] = jnp.zeros((pad, n), F32)
    pad_scr[pad + total : 2 * pad + total] = jnp.zeros((pad, n), F32)
    for b, block in enumerate(blocks):
        at = pl.multiple_of((me ^ b) * size + pad, 8)
        pad_scr[pl.ds(at, size)] = block[...].astype(F32)


def mm(a, b, ca=1, cb=0):
    return lax.dot_general(a, b, (((ca,), (cb,)), ((), ())), preferred_element_type=F32)


def forward_kernel(dims, spacing, parts, w_ref, *refs):
    columns, stride = dims
    blocks, outs = refs[:parts], refs[parts : 2 * parts]
    pad_scr, half_scr, stack, acc = refs[2 * parts :]
    me = lax.axis_index("space")
    total = acc.shape[0]
    n = blocks[0].shape[1]
    gather_blocks(blocks, pad_scr, stride)
    shifted_copies(pad_scr, half_scr, stack, columns, stride, (-spacing, 0, spacing))
    step = spacing * stride
    taps = [w_ref[0, 3 * a : 3 * a + 3].reshape(3 * n, w_ref.shape[3]) for a in range(3)]
    acc[...] = mm(stack[...], taps[1])
    acc[step:] += mm(stack[: total - step], taps[0])
    acc[: total - step] += mm(stack[step:], taps[2])
    size = outs[0].shape[0]
    for b in range(parts):
        at = pl.multiple_of((me ^ b) * size, 8)
        outs[b][...] = acc[pl.ds(at, size)].astype(outs[b].dtype)


def act_kernel(dims, branch, parts, *refs):
    rows, columns, stride = dims
    partials, bias_ref, go_ref = refs[:parts], refs[parts], refs[parts + 1]
    act_ref, grad_ref, scr = refs[parts + 2 :]
    flatten_rows(go_ref, scr, rows, columns, stride)
    pre = partials[0][...]
    for part in partials[1:]:
        pre = pre + part[...].astype(F32)
    pre = pre + bias_ref[branch : branch + 1, :]
    squash = jax.nn.sigmoid(pre)
    slope = squash * (1.0 + pre * (1.0 - squash))
    grad_ref[...] = (scr[...] * slope).astype(BF)
    scr[...] = pre * squash
    for r in range(rows):
        act_ref[0, r] = scr[stride * r : stride * r + columns].astype(BF)


def weight_kernel(dims, spacing, parts, *refs):
    columns, stride = dims
    grads, feats = refs[:parts], refs[parts : 2 * parts]
    keep, send = refs[2 * parts : 2 * parts + 2]
    gpad, ghalf, gstack, fpad, feat, full = refs[2 * parts + 2 :]
    core = lax.axis_index("dp") % 2
    total = gstack.shape[0]
    outputs = gpad.shape[1]
    gather_blocks(grads, gpad, stride)
    shifted_copies(gpad, ghalf, gstack, columns, stride, (spacing, 0, -spacing))
    me = lax.axis_index("space")
    size = feats[0].shape[0]
    for b in range(parts):
        at = pl.multiple_of((me ^ b) * size, 8)
        fpad[pl.ds(at, size)] = feats[b][...].astype(F32)
    feat[...] = fpad[...].astype(BF)
    step = spacing * stride
    for a in range(3):
        if a == 0:
            f, g = feat[: total - step], gstack[step:]
        elif a == 1:
            f, g = feat[...], gstack[...]
        else:
            f, g = feat[step:], gstack[: total - step]
        r = mm(f, g, 0, 0)
        for c in range(3):
            full[3 * a + c] = r[:, c * outputs : (c + 1) * outputs]
    half = full.shape[1] // 2
    body = 9 * half
    mine = full[:, pl.ds(pl.multiple_of(core * half, half), half)]
    other = full[:, pl.ds(pl.multiple_of((1 - core) * half, half), half)]
    keep[:body] = mine.reshape(body, outputs)
    send[:body] = other.reshape(body, outputs).astype(BF)
    total_bias = jnp.sum(gpad[...], axis=0, keepdims=True)
    high = total_bias.astype(BF).astype(F32)
    low = total_bias - high
    row = lax.broadcasted_iota(jnp.int32, (EXTRA, outputs), 0)
    keep[body:] = jnp.where(row == 0, total_bias, 0.0)
    send[body:] = jnp.where(row == 0, high, jnp.where(row == 1, low, 0.0)).astype(BF)


def fold_extra(x):
    row = lax.broadcasted_iota(jnp.int32, x.shape, 0)
    return jnp.where(row == 0, jnp.sum(x, axis=0, keepdims=True), 0.0)


def pack_extra(x):
    total = jnp.sum(x, axis=0, keepdims=True)
    high = total.astype(BF).astype(F32)
    row = lax.broadcasted_iota(jnp.int32, x.shape, 0)
    return jnp.where(row == 0, high, jnp.where(row == 1, total - high, 0.0)).astype(BF)


def add_pack_kernel(a_ref, b_ref, out_ref):
    body = out_ref.shape[0] - EXTRA
    total = a_ref[...].astype(F32) + b_ref[...].astype(F32)
    out_ref[:body] = total[:body].astype(BF)
    out_ref[body:] = pack_extra(total[body:])


def round_kernel(a_ref, out_ref):
    body = out_ref.shape[0] - EXTRA
    out_ref[:body] = a_ref[:body].astype(BF)
    out_ref[body:] = pack_extra(a_ref[body:])


def weight_out_kernel(scale, n, *refs):
    ins, (w_ref, b_ref) = refs[: 2 * n], refs[2 * n :]
    core = lax.axis_index("dp") % 2
    for k in range(n):
        mine, other = ins[2 * k], ins[2 * k + 1]
        half = w_ref.shape[2] // 2
        outputs = w_ref.shape[3]
        body = 9 * half
        at = pl.multiple_of(core * half, half)
        w_ref[k, :, pl.ds(at, half)] = (mine[:body].astype(F32) * scale).reshape(9, half, outputs)
        at = pl.multiple_of((1 - core) * half, half)
        w_ref[k, :, pl.ds(at, half)] = (other[:body].astype(F32) * scale).reshape(9, half, outputs)
        extra = jnp.sum(mine[body:].astype(F32), axis=0, keepdims=True)
        b_ref[k : k + 1, :] = extra * scale


def input_kernel(dims, parts, w_ref, *refs):
    columns, stride = dims
    grads, outs = refs[: 3 * parts], refs[3 * parts : 4 * parts]
    gpad, ghalf, gstack, acc = refs[4 * parts :]
    me = lax.axis_index("space")
    total = acc.shape[0]
    outputs = w_ref.shape[3]
    for k, spacing in enumerate(dilations):
        gather_blocks(grads[k * parts : (k + 1) * parts], gpad, stride)
        shifted_copies(gpad, ghalf, gstack, columns, stride, (spacing, 0, -spacing))
        step = spacing * stride
        for a in (1, 0, 2):
            w = jnp.concatenate([w_ref[k, 3 * a + c] for c in range(3)], axis=1)
            if a == 1:
                r = mm(gstack[...], w, 1, 1)
                if k == 0:
                    acc[...] = r
                else:
                    acc[...] += r
            elif a == 0:
                acc[: total - step] += mm(gstack[step:], w, 1, 1)
            else:
                acc[step:] += mm(gstack[: total - step], w, 1, 1)
    size = outs[0].shape[0]
    for b in range(parts):
        at = pl.multiple_of((me ^ b) * size, 8)
        outs[b][...] = acc[pl.ds(at, size)].astype(BF)


def join_kernel(dims, parts, *refs):
    rows, columns, stride = dims
    blocks, out_ref, scr = refs[:parts], refs[parts], refs[parts + 1]
    me = lax.axis_index("space")
    width = blocks[0].shape[1]
    for b in range(parts):
        at = pl.multiple_of((me ^ b) * width, width)
        scr[:, pl.ds(at, width)] = blocks[b][...].astype(F32)
    for r in range(rows):
        out_ref[0, r] = scr[stride * r : stride * r + columns].astype(BF)


def merge_kernel(*refs):
    ins, out = refs[:-1], refs[-1]
    n = ins[0].shape[3]
    for k, x in enumerate(ins):
        out[:, :, :, k * n : (k + 1) * n] = x[...]


def swap(x, bit):
    n = lax.axis_size("space")
    return lax.ppermute(x, "space", [(i, i ^ bit) for i in range(n)])


def line_sum(kept, size):
    rows, outputs = kept.shape
    n = size // 2
    packed = shape((rows, outputs), BF)
    if n != 4:
        groups = [[2 * i + c for i in range(n)] for c in range(2)]
        total = lax.psum(kept, "dp", axis_index_groups=groups)
        return call(round_kernel, [total], [packed], [], "round_rows")[0]
    start = call(round_kernel, [kept], [packed], [], "round_rows")[0]

    def chips(pairs):
        return [(2 * a + c, 2 * b + c) for a, b in pairs for c in range(2)]

    inward = lax.ppermute(start, "dp", chips([(0, 1), (3, 2)]))
    near = call(add_pack_kernel, [kept, inward], [packed], [], "add_near")[0]
    across = lax.ppermute(near, "dp", chips([(1, 2), (2, 1)]))
    total = call(add_pack_kernel, [near, across], [packed], [], "add_far")[0]
    outward = lax.ppermute(total, "dp", chips([(1, 0), (2, 3)]))
    chip = lax.axis_index("dp") // 2
    inner = (chip == 1) | (chip == 2)
    return jnp.where(inner, total, outward)


def per_device(features, weights, bias, grad_out):
    images, rows, columns, channels_all = features.shape
    assert images == 1
    parts = lax.axis_size("space")
    dp = lax.axis_size("dp")
    channels, outputs = weights.shape[2], weights.shape[3]
    stride = stride_of(columns)
    size = rows * stride
    total = size * parts
    padded = total + 2 * stride
    vm = pltpu.VMEM

    mine = call(
        functools.partial(split_kernel, (rows, columns, stride, parts)),
        [features],
        [shape((size, channels), BF)] * parts,
        [vm((size, channels_all), F32)],
        "split_channels",
    )
    feats = [mine[0]] + [swap(mine[b], b) for b in range(1, parts)]

    def branch_weights(k):
        return pl.BlockSpec((1, 9, channels, outputs), lambda i: (k, 0, 0, 0))

    whole = pl.BlockSpec(memory_space=pltpu.VMEM)
    acts, grads, sums = [], [], []
    partials = []
    for k, spacing in enumerate(dilations):
        part = call(
            functools.partial(forward_kernel, (columns, stride), spacing, parts),
            [weights] + feats,
            [shape((size, outputs), F32)] + [shape((size, outputs), BF)] * (parts - 1),
            [
                vm((padded, channels), F32),
                vm((padded, channels), F32),
                vm((total, 3 * channels), BF),
                vm((total, outputs), F32),
            ],
            f"forward_{k}",
            flops=2 * total * 6 * channels * outputs,
            in_specs=[branch_weights(k)] + [whole] * parts,
        )
        partials.append([part[0]] + [swap(part[b], b) for b in range(1, parts)])
    for k in range(3):
        act, grad = call(
            functools.partial(act_kernel, (rows, columns, stride), k, parts),
            partials[k] + [bias, grad_out],
            [shape((1, rows, columns, outputs), BF), shape((size, outputs), BF)],
            [vm((size, outputs), F32)],
            f"activation_{k}",
            in_specs=[whole] * (parts + 1)
            + [pl.BlockSpec((1, rows, columns, outputs), lambda i, k=k: (0, 0, 0, k))],
        )
        acts.append(act)
        grads.append([grad] + [swap(grad, b) for b in range(1, parts)])
    half = channels // 2
    kept_rows = 9 * half + EXTRA
    for k, spacing in enumerate(dilations):
        keep, send = call(
            functools.partial(weight_kernel, (columns, stride), spacing, parts),
            grads[k] + feats,
            [shape((kept_rows, outputs), F32), shape((kept_rows, outputs), BF)],
            [
                vm((padded, outputs), F32),
                vm((padded, outputs), F32),
                vm((total, 3 * outputs), BF),
                vm((total, channels), F32),
                vm((total, channels), BF),
                vm((9, channels, outputs), F32),
            ],
            f"weight_grad_{k}",
            flops=2 * total * 6 * channels * outputs,
        )
        other = lax.ppermute(send, "dp", [(i, i ^ 1) for i in range(dp)])
        kept = call(
            add_fold_kernel,
            [keep, other],
            [shape((kept_rows, outputs), F32)],
            [],
            "add_cores",
        )[0]
        sums.append(line_sum(kept, dp))
    back = call(
        functools.partial(input_kernel, (columns, stride), parts),
        [weights] + grads[0] + grads[1] + grads[2],
        [shape((size, channels), BF)] * parts,
        [
            vm((padded, outputs), F32),
            vm((padded, outputs), F32),
            vm((total, 3 * outputs), BF),
            vm((total, channels), F32),
        ],
        "input_grad",
        flops=2 * total * 18 * channels * outputs,
    )
    blocks = [back[0]] + [swap(back[b], b) for b in range(1, parts)]
    input_grad = call(
        functools.partial(join_kernel, (rows, columns, stride), parts),
        blocks,
        [shape(features.shape, BF)],
        [vm((size, channels_all), F32)],
        "join_channels",
    )[0]
    active = call(merge_kernel, acts, [shape(grad_out.shape, BF)], [], "merge_branches")[0]
    final = []
    for s in sums:
        final += [s, lax.ppermute(s, "dp", [(i, i ^ 1) for i in range(dp)])]
    weight_grad, bias_grad = call(
        functools.partial(weight_out_kernel, 1.0 / dp, 3),
        final,
        [shape((3, 9, channels, outputs), F32), shape((3, outputs), F32)],
        [],
        "weight_grad_out",
    )
    return active, input_grad, weight_grad, bias_grad


def add_fold_kernel(a_ref, b_ref, out_ref):
    body = out_ref.shape[0] - EXTRA
    total = a_ref[...] + b_ref[...].astype(F32)
    out_ref[:body] = total[:body]
    out_ref[body:] = fold_extra(total[body:])


def solution(mesh):
    placed = (
        P("dp", "space", None, None),
        P(None, None, "space", None),
        P(),
        P("dp", "space", None, None),
    )
    return jax.shard_map(
        per_device,
        mesh=mesh,
        in_specs=placed,
        out_specs=(
            P("dp", "space", None, None),
            P("dp", "space", None, None),
            P(None, None, "space", None),
            P(),
        ),
        check_vma=False,
    )
```

time: 276 us -> 139 us (0.50)
  waiting for transfers between devices: 136 us -> 57.8 us
  local copies, waits for them, and re-layouts: 64.8 us -> 14.1 us
  starting transfers between devices: 8.75 us -> 42.9 us
  matrix products: 23 us -> 0 us
  Pallas kernels: 0 us -> 21 us
  blocking collectives: 16.5 us -> 0 us
  between operations: 14.8 us -> 1.18 us
  other arithmetic: 11.6 us -> 1.08 us
    unnamed x4 -> x0, waiting for transfers between devices: 71.8 us -> none
    ppermute x0 -> x39, waiting for transfers between devices: none -> 57.8 us  [the longest x24 26.5 us: swap(): return lax.ppermute(x, 'space', [(i, i ^ bit) for i in range(n)])]
    ppermute x0 -> x39, starting transfers between devices: none -> 42.9 us  [the longest x24 30.3 us: swap(): return lax.ppermute(x, 'space', [(i, i ^ bit) for i in range(n)])]
    unnamed x81 -> x64, local copies, waits for them, and re-layouts: 48.6 us -> 14.1 us
    psum x1 -> x0, waiting for transfers between devices: 29.1 us -> none  [per_device(): weight_sum, bias_sum = lax.psum((weight_sum, bias_sum), 'dp')]
    all_gather x1 -> x0, waiting for transfers between devices: 26 us -> none  [per_device(): grad_full = lax.all_gather(grad_local, 'space', axis=1, tiled=True)]
    dot_general x7 -> x0, matrix products: 23 us -> none  [the longest x3 9.89 us: per_device(): jnp.einsum('bhwc,bhwo->co', stacked[branch], branch_grad, preferred_eleme...]
    pallas_call x0 -> x26, Pallas kernels: none -> 21 us  [call(): pl.pallas_call(kernel, grid=(1,), out_shape=tuple(outs), in_specs=in_spec...]
  transfers between devices with their start and end apart: 5 -> 39, of which waited for: 4 -> 16; matrix products, arithmetic and copies ran while one was open for 14% -> 1% of each run, Pallas kernels for 0% -> 12%
where the time goes in v1:
time: 139 us; the launch traced here: 138 us
  waiting for transfers between devices  57.8 us (42%)
  starting transfers between devices  42.9 us (31%)
  Pallas kernels  21 us (15%)
  local copies, waits for them, and re-layouts  14.1 us (10%)
    ppermute x24, starting transfers between devices, swap(): return lax.ppermute(x, 'space', [(i, i ^ bit) for i in range(n)])  30.3 us
    ppermute x24, waiting for transfers between devices, swap(): return lax.ppermute(x, 'space', [(i, i ^ bit) for i in range(n)])  26.5 us
    pallas_call x26, Pallas kernels, call(): pl.pallas_call(kernel, grid=(1,), out_shape=tuple(outs), in_specs=in_spec...  21 us
    ppermute x3, waiting for transfers between devices, line_sum(): outward = lax.ppermute(total, 'dp', chips([(1, 0), (2, 3)]))  16.2 us
    ppermute x3, waiting for transfers between devices, line_sum(): inward = lax.ppermute(start, 'dp', chips([(0, 1), (3, 2)]))  15.1 us
    unnamed x64, local copies, waits for them, and re-layouts  14.1 us
    ppermute x3, starting transfers between devices, line_sum(): inward = lax.ppermute(start, 'dp', chips([(0, 1), (3, 2)]))  6.12 us
    ppermute x3, starting transfers between devices, line_sum(): outward = lax.ppermute(total, 'dp', chips([(1, 0), (2, 3)]))  3.87 us
  transfers between devices with their start and end apart: 39, of which 16 were waited for; matrix products, arithmetic and copies ran while one was open for 1% of the time, Pallas kernels for 12%

profile of v1, /device:TPU:0, one launch (start us, length us, event | category | flops | bytes accessed | tf_op | source)
XLA Modules:
  0.0 138.1 jit_solution(17596225996336253023)
XLA Ops:
  2.1 3.0 %collective-permute-start = (bf16[400,256]{1,0:T(8,128)(2,1)S(1)}, bf16[400,256]{1,0:T(8,128)(2,1)S(1)}, u32[]{:S(2)}, u32[]{:S(2)}) collective-permute-start(bf16[400,256]{1,0:T(8,128)(2,1)S(1)} %get-tuple-element.39), channel_id=1, source_target_pairs={{0,1},{1,0},{2,3},{3,2},{4,5},{5,4},{6,7},{7,6},{8,9},{9,8},{10,11... | collective-permute-start | bytes 614408 | tf_op jit(solution)/shard_map/ppermute | solution.py:270
  5.1 1.5 %collective-permute-start.1 = (bf16[400,256]{1,0:T(8,128)(2,1)S(1)}, bf16[400,256]{1,0:T(8,128)(2,1)S(1)}, u32[]{:S(2)}, u32[]{:S(2)}) collective-permute-start(bf16[400,256]{1,0:T(8,128)(2,1)S(1)} %get-tuple-element.40), channel_id=1, source_target_pairs={{0,2},{1,3},{2,0},{3,1},{4,6},{5,7},{6,4},{7,5},{8,10},{9,11},{10,... | collective-permute-start | bytes 614408 | tf_op jit(solution)/shard_map/ppermute | solution.py:270
  6.6 4.4 %collective-permute-done.refs_1_.refs_5_ = bf16[400,256]{1,0:T(8,128)(2,1)S(1)} collective-permute-done((bf16[400,256]{1,0:T(8,128)(2,1)S(1)}, bf16[400,256]{1,0:T(8,128)(2,1)S(1)}, u32[]{:S(2)}, u32[]{:S(2)}) %collective-permute-start) | collective-permute-done | bytes 204832 | tf_op jit(solution)/shard_map/ppermute | solution.py:270
  11.0 5.0 %collective-permute-done.1.refs_2_.refs_6_ = bf16[400,256]{1,0:T(8,128)(2,1)S(1)} collective-permute-done((bf16[400,256]{1,0:T(8,128)(2,1)S(1)}, bf16[400,256]{1,0:T(8,128)(2,1)S(1)}, u32[]{:S(2)}, u32[]{:S(2)}) %collective-permute-start.1) | collective-permute-done | bytes 204832 | tf_op jit(solution)/shard_map/ppermute | solution.py:270
  22.5 2.1 %collective-permute-done.9.refs_1_ = bf16[400,128]{1,0:T(8,128)(2,1)S(1)} collective-permute-done((bf16[400,128]{1,0:T(8,128)(2,1)S(1)}, bf16[400,128]{1,0:T(8,128)(2,1)S(1)}, u32[]{:S(2)}, u32[]{:S(2)}) %collective-permute-start.9) | collective-permute-done | bytes 102432 | tf_op jit(solution)/shard_map/ppermute | solution.py:270
  25.1 1.6 %collective-permute-done.11.refs_3_ = bf16[400,128]{1,0:T(8,128)(2,1)S(1)} collective-permute-done((bf16[400,128]{1,0:T(8,128)(2,1)S(1)}, bf16[400,128]{1,0:T(8,128)(2,1)S(1)}, u32[]{:S(2)}, u32[]{:S(2)}) %collective-permute-start.11) | collective-permute-done | bytes 102432 | tf_op jit(solution)/shard_map/ppermute | solution.py:270
  31.1 1.8 %forward_1.1 = (f32[400,128]{1,0:T(8,128)S(1)}, bf16[400,128]{1,0:T(8,128)(2,1)S(1)}, bf16[400,128]{1,0:T(8,128)(2,1)S(1)}, bf16[400,128]{1,0:T(8,128)(2,1)S(1)}) custom-call(bf16[3,9,256,128]{3,2,1,0:T(8,128)(2,1)S(1)} %copy-done.1, bf16[400,256]{1,0:T(8,128)(2,1)S(1)} %get-tuple-element.38.refs_0_.refs_4_, ...), custom_call_target="tpu_custom_call" | custom-call | flops 629145600 | bytes 3100672 | tf_op jit(solution)/shard_map/forward_1/pallas_call | solution.py:25
  32.9 1.6 %collective-permute-start.6 = (bf16[400,128]{1,0:T(8,128)(2,1)S(1)}, bf16[400,128]{1,0:T(8,128)(2,1)S(1)}, u32[]{:S(2)}, u32[]{:S(2)}) collective-permute-start(bf16[400,128]{1,0:T(8,128)(2,1)S(1)} %get-tuple-element.48), channel_id=1, source_target_pairs={{0,1},{1,0},{2,3},{3,2},{4,5},{5,4},{6,7},{7,6},{8,9},{9,8},{10,11... | collective-permute-start | bytes 307208 | tf_op jit(solution)/shard_map/ppermute | solution.py:270
  36.5 2.3 %forward_0.1 = (f32[400,128]{1,0:T(8,128)S(1)}, bf16[400,128]{1,0:T(8,128)(2,1)S(1)}, bf16[400,128]{1,0:T(8,128)(2,1)S(1)}, bf16[400,128]{1,0:T(8,128)(2,1)S(1)}) custom-call(bf16[3,9,256,128]{3,2,1,0:T(8,128)(2,1)S(1)} %copy-done.1, bf16[400,256]{1,0:T(8,128)(2,1)S(1)} %get-tuple-element.38.refs_0_.refs_4_, ...), custom_call_target="tpu_custom_call" | custom-call | flops 629145600 | bytes 3100672 | tf_op jit(solution)/shard_map/forward_0/pallas_call | solution.py:25
  38.8 1.6 %collective-permute-start.3 = (bf16[400,128]{1,0:T(8,128)(2,1)S(1)}, bf16[400,128]{1,0:T(8,128)(2,1)S(1)}, u32[]{:S(2)}, u32[]{:S(2)}) collective-permute-start(bf16[400,128]{1,0:T(8,128)(2,1)S(1)} %get-tuple-element.43), channel_id=1, source_target_pairs={{0,1},{1,0},{2,3},{3,2},{4,5},{5,4},{6,7},{7,6},{8,9},{9,8},{10,11... | collective-permute-start | bytes 307208 | tf_op jit(solution)/shard_map/ppermute | solution.py:270
  42.5 1.5 %collective-permute-start.5 = (bf16[400,128]{1,0:T(8,128)(2,1)S(1)}, bf16[400,128]{1,0:T(8,128)(2,1)S(1)}, u32[]{:S(2)}, u32[]{:S(2)}) collective-permute-start(bf16[400,128]{1,0:T(8,128)(2,1)S(1)} %get-tuple-element.45), channel_id=1, source_target_pairs={{0,3},{1,2},{2,1},{3,0},{4,7},{5,6},{6,5},{7,4},{8,11},{9,10},{10,... | collective-permute-start | bytes 307208 | tf_op jit(solution)/shard_map/ppermute | solution.py:270
  44.2 1.5 %collective-permute-start.17 = (bf16[400,128]{1,0:T(8,128)(2,1)S(1)}, bf16[400,128]{1,0:T(8,128)(2,1)S(1)}, u32[]{:S(2)}, u32[]{:S(2)}) collective-permute-start(bf16[400,128]{1,0:T(8,128)(2,1)S(1)} %get-tuple-element.58.refs_4_.refs_0_), channel_id=1, source_target_pairs={{0,3},{1,2},{2,1},{3,0},{4,7},{5,6},{6,5},{7,4},{8,11},{9,10},{10,... | collective-permute-start | bytes 307208 | tf_op jit(solution)/shard_map/ppermute | solution.py:270
  49.4 1.5 %collective-permute-start.14 = (bf16[400,128]{1,0:T(8,128)(2,1)S(1)}, bf16[400,128]{1,0:T(8,128)(2,1)S(1)}, u32[]{:S(2)}, u32[]{:S(2)}) collective-permute-start(bf16[400,128]{1,0:T(8,128)(2,1)S(1)} %get-tuple-element.57.refs_0_), channel_id=1, source_target_pairs={{0,3},{1,2},{2,1},{3,0},{4,7},{5,6},{6,5},{7,4},{8,11},{9,10},{10,... | collective-permute-start | bytes 307208 | tf_op jit(solution)/shard_map/ppermute | solution.py:270
  54.8 1.7 %weight_grad_1.1 = (f32[1168,128]{1,0:T(8,128)S(1)}, bf16[1168,128]{1,0:T(8,128)(2,1)S(1)}) custom-call(bf16[400,128]{1,0:T(8,128)(2,1)S(1)} %get-tuple-element.58.refs_4_.refs_0_, bf16[400,128]{1,0:T(8,128)(2,1)S(1)} %collective-permute-done.15.refs_5_.refs_1_, bf16[400,128]{1,0:T(8,128)(2,1)S(1)} %collective-permute-done.16.refs_6_.refs_2_, ...), custom_call_target="tpu_custom_call" | custom-call | flops 629145600 | bytes 2125824 | tf_op jit(solution)/shard_map/weight_grad_1/pallas_call | solution.py:25
  58.3 2.0 %weight_grad_0.1 = (f32[1168,128]{1,0:T(8,128)S(1)}, bf16[1168,128]{1,0:T(8,128)(2,1)S(1)}) custom-call(bf16[400,128]{1,0:T(8,128)(2,1)S(1)} %get-tuple-element.57.refs_0_, bf16[400,128]{1,0:T(8,128)(2,1)S(1)} %collective-permute-done.12.refs_1_, bf16[400,128]{1,0:T(8,128)(2,1)S(1)} %collective-permute-done.13.refs_2_, ...), custom_call_target="tpu_custom_call" | custom-call | flops 629145600 | bytes 2125824 | tf_op jit(solution)/shard_map/weight_grad_0/pallas_call | solution.py:25
  60.6 3.5 %collective-permute-start.35 = (bf16[1168,128]{1,0:T(8,128)(2,1)S(1)}, bf16[1168,128]{1,0:T(8,128)(2,1)S(1)}, u32[]{:S(2)}, u32[]{:S(2)}) collective-permute-start(bf16[1168,128]{1,0:T(8,128)(2,1)S(1)} %round_rows.5), channel_id=1, source_target_pairs={{0,8},{4,12},{24,16},{28,20},{1,9},{5,13},{25,17},{29,21},{2,10},{... | collective-permute-start | bytes 897032 | tf_op jit(solution)/shard_map/ppermute | solution.py:286
  67.0 4.5 %collective-permute-done.35.b_ref = bf16[1168,128]{1,0:T(8,128)(2,1)S(1)} collective-permute-done((bf16[1168,128]{1,0:T(8,128)(2,1)S(1)}, bf16[1168,128]{1,0:T(8,128)(2,1)S(1)}, u32[]{:S(2)}, u32[]{:S(2)}) %collective-permute-start.35) | collective-permute-done | bytes 299040 | tf_op jit(solution)/shard_map/ppermute | solution.py:286
  72.4 5.5 %collective-permute-done.30.b_ref = bf16[1168,128]{1,0:T(8,128)(2,1)S(1)} collective-permute-done((bf16[1168,128]{1,0:T(8,128)(2,1)S(1)}, bf16[1168,128]{1,0:T(8,128)(2,1)S(1)}, u32[]{:S(2)}, u32[]{:S(2)}) %collective-permute-start.30) | collective-permute-done | bytes 299040 | tf_op jit(solution)/shard_map/ppermute | solution.py:286
  78.6 5.2 %collective-permute-done.25.b_ref = bf16[1168,128]{1,0:T(8,128)(2,1)S(1)} collective-permute-done((bf16[1168,128]{1,0:T(8,128)(2,1)S(1)}, bf16[1168,128]{1,0:T(8,128)(2,1)S(1)}, u32[]{:S(2)}, u32[]{:S(2)}) %collective-permute-start.25) | collective-permute-done | bytes 299040 | tf_op jit(solution)/shard_map/ppermute | solution.py:286
  96.8 4.7 %input_grad.1 = (bf16[400,256]{1,0:T(8,128)(2,1)S(1)}, bf16[400,256]{1,0:T(8,128)(2,1)S(1)}, bf16[400,256]{1,0:T(8,128)(2,1)S(1)}, bf16[400,256]{1,0:T(8,128)(2,1)S(1)}) custom-call(bf16[3,9,256,128]{3,2,1,0:T(8,128)(2,1)S(1)} %copy-done.1, bf16[400,128]{1,0:T(8,128)(2,1)S(1)} %copy-done.25, bf16[400,128]{1,0:T(8,128)(2,1)S(1)} %copy-done.31, ...), custom_call_target="tpu_custom_call" | custom-call | flops 1887436800 | bytes 3817472 | tf_op jit(solution)/shard_map/input_grad/pallas_call | solution.py:25
  106.6 11.5 %collective-permute-done.32 = bf16[1168,128]{1,0:T(8,128)(2,1)S(1)} collective-permute-done((bf16[1168,128]{1,0:T(8,128)(2,1)S(1)}, bf16[1168,128]{1,0:T(8,128)(2,1)S(1)}, u32[]{:S(2)}, u32[]{:S(2)}) %collective-permute-start.32) | collective-permute-done | bytes 299040 | tf_op jit(solution)/shard_map/ppermute | solution.py:290
  118.3 4.7 %collective-permute-done.27 = bf16[1168,128]{1,0:T(8,128)(2,1)S(1)} collective-permute-done((bf16[1168,128]{1,0:T(8,128)(2,1)S(1)}, bf16[1168,128]{1,0:T(8,128)(2,1)S(1)}, u32[]{:S(2)}, u32[]{:S(2)}) %collective-permute-start.27) | collective-permute-done | bytes 299040 | tf_op jit(solution)/shard_map/ppermute | solution.py:290
  126.2 8.7 %collective-permute-done.22.refs_2_ = bf16[400,256]{1,0:T(8,128)(2,1)S(1)} collective-permute-done((bf16[400,256]{1,0:T(8,128)(2,1)S(1)}, bf16[400,256]{1,0:T(8,128)(2,1)S(1)}, u32[]{:S(2)}, u32[]{:S(2)}) %collective-permute-start.22) | collective-permute-done | bytes 204832 | tf_op jit(solution)/shard_map/ppermute | solution.py:270
  136.0 2.0 %weight_grad_out.1 = (f32[3,9,256,128]{3,2,1,0:T(8,128)}, f32[3,128]{1,0:T(4,128)}) custom-call(bf16[1168,128]{1,0:T(8,128)(2,1)S(1)} %broadcast_select_fusion.2.refs_0_, bf16[1168,128]{1,0:T(8,128)(2,1)S(1)} %collective-permute-done.28.refs_1_, bf16[1168,128]{1,0:T(8,128)(2,1)S(1)} %broadcast_select_fusion.1.refs_2_, ...), custom_call_target="tpu_custom_call" | custom-call | bytes 5334528 | tf_op jit(solution)/shard_map/weight_grad_out/pallas_call | solution.py:25
  (147 shorter events, 53.5 us)
Async XLA Ops:
  2.1 8.9 %collective-permute-start = (bf16[400,256]{1,0:T(8,128)(2,1)S(1)}, bf16[400,256]{1,0:T(8,128)(2,1)S(1)}, u32[]{:S(2)}, u32[]{:S(2)}) collective-permute-start(bf16[400,256]{1,0:T(8,128)(2,1)S(1)} %get-tuple-element.39), channel_id=1, source_target_pairs={{0,1},{1,0},{2,3},{3,2},{4,5},{5,4},{6,7},{7,6},{8,9},{9,8},{10,11... | collective-permute-start | bytes 614408 | tf_op jit(solution)/shard_map/ppermute | solution.py:270
  5.1 10.9 %collective-permute-start.1 = (bf16[400,256]{1,0:T(8,128)(2,1)S(1)}, bf16[400,256]{1,0:T(8,128)(2,1)S(1)}, u32[]{:S(2)}, u32[]{:S(2)}) collective-permute-start(bf16[400,256]{1,0:T(8,128)(2,1)S(1)} %get-tuple-element.40), channel_id=1, source_target_pairs={{0,2},{1,3},{2,0},{3,1},{4,6},{5,7},{6,4},{7,5},{8,10},{9,11},{10,... | collective-permute-start | bytes 614408 | tf_op jit(solution)/shard_map/ppermute | solution.py:270
  6.6 9.4 %collective-permute-start.2 = (bf16[400,256]{1,0:T(8,128)(2,1)S(1)}, bf16[400,256]{1,0:T(8,128)(2,1)S(1)}, u32[]{:S(2)}, u32[]{:S(2)}) collective-permute-start(bf16[400,256]{1,0:T(8,128)(2,1)S(1)} %get-tuple-element.41), channel_id=1, source_target_pairs={{0,3},{1,2},{2,1},{3,0},{4,7},{5,6},{6,5},{7,4},{8,11},{9,10},{10,... | collective-permute-start | bytes 614408 | tf_op jit(solution)/shard_map/ppermute | solution.py:270
  29.1 9.7 %collective-permute-start.19 = (bf16[400,128]{1,0:T(8,128)(2,1)S(1)}, bf16[400,128]{1,0:T(8,128)(2,1)S(1)}, u32[]{:S(2)}, u32[]{:S(2)}) collective-permute-start(bf16[400,128]{1,0:T(8,128)(2,1)S(1)} %get-tuple-element.59.refs_8_.refs_0_), channel_id=1, source_target_pairs={{0,2},{1,3},{2,0},{3,1},{4,6},{5,7},{6,4},{7,5},{8,10},{9,11},{10,... | collective-permute-start | bytes 307208 | tf_op jit(solution)/shard_map/ppermute | solution.py:270
  30.6 9.8 %collective-permute-start.18 = (bf16[400,128]{1,0:T(8,128)(2,1)S(1)}, bf16[400,128]{1,0:T(8,128)(2,1)S(1)}, u32[]{:S(2)}, u32[]{:S(2)}) collective-permute-start(bf16[400,128]{1,0:T(8,128)(2,1)S(1)} %get-tuple-element.59.refs_8_.refs_0_), channel_id=1, source_target_pairs={{0,1},{1,0},{2,3},{3,2},{4,5},{5,4},{6,7},{7,6},{8,9},{9,8},{10,11... | collective-permute-start | bytes 307208 | tf_op jit(solution)/shard_map/ppermute | solution.py:270
  32.9 9.5 %collective-permute-start.6 = (bf16[400,128]{1,0:T(8,128)(2,1)S(1)}, bf16[400,128]{1,0:T(8,128)(2,1)S(1)}, u32[]{:S(2)}, u32[]{:S(2)}) collective-permute-start(bf16[400,128]{1,0:T(8,128)(2,1)S(1)} %get-tuple-element.48), channel_id=1, source_target_pairs={{0,1},{1,0},{2,3},{3,2},{4,5},{5,4},{6,7},{7,6},{8,9},{9,8},{10,11... | collective-permute-start | bytes 307208 | tf_op jit(solution)/shard_map/ppermute | solution.py:270
  34.5 8.0 %collective-permute-start.7 = (bf16[400,128]{1,0:T(8,128)(2,1)S(1)}, bf16[400,128]{1,0:T(8,128)(2,1)S(1)}, u32[]{:S(2)}, u32[]{:S(2)}) collective-permute-start(bf16[400,128]{1,0:T(8,128)(2,1)S(1)} %get-tuple-element.49), channel_id=1, source_target_pairs={{0,2},{1,3},{2,0},{3,1},{4,6},{5,7},{6,4},{7,5},{8,10},{9,11},{10,... | collective-permute-start | bytes 307208 | tf_op jit(solution)/shard_map/ppermute | solution.py:270
  35.0 9.0 %collective-permute-start.8 = (bf16[400,128]{1,0:T(8,128)(2,1)S(1)}, bf16[400,128]{1,0:T(8,128)(2,1)S(1)}, u32[]{:S(2)}, u32[]{:S(2)}) collective-permute-start(bf16[400,128]{1,0:T(8,128)(2,1)S(1)} %get-tuple-element.50), channel_id=1, source_target_pairs={{0,3},{1,2},{2,1},{3,0},{4,7},{5,6},{6,5},{7,4},{8,11},{9,10},{10,... | collective-permute-start | bytes 307208 | tf_op jit(solution)/shard_map/ppermute | solution.py:270
  42.4 18.0 %collective-permute-start.34 = (bf16[1168,128]{1,0:T(8,128)(2,1)S(1)}, bf16[1168,128]{1,0:T(8,128)(2,1)S(1)}, u32[]{:S(2)}, u32[]{:S(2)}) collective-permute-start(bf16[1168,128]{1,0:T(8,128)(2,1)S(1)} %get-tuple-element.69), channel_id=1, source_target_pairs={{0,4},{4,0},{8,12},{12,8},{16,20},{20,16},{24,28},{28,24},{1,5},{5... | collective-permute-start | bytes 897032 | tf_op jit(solution)/shard_map/ppermute | solution.py:369
  60.6 10.9 %collective-permute-start.35 = (bf16[1168,128]{1,0:T(8,128)(2,1)S(1)}, bf16[1168,128]{1,0:T(8,128)(2,1)S(1)}, u32[]{:S(2)}, u32[]{:S(2)}) collective-permute-start(bf16[1168,128]{1,0:T(8,128)(2,1)S(1)} %round_rows.5), channel_id=1, source_target_pairs={{0,8},{4,12},{24,16},{28,20},{1,9},{5,13},{25,17},{29,21},{2,10},{... | collective-permute-start | bytes 897032 | tf_op jit(solution)/shard_map/ppermute | solution.py:286
  64.2 13.6 %collective-permute-start.30 = (bf16[1168,128]{1,0:T(8,128)(2,1)S(1)}, bf16[1168,128]{1,0:T(8,128)(2,1)S(1)}, u32[]{:S(2)}, u32[]{:S(2)}) collective-permute-start(bf16[1168,128]{1,0:T(8,128)(2,1)S(1)} %round_rows.4), channel_id=1, source_target_pairs={{0,8},{4,12},{24,16},{28,20},{1,9},{5,13},{25,17},{29,21},{2,10},{... | collective-permute-start | bytes 897032 | tf_op jit(solution)/shard_map/ppermute | solution.py:286
  65.7 18.2 %collective-permute-start.25 = (bf16[1168,128]{1,0:T(8,128)(2,1)S(1)}, bf16[1168,128]{1,0:T(8,128)(2,1)S(1)}, u32[]{:S(2)}, u32[]{:S(2)}) collective-permute-start(bf16[1168,128]{1,0:T(8,128)(2,1)S(1)} %round_rows.3), channel_id=1, source_target_pairs={{0,8},{4,12},{24,16},{28,20},{1,9},{5,13},{25,17},{29,21},{2,10},{... | collective-permute-start | bytes 897032 | tf_op jit(solution)/shard_map/ppermute | solution.py:286
  71.5 13.1 %collective-permute-start.36 = (bf16[1168,128]{1,0:T(8,128)(2,1)S(1)}, bf16[1168,128]{1,0:T(8,128)(2,1)S(1)}, u32[]{:S(2)}, u32[]{:S(2)}) collective-permute-start(bf16[1168,128]{1,0:T(8,128)(2,1)S(1)} %add_near.5.a_ref), channel_id=1, source_target_pairs={{8,16},{12,20},{16,8},{20,12},{9,17},{13,21},{17,9},{21,13},{10,18... | collective-permute-start | bytes 897032 | tf_op jit(solution)/shard_map/ppermute | solution.py:288
  77.9 24.8 %collective-permute-start.31 = (bf16[1168,128]{1,0:T(8,128)(2,1)S(1)}, bf16[1168,128]{1,0:T(8,128)(2,1)S(1)}, u32[]{:S(2)}, u32[]{:S(2)}) collective-permute-start(bf16[1168,128]{1,0:T(8,128)(2,1)S(1)} %add_near.4.a_ref), channel_id=1, source_target_pairs={{8,16},{12,20},{16,8},{20,12},{9,17},{13,21},{17,9},{21,13},{10,18... | collective-permute-start | bytes 897032 | tf_op jit(solution)/shard_map/ppermute | solution.py:288
  83.9 20.2 %collective-permute-start.26 = (bf16[1168,128]{1,0:T(8,128)(2,1)S(1)}, bf16[1168,128]{1,0:T(8,128)(2,1)S(1)}, u32[]{:S(2)}, u32[]{:S(2)}) collective-permute-start(bf16[1168,128]{1,0:T(8,128)(2,1)S(1)} %add_near.3.a_ref), channel_id=1, source_target_pairs={{8,16},{12,20},{16,8},{20,12},{9,17},{13,21},{17,9},{21,13},{10,18... | collective-permute-start | bytes 897032 | tf_op jit(solution)/shard_map/ppermute | solution.py:288
  84.7 20.8 %collective-permute-start.37 = (bf16[1168,128]{1,0:T(8,128)(2,1)S(1)}, bf16[1168,128]{1,0:T(8,128)(2,1)}, u32[]{:S(2)}, u32[]{:S(2)}) collective-permute-start(bf16[1168,128]{1,0:T(8,128)(2,1)S(1)} %add_far.5), channel_id=1, source_target_pairs={{8,0},{12,4},{16,24},{20,28},{9,1},{13,5},{17,25},{21,29},{10,2},{... | collective-permute-start | bytes 897032 | tf_op jit(solution)/shard_map/ppermute | solution.py:290
  101.5 22.5 %collective-permute-start.21 = (bf16[400,256]{1,0:T(8,128)(2,1)S(1)}, bf16[400,256]{1,0:T(8,128)(2,1)S(1)}, u32[]{:S(2)}, u32[]{:S(2)}) collective-permute-start(bf16[400,256]{1,0:T(8,128)(2,1)S(1)} %get-tuple-element.61), channel_id=1, source_target_pairs={{0,1},{1,0},{2,3},{3,2},{4,5},{5,4},{6,7},{7,6},{8,9},{9,8},{10,11... | collective-permute-start | bytes 614408 | tf_op jit(solution)/shard_map/ppermute | solution.py:270
  102.8 15.3 %collective-permute-start.32 = (bf16[1168,128]{1,0:T(8,128)(2,1)S(1)}, bf16[1168,128]{1,0:T(8,128)(2,1)S(1)}, u32[]{:S(2)}, u32[]{:S(2)}) collective-permute-start(bf16[1168,128]{1,0:T(8,128)(2,1)S(1)} %add_far.4), channel_id=1, source_target_pairs={{8,0},{12,4},{16,24},{20,28},{9,1},{13,5},{17,25},{21,29},{10,2},{... | collective-permute-start | bytes 897032 | tf_op jit(solution)/shard_map/ppermute | solution.py:290
  104.2 18.7 %collective-permute-start.27 = (bf16[1168,128]{1,0:T(8,128)(2,1)S(1)}, bf16[1168,128]{1,0:T(8,128)(2,1)S(1)}, u32[]{:S(2)}, u32[]{:S(2)}) collective-permute-start(bf16[1168,128]{1,0:T(8,128)(2,1)S(1)} %add_far.3), channel_id=1, source_target_pairs={{8,0},{12,4},{16,24},{20,28},{9,1},{13,5},{17,25},{21,29},{10,2},{... | collective-permute-start | bytes 897032 | tf_op jit(solution)/shard_map/ppermute | solution.py:290
  106.6 29.5 %collective-permute-start.38 = (bf16[1168,128]{1,0:T(8,128)(2,1)S(1)}, bf16[1168,128]{1,0:T(8,128)(2,1)S(1)}, u32[]{:S(2)}, u32[]{:S(2)}) collective-permute-start(bf16[1168,128]{1,0:T(8,128)(2,1)S(1)} %broadcast_select_fusion.refs_4_), channel_id=1, source_target_pairs={{0,4},{4,0},{8,12},{12,8},{16,20},{20,16},{24,28},{28,24},{1,5},{5... | collective-permute-start | bytes 897032 | tf_op jit(solution)/shard_map/ppermute | solution.py:402
  118.2 17.9 %collective-permute-start.33 = (bf16[1168,128]{1,0:T(8,128)(2,1)S(1)}, bf16[1168,128]{1,0:T(8,128)(2,1)S(1)}, u32[]{:S(2)}, u32[]{:S(2)}) collective-permute-start(bf16[1168,128]{1,0:T(8,128)(2,1)S(1)} %broadcast_select_fusion.1.refs_2_), channel_id=1, source_target_pairs={{0,4},{4,0},{8,12},{12,8},{16,20},{20,16},{24,28},{28,24},{1,5},{5... | collective-permute-start | bytes 897032 | tf_op jit(solution)/shard_map/ppermute | solution.py:402
  123.0 13.1 %collective-permute-start.28 = (bf16[1168,128]{1,0:T(8,128)(2,1)S(1)}, bf16[1168,128]{1,0:T(8,128)(2,1)S(1)}, u32[]{:S(2)}, u32[]{:S(2)}) collective-permute-start(bf16[1168,128]{1,0:T(8,128)(2,1)S(1)} %broadcast_select_fusion.2.refs_0_), channel_id=1, source_target_pairs={{0,4},{4,0},{8,12},{12,8},{16,20},{20,16},{24,28},{28,24},{1,5},{5... | collective-permute-start | bytes 897032 | tf_op jit(solution)/shard_map/ppermute | solution.py:402
  123.0 11.9 %collective-permute-start.22 = (bf16[400,256]{1,0:T(8,128)(2,1)S(1)}, bf16[400,256]{1,0:T(8,128)(2,1)S(1)}, u32[]{:S(2)}, u32[]{:S(2)}) collective-permute-start(bf16[400,256]{1,0:T(8,128)(2,1)S(1)} %get-tuple-element.62), channel_id=1, source_target_pairs={{0,2},{1,3},{2,0},{3,1},{4,6},{5,7},{6,4},{7,5},{8,10},{9,11},{10,... | collective-permute-start | bytes 614408 | tf_op jit(solution)/shard_map/ppermute | solution.py:270
  124.0 11.0 %collective-permute-start.23 = (bf16[400,256]{1,0:T(8,128)(2,1)S(1)}, bf16[400,256]{1,0:T(8,128)(2,1)S(1)}, u32[]{:S(2)}, u32[]{:S(2)}) collective-permute-start(bf16[400,256]{1,0:T(8,128)(2,1)S(1)} %get-tuple-element.63), channel_id=1, source_target_pairs={{0,3},{1,2},{2,1},{3,0},{4,7},{5,6},{6,5},{7,4},{8,11},{9,10},{10,... | collective-permute-start | bytes 614408 | tf_op jit(solution)/shard_map/ppermute | solution.py:270
  (47 other events, 305.6 us)

commit v2 on v1

v2 whole, which is shorter than its diff:
```python
import functools

import jax
import jax.numpy as jnp
from jax import lax
from jax.experimental import pallas as pl
from jax.experimental.pallas import tpu as pltpu
from jax.sharding import PartitionSpec as P

dilations = (12, 24, 36)
BF = jnp.bfloat16
F32 = jnp.float32
EXTRA = 16


def stride_of(columns):
    return -(-columns // 8) * 8


COSTS = {"input_grad": 0.05, "add_near_0": 0.05, "add_near_1": 0.05, "add_near_2": 0.05, "split_rows": 0.05, "add_far_0": 0.05, "add_far_1": 0.05, "add_far_2": 0.05, "merge_branches": 0.05, "join_channels": 0.05, "choose_0": 0.05, "choose_1": 0.05, "choose_2": 0.05, "weight_out_0": 0.05, "weight_out_1": 0.05, "weight_out_2": 0.05, "bias_out": 0.05}
UNIT = 1_150_000_000


def call(chain, kernel, ins, outs, scratch, name, in_specs=None, out_specs=None, aliases=None):
    after = chain[-1:]
    vmem = pl.BlockSpec(memory_space=pltpu.VMEM)
    specs = list(in_specs or [vmem] * len(ins)) + [pl.BlockSpec(memory_space=pl.ANY)] * len(after)
    n, m, k = len(ins), len(after), len(outs)

    def body(*refs):
        token = refs[n + m + k]
        token[...] = jnp.zeros(token.shape, F32)
        kernel(*refs[:n], *refs[n + m : n + m + k], *refs[n + m + k + 1 :])

    *got, token = pl.pallas_call(
        body,
        grid=(1,),
        out_shape=(*outs, shape((8, 128), F32)),
        in_specs=specs,
        out_specs=(*(out_specs or [vmem] * k), vmem),
        scratch_shapes=scratch,
        name=name,
        input_output_aliases=aliases or {},
        compiler_params=pltpu.CompilerParams(vmem_limit_bytes=40 * 1024 * 1024),
        cost_estimate=pl.CostEstimate(
            flops=int(COSTS.get(name, 1.0) * UNIT), bytes_accessed=1024, transcendentals=0
        ),
    )(*ins, *after)
    chain.append(token)
    return got


def shape(dims, kind):
    return jax.ShapeDtypeStruct(dims, kind)


def flatten_rows(src, scr, rows, columns, stride):
    for r in range(rows):
        scr[stride * r : stride * r + columns] = src[0, r].astype(F32)
        if stride > columns:
            scr[stride * r + columns : stride * (r + 1)] = jnp.zeros(
                (stride - columns, scr.shape[1]), F32
            )


def levels(parts):
    return parts.bit_length() - 1


def flip_bit(core, level, parts):
    return 1 << ((level + core) % levels(parts))


def owner(q, parts):
    core = lax.axis_index("dp") % 2
    at = lax.axis_index("space")
    for level in range(levels(parts)):
        if (q >> (levels(parts) - 1 - level)) & 1:
            at = at ^ jnp.where(core == 0, flip_bit(0, level, parts), flip_bit(1, level, parts))
    return at


def exchange(x, level, parts, dp):
    pairs = []
    for d in range(dp):
        for p in range(parts):
            pairs.append((d * parts + p, d * parts + (p ^ flip_bit(d % 2, level, parts))))
    return lax.ppermute(x, ("dp", "space"), pairs)


def split_kernel(dims, x_ref, *refs):
    rows, columns, stride, parts = dims
    outs, scr = refs[:parts], refs[parts]
    me = lax.axis_index("space")
    flatten_rows(x_ref, scr, rows, columns, stride)
    width = outs[0].shape[1]
    for b in range(parts):
        at = pl.multiple_of((me ^ b) * width, width)
        outs[b][...] = scr[:, pl.ds(at, width)].astype(BF)


def shifted_copies(pad_scr, half_scr, out, columns, stride, shifts):
    total, n = out.shape[0], pad_scr.shape[1]
    pad = (pad_scr.shape[0] - total) // 2
    limit = pad_scr.shape[0] - 8
    half_scr[0:limit] = pad_scr[4 : limit + 4]
    step = 2 * stride
    col = lax.broadcasted_iota(jnp.int32, (step, n), 0)
    col = jnp.where(col >= stride, col - stride, col)

    @pl.loop(0, total // step)
    def _(p):
        base = pl.multiple_of(p * step, step)
        for j, shift in enumerate(shifts):
            off = pad + shift
            if off % 8 == 0:
                v = pad_scr[pl.ds(pl.multiple_of(base + off, 8), step)]
            else:
                v = half_scr[pl.ds(pl.multiple_of(base + off - 4, 8), step)]
            if shift:
                ok = (col + shift >= 0) & (col + shift < columns)
                v = jnp.where(ok, v, 0.0)
            out[pl.ds(base, step), j * n : (j + 1) * n] = v.astype(BF)


def gather_blocks(blocks, pad_scr, pad):
    me = lax.axis_index("space")
    size, n = blocks[0].shape
    total = size * len(blocks)
    pad_scr[0:pad] = jnp.zeros((pad, n), F32)
    pad_scr[pad + total : 2 * pad + total] = jnp.zeros((pad, n), F32)
    for b, block in enumerate(blocks):
        at = pl.multiple_of((me ^ b) * size + pad, 8)
        pad_scr[pl.ds(at, size)] = block[...].astype(F32)


def mm(a, b, ca=1, cb=0):
    return lax.dot_general(a, b, (((ca,), (cb,)), ((), ())), preferred_element_type=F32)


def take_rows(scr, places, size, parts):
    rows = [scr[pl.ds(pl.multiple_of(owner(q, parts) * size, 8), size)] for q in places]
    return jnp.concatenate(rows, axis=0)


def forward_kernel(dims, branch, parts, w_ref, *refs):
    columns, stride = dims
    blocks, outs = refs[:parts], refs[parts:-6]
    pad_scr, half_scr, stack, acc, taps, sem = refs[-6:]
    copy = pltpu.make_async_copy(w_ref.at[branch], taps, sem)
    copy.start()
    spacing = dilations[branch]
    total = acc.shape[0]
    n = blocks[0].shape[1]
    gather_blocks(blocks, pad_scr, stride)
    shifted_copies(pad_scr, half_scr, stack, columns, stride, (-spacing, 0, spacing))
    copy.wait()
    step = spacing * stride
    w = [taps[3 * a : 3 * a + 3].reshape(3 * n, taps.shape[2]) for a in range(3)]
    acc[...] = mm(stack[...], w[1])
    acc[step:] += mm(stack[: total - step], w[0])
    acc[: total - step] += mm(stack[step:], w[2])
    keep, send = outs[:2]
    size = blocks[0].shape[0]
    keep[...] = take_rows(acc, range(parts // 2), size, parts)
    send[...] = take_rows(acc, range(parts // 2, parts), size, parts).astype(BF)
    if len(outs) > 2:
        outs[2][...] = stack[:, n : 2 * n]


def add_half_kernel(kept, got, keep, send):
    x = kept[...] + got[...].astype(F32)
    size = keep.shape[0]
    keep[...] = x[:size]
    send[...] = x[size:].astype(BF)


def join_rows_kernel(a, b, out):
    out[...] = jnp.concatenate([a[...].astype(F32), b[...].astype(F32)], axis=0).astype(BF)


def act_kernel(dims, branch, kept, got, bias_ref, go_ref, act_ref, grad_ref, scr):
    rows, columns, stride = dims
    flatten_rows(go_ref, scr, rows, columns, stride)
    pre = kept[...] + got[...].astype(F32) + bias_ref[branch : branch + 1, :]
    squash = jax.nn.sigmoid(pre)
    slope = squash * (1.0 + pre * (1.0 - squash))
    grad_ref[...] = (scr[...] * slope).astype(BF)
    scr[...] = pre * squash
    for r in range(rows):
        act_ref[0, r] = scr[stride * r : stride * r + columns].astype(BF)


def weight_kernel(dims, spacing, parts, mine, theirs, feat, keep, send, gstack, *scratch):
    columns, stride = dims
    gpad, ghalf, full = scratch
    core = lax.axis_index("dp") % 2
    total = gstack.shape[0]
    outputs = gpad.shape[1]
    size = total // parts
    gpad[0:stride] = jnp.zeros((stride, outputs), F32)
    gpad[stride + total :] = jnp.zeros((stride, outputs), F32)
    for q in range(parts):
        block = (mine, theirs)[2 * q // parts][...].astype(F32)
        at = q % (parts // 2) * size
        to = pl.multiple_of(owner(q, parts) * size + stride, 8)
        gpad[pl.ds(to, size)] = block[at : at + size]
    shifted_copies(gpad, ghalf, gstack, columns, stride, (spacing, 0, -spacing))
    step = spacing * stride
    for a in range(3):
        if a == 0:
            f, g = feat[: total - step], gstack[step:]
        elif a == 1:
            f, g = feat[...], gstack[...]
        else:
            f, g = feat[step:], gstack[: total - step]
        r = mm(f, g, 0, 0)
        for c in range(3):
            full[3 * a + c] = r[:, c * outputs : (c + 1) * outputs]
    half = full.shape[1] // 2
    body = 9 * half
    own = full[:, pl.ds(pl.multiple_of(core * half, half), half)]
    other = full[:, pl.ds(pl.multiple_of((1 - core) * half, half), half)]
    keep[:body] = own.reshape(body, outputs)
    send[:body] = other.reshape(body, outputs).astype(BF)
    total_bias = jnp.sum(gpad[...], axis=0, keepdims=True)
    row = lax.broadcasted_iota(jnp.int32, (EXTRA, outputs), 0)
    own_bias = jnp.where(row == 0, total_bias, 0.0)
    keep[body:] = own_bias
    send[body:] = pack_extra(own_bias)


def pack_extra(x):
    total = jnp.sum(x, axis=0, keepdims=True)
    high = total.astype(BF).astype(F32)
    row = lax.broadcasted_iota(jnp.int32, x.shape, 0)
    return jnp.where(row == 0, high, jnp.where(row == 1, total - high, 0.0)).astype(BF)


def add_pack_kernel(*refs):
    ins, out_ref = refs[:-1], refs[-1]
    body = out_ref.shape[0] - EXTRA
    total = ins[0][...].astype(F32)
    for x in ins[1:]:
        total = total + x[...].astype(F32)
    out_ref[:body] = total[:body].astype(BF)
    out_ref[body:] = pack_extra(total[body:])


def choose_kernel(inner_ref, outer_ref, out_ref):
    chip = lax.axis_index("dp") // 2
    inner = (chip == 1) | (chip == 2)
    out_ref[...] = jnp.where(inner, inner_ref[...], outer_ref[...])


def weight_out_kernel(scale, place, first, *refs):
    mine, other = refs[:2]
    out, full, sem = refs[2 if first else 3 :]
    core = lax.axis_index("dp") % 2
    half, outputs = full.shape[1] // 2, full.shape[2]
    body = 9 * half
    for x, at in ((mine, core), (other, 1 - core)):
        rows = (x[:body].astype(F32) * scale).reshape(9, half, outputs)
        full[:, pl.ds(pl.multiple_of(at * half, half), half)] = rows
    copy = pltpu.make_async_copy(full, out.at[place], sem)
    copy.start()
    copy.wait()


def bias_out_kernel(scale, *refs):
    ins, out = refs[:-1], refs[-1]
    for k, x in enumerate(ins):
        extra = x[x.shape[0] - EXTRA :].astype(F32)
        out[k : k + 1, :] = jnp.sum(extra, axis=0, keepdims=True) * scale


def touch_kernel(w_ref):
    pass


def input_kernel(dims, parts, w_ref, *refs):
    stacks = refs[:3]
    acc, taps, sem = refs[3:]
    copy = pltpu.make_async_copy(w_ref, taps, sem)
    copy.start()
    copy.wait()
    total = acc.shape[0]
    for k, spacing in enumerate(dilations):
        g = stacks[k]
        step = spacing * dims[1]
        for a in (1, 0, 2):
            w = jnp.concatenate([taps[k, 3 * a + c] for c in range(3)], axis=1)
            if a == 1:
                r = mm(g[...], w, 1, 1)
                if k == 0:
                    acc[...] = r
                else:
                    acc[...] += r
            elif a == 0:
                acc[: total - step] += mm(g[step:], w, 1, 1)
            else:
                acc[step:] += mm(g[: total - step], w, 1, 1)


def split_rows_kernel(parts, acc, *outs):
    me = lax.axis_index("space")
    size = outs[0].shape[0]
    for b in range(parts):
        at = pl.multiple_of((me ^ b) * size, 8)
        outs[b][...] = acc[pl.ds(at, size)].astype(BF)


def join_kernel(dims, parts, *refs):
    rows, columns, stride = dims
    blocks, out_ref, scr = refs[:parts], refs[parts], refs[parts + 1]
    me = lax.axis_index("space")
    width = blocks[0].shape[1]
    for b in range(parts):
        at = pl.multiple_of((me ^ b) * width, width)
        scr[:, pl.ds(at, width)] = blocks[b][...].astype(F32)
    for r in range(rows):
        out_ref[0, r] = scr[stride * r : stride * r + columns].astype(BF)


def merge_kernel(*refs):
    ins, out = refs[:-1], refs[-1]
    n = ins[0].shape[3]
    for k, x in enumerate(ins):
        out[:, :, :, k * n : (k + 1) * n] = x[...]


def swap(x, bit):
    n = lax.axis_size("space")
    return lax.ppermute(x, "space", [(i, i ^ bit) for i in range(n)])


def per_device(features, weights, bias, grad_out):
    images, rows, columns, channels_all = features.shape
    assert images == 1
    parts = lax.axis_size("space")
    dp = lax.axis_size("dp")
    channels, outputs = weights.shape[2], weights.shape[3]
    stride = stride_of(columns)
    size = rows * stride
    total = size * parts
    padded = total + 2 * stride
    vm = pltpu.VMEM
    whole = pl.BlockSpec(memory_space=pltpu.VMEM)
    far = pl.BlockSpec(memory_space=pltpu.HBM)
    top = levels(parts)
    cores = [(i, i ^ 1) for i in range(dp)]
    half = channels // 2
    kept_rows = 9 * half + EXTRA
    packed = [shape((kept_rows, outputs), BF)]
    chain = []
    run = functools.partial(call, chain)

    mine = run(
        functools.partial(split_kernel, (rows, columns, stride, parts)),
        [features],
        [shape((size, channels), BF)] * parts,
        [vm((size, channels_all), F32)],
        "split_channels",
    )
    feats = [mine[0]] + [swap(mine[b], b) for b in range(1, parts)]

    state = {}
    rows_kept = size * parts // 2

    def forward(k, with_feat=False):
        outs = [shape((rows_kept, outputs), F32), shape((rows_kept, outputs), BF)]
        if with_feat:
            outs.append(shape((total, channels), BF))
        got = run(
            functools.partial(forward_kernel, (columns, stride), k, parts),
            [weights] + feats,
            outs,
            [
                vm((padded, channels), F32),
                vm((padded, channels), F32),
                vm((total, 3 * channels), BF),
                vm((total, outputs), F32),
                vm((9, channels, outputs), BF),
                pltpu.SemaphoreType.DMA,
            ],
            f"forward_{k}",
            in_specs=[far] + [whole] * parts,
        )
        if with_feat:
            state["feat"] = got[2]
        state[k] = (got[0], exchange(got[1], 0, parts, dp))

    def reduce_step(k, level):
        keep, got = state[k]
        n = keep.shape[0] // 2
        outs = [shape((n, outputs), F32), shape((n, outputs), BF)]
        keep, send = run(add_half_kernel, [keep, got], outs, [], f"add_{k}")
        state[k] = (keep, exchange(send, level, parts, dp))

    def activate(k):
        keep, got = state[k]
        act, grad = run(
            functools.partial(act_kernel, (rows, columns, stride), k),
            [keep, got, bias, grad_out],
            [shape((1, rows, columns, outputs), BF), shape((size, outputs), BF)],
            [vm((size, outputs), F32)],
            f"activation_{k}",
            in_specs=[whole] * 3 + [pl.BlockSpec((1, rows, columns, outputs), lambda i: (0, 0, 0, k))],
        )
        state[k] = (grad, exchange(grad, top - 1, parts, dp))
        state["act", k] = act

    def gather_step(k, level):
        own, got = state[k]
        outs = [shape((2 * own.shape[0], outputs), BF)]
        both = run(join_rows_kernel, [own, got], outs, [], f"join_{k}")[0]
        state[k] = (both, exchange(both, level, parts, dp))

    def weight_part(k):
        own, got = state[k]
        keep, send, stack = run(
            functools.partial(weight_kernel, (columns, stride), dilations[k], parts),
            [own, got, state["feat"]],
            [
                shape((kept_rows, outputs), F32),
                shape((kept_rows, outputs), BF),
                shape((total, 3 * outputs), BF),
            ],
            [
                vm((padded, outputs), F32),
                vm((padded, outputs), F32),
                vm((9, channels, outputs), F32),
            ],
            f"weight_grad_{k}",
        )
        state["stack", k] = stack
        state["sum", k] = (keep, lax.ppermute(send, "dp", cores))

    def line(pairs):
        return [(2 * a + c, 2 * b + c) for a, b in pairs for c in range(2)]

    def add_cores(k):
        keep, other = state["sum", k]
        if dp != 8:
            groups = [[2 * i + c for i in range(dp // 2)] for c in range(2)]
            state["sum", k] = lax.psum(keep + other.astype(F32), "dp", axis_index_groups=groups)
            return
        near = run(add_pack_kernel, [keep, other], packed, [], f"add_cores_{k}")[0]
        state["sum", k] = (keep, other, lax.ppermute(near, "dp", line([(0, 1), (3, 2)])))

    def add_near(k):
        if dp == 8:
            near = run(add_pack_kernel, list(state["sum", k]), packed, [], f"add_near_{k}")[0]
            state["sum", k] = (near, lax.ppermute(near, "dp", line([(1, 2), (2, 1)])))

    def add_far(k):
        if dp != 8:
            state["sum", k] = run(add_pack_kernel, [state["sum", k]], packed, [], f"round_{k}")[0]
            return
        total_rows = run(add_pack_kernel, list(state["sum", k]), packed, [], f"add_far_{k}")[0]
        state["sum", k] = (total_rows, lax.ppermute(total_rows, "dp", line([(1, 0), (2, 3)])))

    def choose(k):
        if dp == 8:
            state["sum", k] = run(choose_kernel, list(state["sum", k]), packed, [], f"choose_{k}")[0]
        state["sum", k] = (state["sum", k], lax.ppermute(state["sum", k], "dp", cores))

    def input_part():
        state["back"] = run(
            functools.partial(input_kernel, (columns, stride), parts),
            [weights] + [state["stack", k] for k in range(3)],
            [shape((total, channels), F32)],
            [vm(weights.shape, BF), pltpu.SemaphoreType.DMA],
            "input_grad",
            in_specs=[far] + [whole] * 3,
        )

    def send_back():
        outs = [shape((size, channels), BF)] * parts
        back = run(functools.partial(split_rows_kernel, parts), state["back"], outs, [], "split_rows")
        state["back"] = [back[0]] + [swap(back[b], b) for b in range(1, parts)]

    def join_back():
        state["input_grad"] = run(
            functools.partial(join_kernel, (rows, columns, stride), parts),
            state["back"],
            [shape(features.shape, BF)],
            [vm((size, channels_all), F32)],
            "join_channels",
        )[0]

    def merge():
        acts = [state["act", k] for k in range(3)]
        state["active"] = run(
            merge_kernel, acts, [shape(grad_out.shape, BF)], [], "merge_branches"
        )[0]

    def weight_out(k):
        first = "weight_grad" not in state
        anywhere = pl.BlockSpec(memory_space=pl.ANY)
        state["weight_grad"] = run(
            functools.partial(weight_out_kernel, 1.0 / dp, k, first),
            list(state["sum", k]) + ([] if first else [state["weight_grad"]]),
            [shape((3, 9, channels, outputs), F32)],
            [vm((9, channels, outputs), F32), pltpu.SemaphoreType.DMA],
            f"weight_out_{k}",
            in_specs=[whole] * 2 + ([] if first else [anywhere]),
            out_specs=[anywhere],
            aliases={} if first else {2: 0},
        )[0]

    k0, k1, k2 = 2, 0, 1
    run(touch_kernel, [weights], [], [], "touch_weights", in_specs=[far])
    forward(k0, with_feat=True)
    forward(k1)
    if top == 2:
        reduce_step(k0, 1)
        forward(k2)
        reduce_step(k1, 1)
        activate(k0)
        reduce_step(k2, 1)
        activate(k1)
        gather_step(k0, 0)
        activate(k2)
        gather_step(k1, 0)
        weight_part(k0)
        gather_step(k2, 0)
        weight_part(k1)
        add_cores(k0)
        weight_part(k2)
        add_cores(k1)
        add_cores(k2)
    else:
        forward(k2)
        for k in (k0, k1, k2):
            for level in range(1, top):
                reduce_step(k, level)
            activate(k)
            for level in range(top - 2, -1, -1):
                gather_step(k, level)
            weight_part(k)
            add_cores(k)
    input_part()
    add_near(k0)
    send_back()
    add_near(k1)
    add_near(k2)
    add_far(k0)
    add_far(k1)
    add_far(k2)
    merge()
    join_back()
    choose(k0)
    choose(k1)
    choose(k2)
    weight_out(k0)
    weight_out(k1)
    weight_out(k2)
    bias_grad = run(
        functools.partial(bias_out_kernel, 1.0 / dp),
        [state["sum", k][0] for k in range(3)],
        [shape((3, outputs), F32)],
        [],
        "bias_out",
    )[0]
    return state["active"], state["input_grad"], state["weight_grad"], bias_grad


def solution(mesh):
    placed = (
        P("dp", "space", None, None),
        P(None, None, "space", None),
        P(),
        P("dp", "space", None, None),
    )
    return jax.shard_map(
        per_device,
        mesh=mesh,
        in_specs=placed,
        out_specs=(
            P("dp", "space", None, None),
            P("dp", "space", None, None),
            P(None, None, "space", None),
            P(),
        ),
        check_vma=False,
    )
```

time: 139 us -> 107 us (0.77)
  local copies, waits for them, and re-layouts: 14.1 us -> 1.28 us
  starting transfers between devices: 42.9 us -> 31.1 us
  waiting for transfers between devices: 57.8 us -> 51.5 us
    ppermute x24 -> x6, starting transfers between devices: 30.3 us -> 7.29 us  [swap(): return lax.ppermute(x, 'space', [(i, i ^ bit) for i in range(n)])]
    unnamed x64 -> x8, local copies, waits for them, and re-layouts: 14.1 us -> 1.28 us
    ppermute x15 -> x27, starting transfers between devices: 12.6 us -> 23.8 us  [the longest x12 10.9 us: exchange(): return lax.ppermute(x, ('dp', 'space'), pairs)]
    ppermute x24 -> x6, waiting for transfers between devices: 26.5 us -> 17.6 us  [swap(): return lax.ppermute(x, 'space', [(i, i ^ bit) for i in range(n)])]
    ppermute x15 -> x27, waiting for transfers between devices: 31.3 us -> 33.9 us  [the longest x12 12.4 us: exchange(): return lax.ppermute(x, ('dp', 'space'), pairs)]
    pallas_call x26 -> x37, Pallas kernels: 21 us -> 21.8 us  [call(): pl.pallas_call(body, grid=(1,), out_shape=(*outs, shape((8, 128), F32)),...]
  transfers between devices with their start and end apart: 39 -> 33, of which waited for: 16 -> 18; matrix products, arithmetic and copies ran while one was open for 1% -> 0% of each run, Pallas kernels for 12% -> 17%
where the time goes in v2:
time: 107 us
  waiting for transfers between devices  51.5 us (48%)
  starting transfers between devices  31.1 us (29%)
  Pallas kernels  21.8 us (20%)
  local copies, waits for them, and re-layouts  1.28 us (1%)
    pallas_call x37, Pallas kernels, call(): pl.pallas_call(body, grid=(1,), out_shape=(*outs, shape((8, 128), F32)),...  21.8 us
    ppermute x6, waiting for transfers between devices, swap(): return lax.ppermute(x, 'space', [(i, i ^ bit) for i in range(n)])  17.6 us
    ppermute x12, waiting for transfers between devices, exchange(): return lax.ppermute(x, ('dp', 'space'), pairs)  12.4 us
    ppermute x3, waiting for transfers between devices, add_cores(): lax.ppermute(near, 'dp', line([(0, 1), (3, 2)]))  12.1 us
    ppermute x12, starting transfers between devices, exchange(): return lax.ppermute(x, ('dp', 'space'), pairs)  10.9 us
    ppermute x3, waiting for transfers between devices, add_far(): lax.ppermute(total_rows, 'dp', line([(1, 0), (2, 3)]))  9.37 us
    ppermute x6, starting transfers between devices, swap(): return lax.ppermute(x, 'space', [(i, i ^ bit) for i in range(n)])  7.29 us
    ppermute x3, starting transfers between devices, add_cores(): lax.ppermute(near, 'dp', line([(0, 1), (3, 2)]))  6.52 us
  transfers between devices with their start and end apart: 33, of which 18 were waited for; matrix products, arithmetic and copies ran while one was open for 0% of the time, Pallas kernels for 17%

profile of v2, /device:TPU:0, one launch (start us, length us, event | category | flops | bytes accessed | tf_op | source)
XLA Modules:
  0.0 106.7 jit_solution(1423503956603059458)
XLA Ops:
  2.2 3.0 %collective-permute-start = (bf16[400,256]{1,0:T(8,128)(2,1)S(1)}, bf16[400,256]{1,0:T(8,128)(2,1)S(1)}, u32[]{:S(2)}, u32[]{:S(2)}) collective-permute-start(bf16[400,256]{1,0:T(8,128)(2,1)S(1)} %get-tuple-element.98), channel_id=1, source_target_pairs={{0,1},{1,0},{2,3},{3,2},{4,5},{5,4},{6,7},{7,6},{8,9},{9,8},{10,11... | collective-permute-start | bytes 614408 | tf_op jit(solution)/shard_map/ppermute | solution.py:334
  5.2 1.5 %collective-permute-start.1 = (bf16[400,256]{1,0:T(8,128)(2,1)S(1)}, bf16[400,256]{1,0:T(8,128)(2,1)S(1)}, u32[]{:S(2)}, u32[]{:S(2)}) collective-permute-start(bf16[400,256]{1,0:T(8,128)(2,1)S(1)} %get-tuple-element.99), channel_id=1, source_target_pairs={{0,2},{1,3},{2,0},{3,1},{4,6},{5,7},{6,4},{7,5},{8,10},{9,11},{10,... | collective-permute-start | bytes 614408 | tf_op jit(solution)/shard_map/ppermute | solution.py:334
  6.7 4.4 %collective-permute-done.refs_2_ = bf16[400,256]{1,0:T(8,128)(2,1)S(1)} collective-permute-done((bf16[400,256]{1,0:T(8,128)(2,1)S(1)}, bf16[400,256]{1,0:T(8,128)(2,1)S(1)}, u32[]{:S(2)}, u32[]{:S(2)}) %collective-permute-start) | collective-permute-done | bytes 204832 | tf_op jit(solution)/shard_map/ppermute | solution.py:334
  11.1 5.0 %collective-permute-done.1.refs_3_ = bf16[400,256]{1,0:T(8,128)(2,1)S(1)} collective-permute-done((bf16[400,256]{1,0:T(8,128)(2,1)S(1)}, bf16[400,256]{1,0:T(8,128)(2,1)S(1)}, u32[]{:S(2)}, u32[]{:S(2)}) %collective-permute-start.1) | collective-permute-done | bytes 204832 | tf_op jit(solution)/shard_map/ppermute | solution.py:334
  16.1 1.7 %forward_2.1 = (f32[800,128]{1,0:T(8,128)S(1)}, bf16[800,128]{1,0:T(8,128)(2,1)S(1)}, bf16[1600,256]{1,0:T(8,128)(2,1)S(1)}, f32[8,128]{1,0:T(8,128)S(1)}) custom-call(bf16[3,9,256,128]{3,2,1,0:T(8,128)(2,1)S(1)} %copy-done, bf16[400,256]{1,0:T(8,128)(2,1)S(1)} %get-tuple-element.97.refs_1_, bf16[400,256]{1,0:T(8,128)(2,1)S(1)} %collective-permute-done.refs_2_, ...), custom_call_target="tpu_custom_call" | custom-call | flops 1150000000 | bytes 1024 | tf_op jit(solution)/shard_map/forward_2/pallas_call | solution.py:35
  19.1 2.5 %forward_0.1 = (f32[800,128]{1,0:T(8,128)S(1)}, bf16[800,128]{1,0:T(8,128)(2,1)S(1)}, f32[8,128]{1,0:T(8,128)S(1)}) custom-call(bf16[3,9,256,128]{3,2,1,0:T(8,128)(2,1)S(1)} %copy-done, bf16[400,256]{1,0:T(8,128)(2,1)S(1)} %get-tuple-element.97.refs_1_, bf16[400,256]{1,0:T(8,128)(2,1)S(1)} %collective-permute-done.refs_2_, ...), custom_call_target="tpu_custom_call" | custom-call | flops 1150000000 | bytes 1024 | tf_op jit(solution)/shard_map/forward_0/pallas_call | solution.py:35
  23.7 2.1 %collective-permute-start.7 = (bf16[400,128]{1,0:T(8,128)(2,1)S(1)}, bf16[400,128]{1,0:T(8,128)(2,1)S(1)}, u32[]{:S(2)}, u32[]{:S(2)}) collective-permute-start(bf16[400,128]{1,0:T(8,128)(2,1)S(1)} %get-tuple-element.115), channel_id=1, source_target_pairs={{0,2},{1,3},{2,0},{3,1},{4,5},{5,4},{6,7},{7,6},{8,10},{9,11},{10,... | collective-permute-start | bytes 307208 | tf_op jit(solution)/shard_map/ppermute | solution.py:88
  25.8 1.9 %forward_1.1 = (f32[800,128]{1,0:T(8,128)S(1)}, bf16[800,128]{1,0:T(8,128)(2,1)S(1)}, f32[8,128]{1,0:T(8,128)S(1)}) custom-call(bf16[3,9,256,128]{3,2,1,0:T(8,128)(2,1)S(1)} %copy-done, bf16[400,256]{1,0:T(8,128)(2,1)S(1)} %get-tuple-element.97.refs_1_, bf16[400,256]{1,0:T(8,128)(2,1)S(1)} %collective-permute-done.refs_2_, ...), custom_call_target="tpu_custom_call" | custom-call | flops 1150000000 | bytes 1024 | tf_op jit(solution)/shard_map/forward_1/pallas_call | solution.py:35
  29.7 1.4 %collective-permute-start.9 = (bf16[400,128]{1,0:T(8,128)(2,1)S(1)}, bf16[400,128]{1,0:T(8,128)(2,1)S(1)}, u32[]{:S(2)}, u32[]{:S(2)}) collective-permute-start(bf16[400,128]{1,0:T(8,128)(2,1)S(1)} %get-tuple-element.122.refs_0_), channel_id=1, source_target_pairs={{0,2},{1,3},{2,0},{3,1},{4,5},{5,4},{6,7},{7,6},{8,10},{9,11},{10,... | collective-permute-start | bytes 307208 | tf_op jit(solution)/shard_map/ppermute | solution.py:88
  31.1 2.7 %collective-permute-done.6.refs_1_ = bf16[800,128]{1,0:T(8,128)(2,1)S(1)} collective-permute-done((bf16[800,128]{1,0:T(8,128)(2,1)S(1)}, bf16[800,128]{1,0:T(8,128)(2,1)S(1)}, u32[]{:S(2)}, u32[]{:S(2)}) %collective-permute-start.6) | collective-permute-done | bytes 204832 | tf_op jit(solution)/shard_map/ppermute | solution.py:88
  34.4 1.8 %collective-permute-start.12 = (bf16[400,128]{1,0:T(8,128)(2,1)S(1)}, bf16[400,128]{1,0:T(8,128)(2,1)S(1)}, u32[]{:S(2)}, u32[]{:S(2)}) collective-permute-start(bf16[400,128]{1,0:T(8,128)(2,1)S(1)} %get-tuple-element.130.refs_0_), channel_id=1, source_target_pairs={{0,2},{1,3},{2,0},{3,1},{4,5},{5,4},{6,7},{7,6},{8,10},{9,11},{10,... | collective-permute-start | bytes 307208 | tf_op jit(solution)/shard_map/ppermute | solution.py:88
  36.4 2.7 %collective-permute-done.8.refs_1_ = bf16[400,128]{1,0:T(8,128)(2,1)S(1)} collective-permute-done((bf16[400,128]{1,0:T(8,128)(2,1)S(1)}, bf16[400,128]{1,0:T(8,128)(2,1)S(1)}, u32[]{:S(2)}, u32[]{:S(2)}) %collective-permute-start.8) | collective-permute-done | bytes 102432 | tf_op jit(solution)/shard_map/ppermute | solution.py:88
  44.9 2.2 %collective-permute-done.15.refs_1_ = bf16[800,128]{1,0:T(8,128)(2,1)S(1)} collective-permute-done((bf16[800,128]{1,0:T(8,128)(2,1)S(1)}, bf16[800,128]{1,0:T(8,128)(2,1)S(1)}, u32[]{:S(2)}, u32[]{:S(2)}) %collective-permute-start.15) | collective-permute-done | bytes 204832 | tf_op jit(solution)/shard_map/ppermute | solution.py:88
  47.1 1.9 %weight_grad_0.1 = (f32[1168,128]{1,0:T(8,128)S(1)}, bf16[1168,128]{1,0:T(8,128)(2,1)S(1)}, bf16[1600,384]{1,0:T(8,128)(2,1)S(1)}, f32[8,128]{1,0:T(8,128)S(1)}) custom-call(bf16[800,128]{1,0:T(8,128)(2,1)S(1)} %get-tuple-element.137.refs_0_, bf16[800,128]{1,0:T(8,128)(2,1)S(1)} %collective-permute-done.15.refs_1_, ...), custom_call_target="tpu_custom_call" | custom-call | flops 1150000000 | bytes 1024 | tf_op jit(solution)/shard_map/weight_grad_0/pallas_call | solution.py:35
  49.8 1.6 %weight_grad_1.1 = (f32[1168,128]{1,0:T(8,128)S(1)}, bf16[1168,128]{1,0:T(8,128)(2,1)S(1)}, bf16[1600,384]{1,0:T(8,128)(2,1)S(1)}, f32[8,128]{1,0:T(8,128)S(1)}) custom-call(bf16[800,128]{1,0:T(8,128)(2,1)S(1)} %get-tuple-element.134.refs_0_, bf16[800,128]{1,0:T(8,128)(2,1)S(1)} %collective-permute-done.13.refs_1_, ...), custom_call_target="tpu_custom_call" | custom-call | flops 1150000000 | bytes 1024 | tf_op jit(solution)/shard_map/weight_grad_1/pallas_call | solution.py:35
  51.4 3.7 %collective-permute-start.20 = (bf16[1168,128]{1,0:T(8,128)(2,1)S(1)}, bf16[1168,128]{1,0:T(8,128)(2,1)S(1)}, u32[]{:S(2)}, u32[]{:S(2)}) collective-permute-start(bf16[1168,128]{1,0:T(8,128)(2,1)S(1)} %get-tuple-element.154), channel_id=1, source_target_pairs={{0,8},{4,12},{24,16},{28,20},{1,9},{5,13},{25,17},{29,21},{2,10},{... | collective-permute-start | bytes 897032 | tf_op jit(solution)/shard_map/ppermute | solution.py:449
  56.6 1.5 %collective-permute-start.18 = (bf16[1168,128]{1,0:T(8,128)(2,1)S(1)}, bf16[1168,128]{1,0:T(8,128)(2,1)S(1)}, u32[]{:S(2)}, u32[]{:S(2)}) collective-permute-start(bf16[1168,128]{1,0:T(8,128)(2,1)S(1)} %get-tuple-element.147), channel_id=1, source_target_pairs={{0,8},{4,12},{24,16},{28,20},{1,9},{5,13},{25,17},{29,21},{2,10},{... | collective-permute-start | bytes 897032 | tf_op jit(solution)/shard_map/ppermute | solution.py:449
  58.1 3.0 %input_grad.1 = (f32[1600,256]{1,0:T(8,128)S(1)}, f32[8,128]{1,0:T(8,128)S(1)}) custom-call(bf16[3,9,256,128]{3,2,1,0:T(8,128)(2,1)S(1)} %copy-done, bf16[1600,384]{1,0:T(8,128)(2,1)S(1)} %get-tuple-element.149.refs_1_, bf16[1600,384]{1,0:T(8,128)(2,1)S(1)} %get-tuple-element.150.refs_2_, bf16[1600,384]{1,0:T(8,128)(2,1)S(1)} %get-tuple-element.151.refs_3_, ...), custom_call_target="tpu_custom_call" | custom-call | flops 57500000 | bytes 1024 | tf_op jit(solution)/shard_map/input_grad/pallas_call | solution.py:35
  61.1 1.4 %collective-permute-done.20.refs_2_ = bf16[1168,128]{1,0:T(8,128)(2,1)S(1)} collective-permute-done((bf16[1168,128]{1,0:T(8,128)(2,1)S(1)}, bf16[1168,128]{1,0:T(8,128)(2,1)S(1)}, u32[]{:S(2)}, u32[]{:S(2)}) %collective-permute-start.20) | collective-permute-done | bytes 299040 | tf_op jit(solution)/shard_map/ppermute | solution.py:449
  63.4 5.5 %collective-permute-done.19.refs_2_ = bf16[1168,128]{1,0:T(8,128)(2,1)S(1)} collective-permute-done((bf16[1168,128]{1,0:T(8,128)(2,1)S(1)}, bf16[1168,128]{1,0:T(8,128)(2,1)S(1)}, u32[]{:S(2)}, u32[]{:S(2)}) %collective-permute-start.19) | collective-permute-done | bytes 299040 | tf_op jit(solution)/shard_map/ppermute | solution.py:449
  69.7 5.2 %collective-permute-done.18.refs_2_ = bf16[1168,128]{1,0:T(8,128)(2,1)S(1)} collective-permute-done((bf16[1168,128]{1,0:T(8,128)(2,1)S(1)}, bf16[1168,128]{1,0:T(8,128)(2,1)S(1)}, u32[]{:S(2)}, u32[]{:S(2)}) %collective-permute-start.18) | collective-permute-done | bytes 299040 | tf_op jit(solution)/shard_map/ppermute | solution.py:449
  84.3 7.4 %collective-permute-done.25.refs_2_ = bf16[400,256]{1,0:T(8,128)(2,1)S(1)} collective-permute-done((bf16[400,256]{1,0:T(8,128)(2,1)S(1)}, bf16[400,256]{1,0:T(8,128)(2,1)S(1)}, u32[]{:S(2)}, u32[]{:S(2)}) %collective-permute-start.25) | collective-permute-done | bytes 204832 | tf_op jit(solution)/shard_map/ppermute | solution.py:334
  93.0 4.7 %collective-permute-done.28.refs_1_ = bf16[1168,128]{1,0:T(8,128)(2,1)S(1)} collective-permute-done((bf16[1168,128]{1,0:T(8,128)(2,1)S(1)}, bf16[1168,128]{1,0:T(8,128)(2,1)S(1)}, u32[]{:S(2)}, u32[]{:S(2)}) %collective-permute-start.28) | collective-permute-done | bytes 299040 | tf_op jit(solution)/shard_map/ppermute | solution.py:461
  97.9 4.6 %collective-permute-done.27.refs_1_ = bf16[1168,128]{1,0:T(8,128)(2,1)S(1)} collective-permute-done((bf16[1168,128]{1,0:T(8,128)(2,1)S(1)}, bf16[1168,128]{1,0:T(8,128)(2,1)S(1)}, u32[]{:S(2)}, u32[]{:S(2)}) %collective-permute-start.27) | collective-permute-done | bytes 299040 | tf_op jit(solution)/shard_map/ppermute | solution.py:461
  (87 shorter events, 32.3 us)
Async XLA Ops:
  2.2 8.9 %collective-permute-start = (bf16[400,256]{1,0:T(8,128)(2,1)S(1)}, bf16[400,256]{1,0:T(8,128)(2,1)S(1)}, u32[]{:S(2)}, u32[]{:S(2)}) collective-permute-start(bf16[400,256]{1,0:T(8,128)(2,1)S(1)} %get-tuple-element.98), channel_id=1, source_target_pairs={{0,1},{1,0},{2,3},{3,2},{4,5},{5,4},{6,7},{7,6},{8,9},{9,8},{10,11... | collective-permute-start | bytes 614408 | tf_op jit(solution)/shard_map/ppermute | solution.py:334
  5.2 10.9 %collective-permute-start.1 = (bf16[400,256]{1,0:T(8,128)(2,1)S(1)}, bf16[400,256]{1,0:T(8,128)(2,1)S(1)}, u32[]{:S(2)}, u32[]{:S(2)}) collective-permute-start(bf16[400,256]{1,0:T(8,128)(2,1)S(1)} %get-tuple-element.99), channel_id=1, source_target_pairs={{0,2},{1,3},{2,0},{3,1},{4,6},{5,7},{6,4},{7,5},{8,10},{9,11},{10,... | collective-permute-start | bytes 614408 | tf_op jit(solution)/shard_map/ppermute | solution.py:334
  6.7 9.4 %collective-permute-start.2 = (bf16[400,256]{1,0:T(8,128)(2,1)S(1)}, bf16[400,256]{1,0:T(8,128)(2,1)S(1)}, u32[]{:S(2)}, u32[]{:S(2)}) collective-permute-start(bf16[400,256]{1,0:T(8,128)(2,1)S(1)} %get-tuple-element.100), channel_id=1, source_target_pairs={{0,3},{1,2},{2,1},{3,0},{4,7},{5,6},{6,5},{7,4},{8,11},{9,10},{10,... | collective-permute-start | bytes 614408 | tf_op jit(solution)/shard_map/ppermute | solution.py:334
  17.8 5.8 %collective-permute-start.4 = (bf16[800,128]{1,0:T(8,128)(2,1)S(1)}, bf16[800,128]{1,0:T(8,128)(2,1)S(1)}, u32[]{:S(2)}, u32[]{:S(2)}) collective-permute-start(bf16[800,128]{1,0:T(8,128)(2,1)S(1)} %get-tuple-element.106), channel_id=1, source_target_pairs={{0,1},{1,0},{2,3},{3,2},{4,6},{5,7},{6,4},{7,5},{8,9},{9,8},{10,11... | collective-permute-start | bytes 614408 | tf_op jit(solution)/shard_map/ppermute | solution.py:88
  21.5 6.2 %collective-permute-start.3 = (bf16[800,128]{1,0:T(8,128)(2,1)S(1)}, bf16[800,128]{1,0:T(8,128)(2,1)S(1)}, u32[]{:S(2)}, u32[]{:S(2)}) collective-permute-start(bf16[800,128]{1,0:T(8,128)(2,1)S(1)} %get-tuple-element.104), channel_id=1, source_target_pairs={{0,1},{1,0},{2,3},{3,2},{4,6},{5,7},{6,4},{7,5},{8,9},{9,8},{10,11... | collective-permute-start | bytes 614408 | tf_op jit(solution)/shard_map/ppermute | solution.py:88
  23.7 5.9 %collective-permute-start.7 = (bf16[400,128]{1,0:T(8,128)(2,1)S(1)}, bf16[400,128]{1,0:T(8,128)(2,1)S(1)}, u32[]{:S(2)}, u32[]{:S(2)}) collective-permute-start(bf16[400,128]{1,0:T(8,128)(2,1)S(1)} %get-tuple-element.115), channel_id=1, source_target_pairs={{0,2},{1,3},{2,0},{3,1},{4,5},{5,4},{6,7},{7,6},{8,10},{9,11},{10,... | collective-permute-start | bytes 307208 | tf_op jit(solution)/shard_map/ppermute | solution.py:88
  27.7 6.1 %collective-permute-start.6 = (bf16[800,128]{1,0:T(8,128)(2,1)S(1)}, bf16[800,128]{1,0:T(8,128)(2,1)S(1)}, u32[]{:S(2)}, u32[]{:S(2)}) collective-permute-start(bf16[800,128]{1,0:T(8,128)(2,1)S(1)} %get-tuple-element.113), channel_id=1, source_target_pairs={{0,1},{1,0},{2,3},{3,2},{4,6},{5,7},{6,4},{7,5},{8,9},{9,8},{10,11... | collective-permute-start | bytes 614408 | tf_op jit(solution)/shard_map/ppermute | solution.py:88
  27.9 6.3 %collective-permute-start.5 = (bf16[400,128]{1,0:T(8,128)(2,1)S(1)}, bf16[400,128]{1,0:T(8,128)(2,1)S(1)}, u32[]{:S(2)}, u32[]{:S(2)}) collective-permute-start(bf16[400,128]{1,0:T(8,128)(2,1)S(1)} %get-tuple-element.111), channel_id=1, source_target_pairs={{0,2},{1,3},{2,0},{3,1},{4,5},{5,4},{6,7},{7,6},{8,10},{9,11},{10,... | collective-permute-start | bytes 307208 | tf_op jit(solution)/shard_map/ppermute | solution.py:88
  29.7 6.5 %collective-permute-start.9 = (bf16[400,128]{1,0:T(8,128)(2,1)S(1)}, bf16[400,128]{1,0:T(8,128)(2,1)S(1)}, u32[]{:S(2)}, u32[]{:S(2)}) collective-permute-start(bf16[400,128]{1,0:T(8,128)(2,1)S(1)} %get-tuple-element.122.refs_0_), channel_id=1, source_target_pairs={{0,2},{1,3},{2,0},{3,1},{4,5},{5,4},{6,7},{7,6},{8,10},{9,11},{10,... | collective-permute-start | bytes 307208 | tf_op jit(solution)/shard_map/ppermute | solution.py:88
  34.4 6.8 %collective-permute-start.12 = (bf16[400,128]{1,0:T(8,128)(2,1)S(1)}, bf16[400,128]{1,0:T(8,128)(2,1)S(1)}, u32[]{:S(2)}, u32[]{:S(2)}) collective-permute-start(bf16[400,128]{1,0:T(8,128)(2,1)S(1)} %get-tuple-element.130.refs_0_), channel_id=1, source_target_pairs={{0,2},{1,3},{2,0},{3,1},{4,5},{5,4},{6,7},{7,6},{8,10},{9,11},{10,... | collective-permute-start | bytes 307208 | tf_op jit(solution)/shard_map/ppermute | solution.py:88
  49.0 6.2 %collective-permute-start.17 = (bf16[1168,128]{1,0:T(8,128)(2,1)S(1)}, bf16[1168,128]{1,0:T(8,128)(2,1)S(1)}, u32[]{:S(2)}, u32[]{:S(2)}) collective-permute-start(bf16[1168,128]{1,0:T(8,128)(2,1)S(1)} %get-tuple-element.144), channel_id=1, source_target_pairs={{0,4},{4,0},{8,12},{12,8},{16,20},{20,16},{24,28},{28,24},{1,5},{5... | collective-permute-start | bytes 897032 | tf_op jit(solution)/shard_map/ppermute | solution.py:437
  51.4 11.1 %collective-permute-start.20 = (bf16[1168,128]{1,0:T(8,128)(2,1)S(1)}, bf16[1168,128]{1,0:T(8,128)(2,1)S(1)}, u32[]{:S(2)}, u32[]{:S(2)}) collective-permute-start(bf16[1168,128]{1,0:T(8,128)(2,1)S(1)} %get-tuple-element.154), channel_id=1, source_target_pairs={{0,8},{4,12},{24,16},{28,20},{1,9},{5,13},{25,17},{29,21},{2,10},{... | collective-permute-start | bytes 897032 | tf_op jit(solution)/shard_map/ppermute | solution.py:449
  55.2 13.7 %collective-permute-start.19 = (bf16[1168,128]{1,0:T(8,128)(2,1)S(1)}, bf16[1168,128]{1,0:T(8,128)(2,1)S(1)}, u32[]{:S(2)}, u32[]{:S(2)}) collective-permute-start(bf16[1168,128]{1,0:T(8,128)(2,1)S(1)} %get-tuple-element.148), channel_id=1, source_target_pairs={{0,8},{4,12},{24,16},{28,20},{1,9},{5,13},{25,17},{29,21},{2,10},{... | collective-permute-start | bytes 897032 | tf_op jit(solution)/shard_map/ppermute | solution.py:449
  56.6 18.3 %collective-permute-start.18 = (bf16[1168,128]{1,0:T(8,128)(2,1)S(1)}, bf16[1168,128]{1,0:T(8,128)(2,1)S(1)}, u32[]{:S(2)}, u32[]{:S(2)}) collective-permute-start(bf16[1168,128]{1,0:T(8,128)(2,1)S(1)} %get-tuple-element.147), channel_id=1, source_target_pairs={{0,8},{4,12},{24,16},{28,20},{1,9},{5,13},{25,17},{29,21},{2,10},{... | collective-permute-start | bytes 897032 | tf_op jit(solution)/shard_map/ppermute | solution.py:449
  62.7 14.0 %collective-permute-start.23 = (bf16[1168,128]{1,0:T(8,128)(2,1)S(1)}, bf16[1168,128]{1,0:T(8,128)(2,1)S(1)}, u32[]{:S(2)}, u32[]{:S(2)}) collective-permute-start(bf16[1168,128]{1,0:T(8,128)(2,1)S(1)} %get-tuple-element.161.refs_0_), channel_id=1, source_target_pairs={{8,16},{12,20},{16,8},{20,12},{9,17},{13,21},{17,9},{21,13},{10,18... | collective-permute-start | bytes 897032 | tf_op jit(solution)/shard_map/ppermute | solution.py:454
  69.1 9.0 %collective-permute-start.22 = (bf16[1168,128]{1,0:T(8,128)(2,1)S(1)}, bf16[1168,128]{1,0:T(8,128)(2,1)S(1)}, u32[]{:S(2)}, u32[]{:S(2)}) collective-permute-start(bf16[1168,128]{1,0:T(8,128)(2,1)S(1)} %get-tuple-element.160.refs_0_), channel_id=1, source_target_pairs={{8,16},{12,20},{16,8},{20,12},{9,17},{13,21},{17,9},{21,13},{10,18... | collective-permute-start | bytes 897032 | tf_op jit(solution)/shard_map/ppermute | solution.py:454
  75.7 6.8 %collective-permute-start.24 = (bf16[400,256]{1,0:T(8,128)(2,1)S(1)}, bf16[400,256]{1,0:T(8,128)(2,1)S(1)}, u32[]{:S(2)}, u32[]{:S(2)}) collective-permute-start(bf16[400,256]{1,0:T(8,128)(2,1)S(1)} %get-tuple-element.168), channel_id=1, source_target_pairs={{0,1},{1,0},{2,3},{3,2},{4,5},{5,4},{6,7},{7,6},{8,9},{9,8},{10,11... | collective-permute-start | bytes 614408 | tf_op jit(solution)/shard_map/ppermute | solution.py:334
  76.8 16.1 %collective-permute-start.29 = (bf16[1168,128]{1,0:T(8,128)(2,1)S(1)}, bf16[1168,128]{1,0:T(8,128)(2,1)S(1)}, u32[]{:S(2)}, u32[]{:S(2)}) collective-permute-start(bf16[1168,128]{1,0:T(8,128)(2,1)S(1)} %get-tuple-element.175.refs_0_), channel_id=1, source_target_pairs={{8,0},{12,4},{16,24},{20,28},{9,1},{13,5},{17,25},{21,29},{10,2},{... | collective-permute-start | bytes 897032 | tf_op jit(solution)/shard_map/ppermute | solution.py:461
  78.2 19.6 %collective-permute-start.28 = (bf16[1168,128]{1,0:T(8,128)(2,1)S(1)}, bf16[1168,128]{1,0:T(8,128)(2,1)S(1)}, u32[]{:S(2)}, u32[]{:S(2)}) collective-permute-start(bf16[1168,128]{1,0:T(8,128)(2,1)S(1)} %get-tuple-element.174.refs_0_), channel_id=1, source_target_pairs={{8,0},{12,4},{16,24},{20,28},{9,1},{13,5},{17,25},{21,29},{10,2},{... | collective-permute-start | bytes 897032 | tf_op jit(solution)/shard_map/ppermute | solution.py:461
  79.5 23.0 %collective-permute-start.27 = (bf16[1168,128]{1,0:T(8,128)(2,1)S(1)}, bf16[1168,128]{1,0:T(8,128)(2,1)S(1)}, u32[]{:S(2)}, u32[]{:S(2)}) collective-permute-start(bf16[1168,128]{1,0:T(8,128)(2,1)S(1)} %get-tuple-element.173.refs_0_), channel_id=1, source_target_pairs={{8,0},{12,4},{16,24},{20,28},{9,1},{13,5},{17,25},{21,29},{10,2},{... | collective-permute-start | bytes 897032 | tf_op jit(solution)/shard_map/ppermute | solution.py:461
  80.8 10.9 %collective-permute-start.25 = (bf16[400,256]{1,0:T(8,128)(2,1)S(1)}, bf16[400,256]{1,0:T(8,128)(2,1)S(1)}, u32[]{:S(2)}, u32[]{:S(2)}) collective-permute-start(bf16[400,256]{1,0:T(8,128)(2,1)S(1)} %get-tuple-element.169), channel_id=1, source_target_pairs={{0,2},{1,3},{2,0},{3,1},{4,6},{5,7},{6,4},{7,5},{8,10},{9,11},{10,... | collective-permute-start | bytes 614408 | tf_op jit(solution)/shard_map/ppermute | solution.py:334
  82.5 9.2 %collective-permute-start.26 = (bf16[400,256]{1,0:T(8,128)(2,1)S(1)}, bf16[400,256]{1,0:T(8,128)(2,1)S(1)}, u32[]{:S(2)}, u32[]{:S(2)}) collective-permute-start(bf16[400,256]{1,0:T(8,128)(2,1)S(1)} %get-tuple-element.170), channel_id=1, source_target_pairs={{0,3},{1,2},{2,1},{3,0},{4,7},{5,6},{6,5},{7,4},{8,11},{9,10},{10,... | collective-permute-start | bytes 614408 | tf_op jit(solution)/shard_map/ppermute | solution.py:334
  92.9 9.8 %collective-permute-start.32 = (bf16[1168,128]{1,0:T(8,128)(2,1)S(1)}, bf16[1168,128]{1,0:T(8,128)(2,1)S(1)}, u32[]{:S(2)}, u32[]{:S(2)}) collective-permute-start(bf16[1168,128]{1,0:T(8,128)(2,1)S(1)} %get-tuple-element.181.refs_0_.refs_2_), channel_id=1, source_target_pairs={{0,4},{4,0},{8,12},{12,8},{16,20},{20,16},{24,28},{28,24},{1,5},{5... | collective-permute-start | bytes 897032 | tf_op jit(solution)/shard_map/ppermute | solution.py:466
  97.8 6.0 %collective-permute-start.31 = (bf16[1168,128]{1,0:T(8,128)(2,1)S(1)}, bf16[1168,128]{1,0:T(8,128)(2,1)S(1)}, u32[]{:S(2)}, u32[]{:S(2)}) collective-permute-start(bf16[1168,128]{1,0:T(8,128)(2,1)S(1)} %get-tuple-element.180.refs_0_), channel_id=1, source_target_pairs={{0,4},{4,0},{8,12},{12,8},{16,20},{20,16},{24,28},{28,24},{1,5},{5... | collective-permute-start | bytes 897032 | tf_op jit(solution)/shard_map/ppermute | solution.py:466
  (13 other events, 55.8 us)

commit v3 on v2

--- a/solution.py
+++ b/solution.py
@@ -17,7 +17,7 @@
     return -(-columns // 8) * 8
 
 
-COSTS = {"input_grad": 0.05, "add_near_0": 0.05, "add_near_1": 0.05, "add_near_2": 0.05, "split_rows": 0.05, "add_far_0": 0.05, "add_far_1": 0.05, "add_far_2": 0.05, "merge_branches": 0.05, "join_channels": 0.05, "choose_0": 0.05, "choose_1": 0.05, "choose_2": 0.05, "weight_out_0": 0.05, "weight_out_1": 0.05, "weight_out_2": 0.05, "bias_out": 0.05}
+COSTS = {"input_grad": 0.05, "add_near_0": 0.05, "add_near_1": 0.05, "add_near_2": 0, "split_rows": 0.05, "add_far_0": 0.05, "add_far_1": 0.05, "add_far_2": 0.05, "merge_branches": 0.05, "join_channels": 0.05, "choose_0": 1, "choose_1": 0.05, "choose_2": 0.05, "weight_out_a": 0.05, "weight_out_b": 0.05, "add_cores_2": 1, "join_1": 3, "add_cores_0": 0, "add_cores_1": 0, "weight_grad_1": 0}
 UNIT = 1_150_000_000
 
 
@@ -191,9 +191,9 @@
         act_ref[0, r] = scr[stride * r : stride * r + columns].astype(BF)
 
 
-def weight_kernel(dims, spacing, parts, mine, theirs, feat, keep, send, gstack, *scratch):
+def weight_kernel(dims, spacing, parts, mine, theirs, feat, keep, *refs):
     columns, stride = dims
-    gpad, ghalf, full = scratch
+    send, gstack, gpad, ghalf, full = refs
     core = lax.axis_index("dp") % 2
     total = gstack.shape[0]
     outputs = gpad.shape[1]
@@ -237,41 +237,57 @@
     return jnp.where(row == 0, high, jnp.where(row == 1, total - high, 0.0)).astype(BF)
 
 
-def add_pack_kernel(*refs):
+def add_pack_kernel(body, *refs):
     ins, out_ref = refs[:-1], refs[-1]
-    body = out_ref.shape[0] - EXTRA
-    total = ins[0][...].astype(F32)
+    end = body + EXTRA
+    total = ins[0][:end].astype(F32)
     for x in ins[1:]:
-        total = total + x[...].astype(F32)
+        total = total + x[:end].astype(F32)
     out_ref[:body] = total[:body].astype(BF)
-    out_ref[body:] = pack_extra(total[body:])
-
-
-def choose_kernel(inner_ref, outer_ref, out_ref):
-    chip = lax.axis_index("dp") // 2
-    inner = (chip == 1) | (chip == 2)
-    out_ref[...] = jnp.where(inner, inner_ref[...], outer_ref[...])
-
-
-def weight_out_kernel(scale, place, first, *refs):
-    mine, other = refs[:2]
-    out, full, sem = refs[2 if first else 3 :]
+    out_ref[body:end] = pack_extra(total[body:])
+    if out_ref.shape[0] > end:
+        out_ref[end:] = jnp.zeros((out_ref.shape[0] - end, out_ref.shape[1]), BF)
+
+
+def put_half(x, out, buf, sem, place, at, scale):
+    half, outputs = buf.shape[1:]
+    buf[...] = (x[: 9 * half].astype(F32) * scale).reshape(9, half, outputs)
+    rows = pl.ds(pl.multiple_of(at * half, half), half)
+    copy = pltpu.make_async_copy(buf, out.at[place, :, rows], sem)
+    copy.start()
+    return copy
+
+
+def choose_kernel(scale, place, lined, *refs):
+    inner = refs[0][...]
+    if lined:
+        chip = lax.axis_index("dp") // 2
+        inner = jnp.where((chip == 1) | (chip == 2), inner, refs[1][...])
+    outs = refs[2 if lined else 1 :]
+    if place is None:
+        outs[0][...] = inner
+        return
+    own, out, buf, sem = outs[-4:]
+    own[...] = inner
+    put_half(inner, out, buf, sem, place, lax.axis_index("dp") % 2, scale).wait()
+
+
+def weight_out_kernel(scale, halves, *refs):
+    n = len(halves)
+    out, bufs, sems = refs[-3:]
     core = lax.axis_index("dp") % 2
-    half, outputs = full.shape[1] // 2, full.shape[2]
-    body = 9 * half
-    for x, at in ((mine, core), (other, 1 - core)):
-        rows = (x[:body].astype(F32) * scale).reshape(9, half, outputs)
-        full[:, pl.ds(pl.multiple_of(at * half, half), half)] = rows
-    copy = pltpu.make_async_copy(full, out.at[place], sem)
-    copy.start()
-    copy.wait()
-
-
-def bias_out_kernel(scale, *refs):
-    ins, out = refs[:-1], refs[-1]
+    copies = []
+    for i, (place, own) in enumerate(halves):
+        at = core if own else 1 - core
+        copies.append(put_half(refs[i], out, bufs.at[i], sems.at[i], place, at, scale))
+    for copy in copies:
+        copy.wait()
+
+
+def bias_kernel(scale, body, ins, out):
     for k, x in enumerate(ins):
-        extra = x[x.shape[0] - EXTRA :].astype(F32)
-        out[k : k + 1, :] = jnp.sum(extra, axis=0, keepdims=True) * scale
+        total = jnp.sum(x[body : body + EXTRA].astype(F32), axis=0, keepdims=True)
+        out[k : k + 1, :] = total * scale
 
 
 def touch_kernel(w_ref):
@@ -351,7 +367,7 @@
     cores = [(i, i ^ 1) for i in range(dp)]
     half = channels // 2
     kept_rows = 9 * half + EXTRA
-    packed = [shape((kept_rows, outputs), BF)]
+    packed = [shape((kept_rows + 16, outputs), BF)]
     chain = []
     run = functools.partial(call, chain)
 
@@ -434,36 +450,89 @@
             f"weight_grad_{k}",
         )
         state["stack", k] = stack
-        state["sum", k] = (keep, lax.ppermute(send, "dp", cores))
+        state["sum", k] = [keep, lax.ppermute(send, "dp", cores)]
 
     def line(pairs):
         return [(2 * a + c, 2 * b + c) for a, b in pairs for c in range(2)]
 
+    def add(name, ins):
+        return run(functools.partial(add_pack_kernel, 9 * half), ins, packed, [], name)[0]
+
     def add_cores(k):
-        keep, other = state["sum", k]
+        got = state["sum", k]
         if dp != 8:
+            kept = got[0] + got[1].astype(F32)
             groups = [[2 * i + c for i in range(dp // 2)] for c in range(2)]
-            state["sum", k] = lax.psum(keep + other.astype(F32), "dp", axis_index_groups=groups)
+            state["sum", k] = lax.psum(kept, "dp", axis_index_groups=groups)
             return
-        near = run(add_pack_kernel, [keep, other], packed, [], f"add_cores_{k}")[0]
-        state["sum", k] = (keep, other, lax.ppermute(near, "dp", line([(0, 1), (3, 2)])))
+        near = add(f"add_cores_{k}", got)
+        state["sum", k] = got + [lax.ppermute(near, "dp", line([(0, 1), (3, 2)]))]
 
     def add_near(k):
         if dp == 8:
-            near = run(add_pack_kernel, list(state["sum", k]), packed, [], f"add_near_{k}")[0]
-            state["sum", k] = (near, lax.ppermute(near, "dp", line([(1, 2), (2, 1)])))
+            near = add(f"add_near_{k}", state["sum", k])
+            state["sum", k] = [near, lax.ppermute(near, "dp", line([(1, 2), (2, 1)]))]
 
     def add_far(k):
         if dp != 8:
-            state["sum", k] = run(add_pack_kernel, [state["sum", k]], packed, [], f"round_{k}")[0]
+            state["sum", k] = [add(f"round_{k}", [state["sum", k]])]
             return
-        total_rows = run(add_pack_kernel, list(state["sum", k]), packed, [], f"add_far_{k}")[0]
-        state["sum", k] = (total_rows, lax.ppermute(total_rows, "dp", line([(1, 0), (2, 3)])))
-
-    def choose(k):
-        if dp == 8:
-            state["sum", k] = run(choose_kernel, list(state["sum", k]), packed, [], f"choose_{k}")[0]
-        state["sum", k] = (state["sum", k], lax.ppermute(state["sum", k], "dp", cores))
+        far_sum = add(f"add_far_{k}", state["sum", k])
+        state["sum", k] = [far_sum, lax.ppermute(far_sum, "dp", line([(1, 0), (2, 3)]))]
+
+    anywhere = pl.BlockSpec(memory_space=pl.ANY)
+    weight_shape = shape((3, 9, channels, outputs), F32)
+
+    def choose(k, last=False):
+        ins = state["sum", k]
+        place, outs, scratch, specs, out_specs, aliases = None, packed, [], None, None, None
+        if not last:
+            place, outs = k, packed + [weight_shape]
+            scratch = [vm((9, half, outputs), F32), pltpu.SemaphoreType.DMA]
+            out_specs = [whole, anywhere]
+            if "weight_grad" in state:
+                ins = ins + [state["weight_grad"]]
+                specs = [whole] * (len(ins) - 1) + [anywhere]
+                aliases = {len(ins) - 1: 1}
+        got = run(
+            functools.partial(choose_kernel, 1.0 / dp, place, dp == 8),
+            ins,
+            outs,
+            scratch,
+            f"choose_{k}",
+            in_specs=specs,
+            out_specs=out_specs,
+            aliases=aliases,
+        )
+        if not last:
+            state["weight_grad"] = got[1]
+        state["own", k] = got[0]
+        state["sum", k] = lax.ppermute(got[0], "dp", cores)
+
+    def weight_out(name, halves, with_bias=False):
+        ins = [state["own" if own else "sum", k] for k, own in halves]
+        n = len(ins)
+        extra = [state["own", k] for k in range(3)] if with_bias else []
+        outs = [weight_shape] + ([shape((3, outputs), F32)] if with_bias else [])
+
+        def kernel(*refs):
+            if with_bias:
+                bias_kernel(1.0 / dp, 9 * half, refs[n : n + 3], refs[-3])
+                refs = (*refs[: -3], *refs[-2:])
+            weight_out_kernel(1.0 / dp, halves, *refs[:n], refs[-3], *refs[-2:])
+
+        got = run(
+            kernel,
+            ins + extra + [state["weight_grad"]],
+            outs,
+            [vm((n, 9, half, outputs), F32), pltpu.SemaphoreType.DMA((n,))],
+            name,
+            in_specs=[whole] * (n + len(extra)) + [anywhere],
+            out_specs=[anywhere] + [whole] * (len(outs) - 1),
+            aliases={n + len(extra): 0},
+        )
+        state["weight_grad"] = got[0]
+        return got[-1]
 
     def input_part():
         state["back"] = run(
@@ -493,20 +562,6 @@
         acts = [state["act", k] for k in range(3)]
         state["active"] = run(
             merge_kernel, acts, [shape(grad_out.shape, BF)], [], "merge_branches"
-        )[0]
-
-    def weight_out(k):
-        first = "weight_grad" not in state
-        anywhere = pl.BlockSpec(memory_space=pl.ANY)
-        state["weight_grad"] = run(
-            functools.partial(weight_out_kernel, 1.0 / dp, k, first),
-            list(state["sum", k]) + ([] if first else [state["weight_grad"]]),
-            [shape((3, 9, channels, outputs), F32)],
-            [vm((9, channels, outputs), F32), pltpu.SemaphoreType.DMA],
-            f"weight_out_{k}",
-            in_specs=[whole] * 2 + ([] if first else [anywhere]),
-            out_specs=[anywhere],
-            aliases={} if first else {2: 0},
         )[0]
 
     k0, k1, k2 = 2, 0, 1
@@ -525,11 +580,20 @@
         gather_step(k1, 0)
         weight_part(k0)
         gather_step(k2, 0)
+        add_cores(k0)
         weight_part(k1)
-        add_cores(k0)
         weight_part(k2)
         add_cores(k1)
         add_cores(k2)
+        add_near(k0)
+        input_part()
+        send_back()
+        add_near(k1)
+        add_far(k0)
+        add_near(k2)
+        add_far(k1)
+        choose(k0)
+        add_far(k2)
     else:
         forward(k2)
         for k in (k0, k1, k2):
@@ -540,29 +604,19 @@
                 gather_step(k, level)
             weight_part(k)
             add_cores(k)
-    input_part()
-    add_near(k0)
-    send_back()
-    add_near(k1)
-    add_near(k2)
-    add_far(k0)
-    add_far(k1)
-    add_far(k2)
+            add_near(k)
+        input_part()
+        send_back()
+        add_far(k0)
+        add_far(k1)
+        choose(k0)
+        add_far(k2)
     merge()
     join_back()
-    choose(k0)
     choose(k1)
-    choose(k2)
-    weight_out(k0)
-    weight_out(k1)
-    weight_out(k2)
-    bias_grad = run(
-        functools.partial(bias_out_kernel, 1.0 / dp),
-        [state["sum", k][0] for k in range(3)],
-        [shape((3, outputs), F32)],
-        [],
-        "bias_out",
-    )[0]
+    choose(k2, last=True)
+    weight_out("weight_out_a", [(k0, False), (k1, False)])
+    bias_grad = weight_out("weight_out_b", [(k2, False), (k2, True)], with_bias=True)
     return state["active"], state["input_grad"], state["weight_grad"], bias_grad
 
 

time: 107 us -> 99 us (0.925)
  waiting for transfers between devices: 51.5 us -> 37 us
  starting transfers between devices: 31.1 us -> 37 us
    ppermute x15, waiting for transfers between devices: 21.5 us -> 13.4 us  [the longest x3 8.71 us: add_far(): lax.ppermute(far_sum, 'dp', line([(1, 0), (2, 3)]))]
    ppermute x15, starting transfers between devices: 12.8 us -> 19.1 us  [the longest x3 12.7 us: add_cores(): state['sum', k] = got + [lax.ppermute(near, 'dp', line([(0, 1), (3, 2)]))]]
    ppermute x6, waiting for transfers between devices: 17.6 us -> 12 us  [swap(): return lax.ppermute(x, 'space', [(i, i ^ bit) for i in range(n)])]
    pallas_call x37 -> x35, Pallas kernels: 21.8 us -> 22.3 us  [call(): pl.pallas_call(body, grid=(1,), out_shape=(*outs, shape((8, 128), F32)),...]
  transfers between devices with their start and end apart: 33 -> 33, of which waited for: 18 -> 17; matrix products, arithmetic and copies ran while one was open for 0% -> 0% of each run, Pallas kernels for 17% -> 19%
where the time goes in v3:
time: 99 us; the launch traced here: 98.7 us
  starting transfers between devices  37 us (37%)
  waiting for transfers between devices  37 us (37%)
  Pallas kernels  22.3 us (23%)
  local copies, waits for them, and re-layouts  1.28 us (1%)
  between operations  1.18 us (1%)
    pallas_call x35, Pallas kernels, call(): pl.pallas_call(body, grid=(1,), out_shape=(*outs, shape((8, 128), F32)),...  22.3 us
    ppermute x3, starting transfers between devices, add_cores(): state['sum', k] = got + [lax.ppermute(near, 'dp', line([(0, 1), (3, 2)]))]  12.7 us
    ppermute x6, waiting for transfers between devices, swap(): return lax.ppermute(x, 'space', [(i, i ^ bit) for i in range(n)])  12 us
    ppermute x12, waiting for transfers between devices, exchange(): return lax.ppermute(x, ('dp', 'space'), pairs)  11.6 us
    ppermute x12, starting transfers between devices, exchange(): return lax.ppermute(x, ('dp', 'space'), pairs)  10.9 us
    ppermute x3, waiting for transfers between devices, add_far(): lax.ppermute(far_sum, 'dp', line([(1, 0), (2, 3)]))  8.71 us
    ppermute x6, starting transfers between devices, swap(): return lax.ppermute(x, 'space', [(i, i ^ bit) for i in range(n)])  7 us
    ppermute x3, waiting for transfers between devices, add_cores(): state['sum', k] = got + [lax.ppermute(near, 'dp', line([(0, 1), (3, 2)]))]  4 us
  transfers between devices with their start and end apart: 33, of which 17 were waited for; matrix products, arithmetic and copies ran while one was open for 0% of the time, Pallas kernels for 19%

profile of v3, /device:TPU:0, one launch (start us, length us, event | category | flops | bytes accessed | tf_op | source)
XLA Modules:
  0.0 98.7 jit_solution(6227143654388791044)
XLA Ops:
  2.2 3.0 %collective-permute-start = (bf16[400,256]{1,0:T(8,128)(2,1)S(1)}, bf16[400,256]{1,0:T(8,128)(2,1)S(1)}, u32[]{:S(2)}, u32[]{:S(2)}) collective-permute-start(bf16[400,256]{1,0:T(8,128)(2,1)S(1)} %get-tuple-element.97), channel_id=1, source_target_pairs={{0,1},{1,0},{2,3},{3,2},{4,5},{5,4},{6,7},{7,6},{8,9},{9,8},{10,11... | collective-permute-start | bytes 614408 | tf_op jit(solution)/shard_map/ppermute | solution.py:350
  5.2 1.5 %collective-permute-start.1 = (bf16[400,256]{1,0:T(8,128)(2,1)S(1)}, bf16[400,256]{1,0:T(8,128)(2,1)S(1)}, u32[]{:S(2)}, u32[]{:S(2)}) collective-permute-start(bf16[400,256]{1,0:T(8,128)(2,1)S(1)} %get-tuple-element.98), channel_id=1, source_target_pairs={{0,2},{1,3},{2,0},{3,1},{4,6},{5,7},{6,4},{7,5},{8,10},{9,11},{10,... | collective-permute-start | bytes 614408 | tf_op jit(solution)/shard_map/ppermute | solution.py:350
  6.7 4.4 %collective-permute-done.refs_2_ = bf16[400,256]{1,0:T(8,128)(2,1)S(1)} collective-permute-done((bf16[400,256]{1,0:T(8,128)(2,1)S(1)}, bf16[400,256]{1,0:T(8,128)(2,1)S(1)}, u32[]{:S(2)}, u32[]{:S(2)}) %collective-permute-start) | collective-permute-done | bytes 204832 | tf_op jit(solution)/shard_map/ppermute | solution.py:350
  11.1 5.0 %collective-permute-done.1.refs_3_ = bf16[400,256]{1,0:T(8,128)(2,1)S(1)} collective-permute-done((bf16[400,256]{1,0:T(8,128)(2,1)S(1)}, bf16[400,256]{1,0:T(8,128)(2,1)S(1)}, u32[]{:S(2)}, u32[]{:S(2)}) %collective-permute-start.1) | collective-permute-done | bytes 204832 | tf_op jit(solution)/shard_map/ppermute | solution.py:350
  16.1 1.7 %forward_2.1 = (f32[800,128]{1,0:T(8,128)S(1)}, bf16[800,128]{1,0:T(8,128)(2,1)S(1)}, bf16[1600,256]{1,0:T(8,128)(2,1)S(1)}, f32[8,128]{1,0:T(8,128)S(1)}) custom-call(bf16[3,9,256,128]{3,2,1,0:T(8,128)(2,1)S(1)} %copy-done, bf16[400,256]{1,0:T(8,128)(2,1)S(1)} %get-tuple-element.96.refs_1_, bf16[400,256]{1,0:T(8,128)(2,1)S(1)} %collective-permute-done.refs_2_, ...), custom_call_target="tpu_custom_call" | custom-call | flops 1150000000 | bytes 1024 | tf_op jit(solution)/shard_map/forward_2/pallas_call | solution.py:35
  19.1 2.5 %forward_0.1 = (f32[800,128]{1,0:T(8,128)S(1)}, bf16[800,128]{1,0:T(8,128)(2,1)S(1)}, f32[8,128]{1,0:T(8,128)S(1)}) custom-call(bf16[3,9,256,128]{3,2,1,0:T(8,128)(2,1)S(1)} %copy-done, bf16[400,256]{1,0:T(8,128)(2,1)S(1)} %get-tuple-element.96.refs_1_, bf16[400,256]{1,0:T(8,128)(2,1)S(1)} %collective-permute-done.refs_2_, ...), custom_call_target="tpu_custom_call" | custom-call | flops 1150000000 | bytes 1024 | tf_op jit(solution)/shard_map/forward_0/pallas_call | solution.py:35
  23.7 2.2 %collective-permute-start.7 = (bf16[400,128]{1,0:T(8,128)(2,1)S(1)}, bf16[400,128]{1,0:T(8,128)(2,1)S(1)}, u32[]{:S(2)}, u32[]{:S(2)}) collective-permute-start(bf16[400,128]{1,0:T(8,128)(2,1)S(1)} %get-tuple-element.114), channel_id=1, source_target_pairs={{0,2},{1,3},{2,0},{3,1},{4,5},{5,4},{6,7},{7,6},{8,10},{9,11},{10,... | collective-permute-start | bytes 307208 | tf_op jit(solution)/shard_map/ppermute | solution.py:88
  25.8 1.9 %forward_1.1 = (f32[800,128]{1,0:T(8,128)S(1)}, bf16[800,128]{1,0:T(8,128)(2,1)S(1)}, f32[8,128]{1,0:T(8,128)S(1)}) custom-call(bf16[3,9,256,128]{3,2,1,0:T(8,128)(2,1)S(1)} %copy-done, bf16[400,256]{1,0:T(8,128)(2,1)S(1)} %get-tuple-element.96.refs_1_, bf16[400,256]{1,0:T(8,128)(2,1)S(1)} %collective-permute-done.refs_2_, ...), custom_call_target="tpu_custom_call" | custom-call | flops 1150000000 | bytes 1024 | tf_op jit(solution)/shard_map/forward_1/pallas_call | solution.py:35
  31.1 2.7 %collective-permute-done.6.refs_1_ = bf16[800,128]{1,0:T(8,128)(2,1)S(1)} collective-permute-done((bf16[800,128]{1,0:T(8,128)(2,1)S(1)}, bf16[800,128]{1,0:T(8,128)(2,1)S(1)}, u32[]{:S(2)}, u32[]{:S(2)}) %collective-permute-start.6) | collective-permute-done | bytes 204832 | tf_op jit(solution)/shard_map/ppermute | solution.py:88
  34.4 1.8 %collective-permute-start.12 = (bf16[400,128]{1,0:T(8,128)(2,1)S(1)}, bf16[400,128]{1,0:T(8,128)(2,1)S(1)}, u32[]{:S(2)}, u32[]{:S(2)}) collective-permute-start(bf16[400,128]{1,0:T(8,128)(2,1)S(1)} %get-tuple-element.129.refs_0_), channel_id=1, source_target_pairs={{0,2},{1,3},{2,0},{3,1},{4,5},{5,4},{6,7},{7,6},{8,10},{9,11},{10,... | collective-permute-start | bytes 307208 | tf_op jit(solution)/shard_map/ppermute | solution.py:88
  36.4 2.7 %collective-permute-done.8.refs_1_ = bf16[400,128]{1,0:T(8,128)(2,1)S(1)} collective-permute-done((bf16[400,128]{1,0:T(8,128)(2,1)S(1)}, bf16[400,128]{1,0:T(8,128)(2,1)S(1)}, u32[]{:S(2)}, u32[]{:S(2)}) %collective-permute-start.8) | collective-permute-done | bytes 102432 | tf_op jit(solution)/shard_map/ppermute | solution.py:88
  45.1 2.0 %collective-permute-done.14.refs_1_ = bf16[800,128]{1,0:T(8,128)(2,1)S(1)} collective-permute-done((bf16[800,128]{1,0:T(8,128)(2,1)S(1)}, bf16[800,128]{1,0:T(8,128)(2,1)S(1)}, u32[]{:S(2)}, u32[]{:S(2)}) %collective-permute-start.14) | collective-permute-done | bytes 204832 | tf_op jit(solution)/shard_map/ppermute | solution.py:88
  47.1 1.9 %weight_grad_0.1 = (f32[1168,128]{1,0:T(8,128)S(1)}, bf16[1168,128]{1,0:T(8,128)(2,1)S(1)}, bf16[1600,384]{1,0:T(8,128)(2,1)S(1)}, f32[8,128]{1,0:T(8,128)S(1)}) custom-call(bf16[800,128]{1,0:T(8,128)(2,1)S(1)} %get-tuple-element.134.refs_0_, bf16[800,128]{1,0:T(8,128)(2,1)S(1)} %collective-permute-done.14.refs_1_, ...), custom_call_target="tpu_custom_call" | custom-call | flops 1150000000 | bytes 1024 | tf_op jit(solution)/shard_map/weight_grad_0/pallas_call | solution.py:35
  49.1 3.7 %collective-permute-start.19 = (bf16[1184,128]{1,0:T(8,128)(2,1)S(1)}, bf16[1184,128]{1,0:T(8,128)(2,1)S(1)}, u32[]{:S(2)}, u32[]{:S(2)}) collective-permute-start(bf16[1184,128]{1,0:T(8,128)(2,1)S(1)} %get-tuple-element.147), channel_id=1, source_target_pairs={{0,8},{4,12},{24,16},{28,20},{1,9},{5,13},{25,17},{29,21},{2,10},{... | collective-permute-start | bytes 909320 | tf_op jit(solution)/shard_map/ppermute | solution.py:469
  52.8 1.6 %weight_grad_1.1 = (f32[1168,128]{1,0:T(8,128)S(1)}, bf16[1168,128]{1,0:T(8,128)(2,1)S(1)}, bf16[1600,384]{1,0:T(8,128)(2,1)S(1)}, f32[8,128]{1,0:T(8,128)S(1)}) custom-call(bf16[800,128]{1,0:T(8,128)(2,1)S(1)} %get-tuple-element.133.refs_0_, bf16[800,128]{1,0:T(8,128)(2,1)S(1)} %collective-permute-done.13.refs_1_, ...), custom_call_target="tpu_custom_call" | custom-call | bytes 1024 | tf_op jit(solution)/shard_map/weight_grad_1/pallas_call | solution.py:35
  54.7 1.6 %collective-permute-start.21 = (bf16[1184,128]{1,0:T(8,128)(2,1)S(1)}, bf16[1184,128]{1,0:T(8,128)(2,1)S(1)}, u32[]{:S(2)}, u32[]{:S(2)}) collective-permute-start(bf16[1184,128]{1,0:T(8,128)(2,1)S(1)} %get-tuple-element.150), channel_id=1, source_target_pairs={{0,8},{4,12},{24,16},{28,20},{1,9},{5,13},{25,17},{29,21},{2,10},{... | collective-permute-start | bytes 909320 | tf_op jit(solution)/shard_map/ppermute | solution.py:469
  56.4 3.9 %collective-permute-done.19.refs_2_ = bf16[1184,128]{1,0:T(8,128)(2,1)S(1)} collective-permute-done((bf16[1184,128]{1,0:T(8,128)(2,1)S(1)}, bf16[1184,128]{1,0:T(8,128)(2,1)S(1)}, u32[]{:S(2)}, u32[]{:S(2)}) %collective-permute-start.19) | collective-permute-done | bytes 303136 | tf_op jit(solution)/shard_map/ppermute | solution.py:469
  61.1 7.4 %collective-permute-start.18 = (bf16[1184,128]{1,0:T(8,128)(2,1)S(1)}, bf16[1184,128]{1,0:T(8,128)(2,1)S(1)}, u32[]{:S(2)}, u32[]{:S(2)}) collective-permute-start(bf16[1184,128]{1,0:T(8,128)(2,1)S(1)} %get-tuple-element.146), channel_id=1, source_target_pairs={{0,8},{4,12},{24,16},{28,20},{1,9},{5,13},{25,17},{29,21},{2,10},{... | collective-permute-start | bytes 909320 | tf_op jit(solution)/shard_map/ppermute | solution.py:469
  68.5 2.9 %input_grad.1 = (f32[1600,256]{1,0:T(8,128)S(1)}, f32[8,128]{1,0:T(8,128)S(1)}) custom-call(bf16[3,9,256,128]{3,2,1,0:T(8,128)(2,1)S(1)} %copy-done, bf16[1600,384]{1,0:T(8,128)(2,1)S(1)} %get-tuple-element.151.refs_1_, bf16[1600,384]{1,0:T(8,128)(2,1)S(1)} %get-tuple-element.152.refs_2_, bf16[1600,384]{1,0:T(8,128)(2,1)S(1)} %get-tuple-element.153.refs_3_, ...), custom_call_target="tpu_custom_call" | custom-call | flops 57500000 | bytes 1024 | tf_op jit(solution)/shard_map/input_grad/pallas_call | solution.py:35
  76.2 1.5 %collective-permute-start.26 = (bf16[400,256]{1,0:T(8,128)(2,1)S(1)}, bf16[400,256]{1,0:T(8,128)(2,1)S(1)}, u32[]{:S(2)}, u32[]{:S(2)}) collective-permute-start(bf16[400,256]{1,0:T(8,128)(2,1)S(1)} %get-tuple-element.170), channel_id=1, source_target_pairs={{0,2},{1,3},{2,0},{3,1},{4,6},{5,7},{6,4},{7,5},{8,10},{9,11},{10,... | collective-permute-start | bytes 614408 | tf_op jit(solution)/shard_map/ppermute | solution.py:350
  77.6 5.3 %collective-permute-done.23.refs_1_ = bf16[1184,128]{1,0:T(8,128)(2,1)S(1)} collective-permute-done((bf16[1184,128]{1,0:T(8,128)(2,1)S(1)}, bf16[1184,128]{1,0:T(8,128)(2,1)S(1)}, u32[]{:S(2)}, u32[]{:S(2)}) %collective-permute-start.23) | collective-permute-done | bytes 303136 | tf_op jit(solution)/shard_map/ppermute | solution.py:481
  87.0 2.6 %collective-permute-done.27.refs_3_ = bf16[400,256]{1,0:T(8,128)(2,1)S(1)} collective-permute-done((bf16[400,256]{1,0:T(8,128)(2,1)S(1)}, bf16[400,256]{1,0:T(8,128)(2,1)S(1)}, u32[]{:S(2)}, u32[]{:S(2)}) %collective-permute-start.27) | collective-permute-done | bytes 204832 | tf_op jit(solution)/shard_map/ppermute | solution.py:350
  91.7 3.4 %collective-permute-done.28.refs_1_ = bf16[1184,128]{1,0:T(8,128)(2,1)S(1)} collective-permute-done((bf16[1184,128]{1,0:T(8,128)(2,1)S(1)}, bf16[1184,128]{1,0:T(8,128)(2,1)S(1)}, u32[]{:S(2)}, u32[]{:S(2)}) %collective-permute-start.28) | collective-permute-done | bytes 303136 | tf_op jit(solution)/shard_map/ppermute | solution.py:481
  96.9 1.7 %weight_out_b.1 = (f32[3,9,256,128]{3,2,1,0:T(8,128)}, f32[3,128]{1,0:T(4,128)}, f32[8,128]{1,0:T(8,128)}) custom-call(bf16[1184,128]{1,0:T(8,128)(2,1)S(1)} %collective-permute-done.30.refs_0_, bf16[1184,128]{1,0:T(8,128)(2,1)S(1)} %get-tuple-element.179.refs_1_.refs_3_, ...), custom_call_target="tpu_custom_call", output_to_operand_aliasing={{0}: (5, {})} | custom-call | flops 57500000 | bytes 1024 | tf_op jit(solution)/shard_map/weight_out_b/pallas_call | solution.py:35
  (85 shorter events, 28.9 us)
Async XLA Ops:
  2.2 8.9 %collective-permute-start = (bf16[400,256]{1,0:T(8,128)(2,1)S(1)}, bf16[400,256]{1,0:T(8,128)(2,1)S(1)}, u32[]{:S(2)}, u32[]{:S(2)}) collective-permute-start(bf16[400,256]{1,0:T(8,128)(2,1)S(1)} %get-tuple-element.97), channel_id=1, source_target_pairs={{0,1},{1,0},{2,3},{3,2},{4,5},{5,4},{6,7},{7,6},{8,9},{9,8},{10,11... | collective-permute-start | bytes 614408 | tf_op jit(solution)/shard_map/ppermute | solution.py:350
  5.2 10.9 %collective-permute-start.1 = (bf16[400,256]{1,0:T(8,128)(2,1)S(1)}, bf16[400,256]{1,0:T(8,128)(2,1)S(1)}, u32[]{:S(2)}, u32[]{:S(2)}) collective-permute-start(bf16[400,256]{1,0:T(8,128)(2,1)S(1)} %get-tuple-element.98), channel_id=1, source_target_pairs={{0,2},{1,3},{2,0},{3,1},{4,6},{5,7},{6,4},{7,5},{8,10},{9,11},{10,... | collective-permute-start | bytes 614408 | tf_op jit(solution)/shard_map/ppermute | solution.py:350
  6.7 9.4 %collective-permute-start.2 = (bf16[400,256]{1,0:T(8,128)(2,1)S(1)}, bf16[400,256]{1,0:T(8,128)(2,1)S(1)}, u32[]{:S(2)}, u32[]{:S(2)}) collective-permute-start(bf16[400,256]{1,0:T(8,128)(2,1)S(1)} %get-tuple-element.99), channel_id=1, source_target_pairs={{0,3},{1,2},{2,1},{3,0},{4,7},{5,6},{6,5},{7,4},{8,11},{9,10},{10,... | collective-permute-start | bytes 614408 | tf_op jit(solution)/shard_map/ppermute | solution.py:350
  17.8 5.8 %collective-permute-start.4 = (bf16[800,128]{1,0:T(8,128)(2,1)S(1)}, bf16[800,128]{1,0:T(8,128)(2,1)S(1)}, u32[]{:S(2)}, u32[]{:S(2)}) collective-permute-start(bf16[800,128]{1,0:T(8,128)(2,1)S(1)} %get-tuple-element.105), channel_id=1, source_target_pairs={{0,1},{1,0},{2,3},{3,2},{4,6},{5,7},{6,4},{7,5},{8,9},{9,8},{10,11... | collective-permute-start | bytes 614408 | tf_op jit(solution)/shard_map/ppermute | solution.py:88
  21.5 6.3 %collective-permute-start.3 = (bf16[800,128]{1,0:T(8,128)(2,1)S(1)}, bf16[800,128]{1,0:T(8,128)(2,1)S(1)}, u32[]{:S(2)}, u32[]{:S(2)}) collective-permute-start(bf16[800,128]{1,0:T(8,128)(2,1)S(1)} %get-tuple-element.103), channel_id=1, source_target_pairs={{0,1},{1,0},{2,3},{3,2},{4,6},{5,7},{6,4},{7,5},{8,9},{9,8},{10,11... | collective-permute-start | bytes 614408 | tf_op jit(solution)/shard_map/ppermute | solution.py:88
  23.7 5.9 %collective-permute-start.7 = (bf16[400,128]{1,0:T(8,128)(2,1)S(1)}, bf16[400,128]{1,0:T(8,128)(2,1)S(1)}, u32[]{:S(2)}, u32[]{:S(2)}) collective-permute-start(bf16[400,128]{1,0:T(8,128)(2,1)S(1)} %get-tuple-element.114), channel_id=1, source_target_pairs={{0,2},{1,3},{2,0},{3,1},{4,5},{5,4},{6,7},{7,6},{8,10},{9,11},{10,... | collective-permute-start | bytes 307208 | tf_op jit(solution)/shard_map/ppermute | solution.py:88
  27.7 6.1 %collective-permute-start.6 = (bf16[800,128]{1,0:T(8,128)(2,1)S(1)}, bf16[800,128]{1,0:T(8,128)(2,1)S(1)}, u32[]{:S(2)}, u32[]{:S(2)}) collective-permute-start(bf16[800,128]{1,0:T(8,128)(2,1)S(1)} %get-tuple-element.112), channel_id=1, source_target_pairs={{0,1},{1,0},{2,3},{3,2},{4,6},{5,7},{6,4},{7,5},{8,9},{9,8},{10,11... | collective-permute-start | bytes 614408 | tf_op jit(solution)/shard_map/ppermute | solution.py:88
  27.9 6.3 %collective-permute-start.5 = (bf16[400,128]{1,0:T(8,128)(2,1)S(1)}, bf16[400,128]{1,0:T(8,128)(2,1)S(1)}, u32[]{:S(2)}, u32[]{:S(2)}) collective-permute-start(bf16[400,128]{1,0:T(8,128)(2,1)S(1)} %get-tuple-element.110), channel_id=1, source_target_pairs={{0,2},{1,3},{2,0},{3,1},{4,5},{5,4},{6,7},{7,6},{8,10},{9,11},{10,... | collective-permute-start | bytes 307208 | tf_op jit(solution)/shard_map/ppermute | solution.py:88
  29.7 6.5 %collective-permute-start.9 = (bf16[400,128]{1,0:T(8,128)(2,1)S(1)}, bf16[400,128]{1,0:T(8,128)(2,1)S(1)}, u32[]{:S(2)}, u32[]{:S(2)}) collective-permute-start(bf16[400,128]{1,0:T(8,128)(2,1)S(1)} %get-tuple-element.121.refs_0_), channel_id=1, source_target_pairs={{0,2},{1,3},{2,0},{3,1},{4,5},{5,4},{6,7},{7,6},{8,10},{9,11},{10,... | collective-permute-start | bytes 307208 | tf_op jit(solution)/shard_map/ppermute | solution.py:88
  34.4 6.9 %collective-permute-start.12 = (bf16[400,128]{1,0:T(8,128)(2,1)S(1)}, bf16[400,128]{1,0:T(8,128)(2,1)S(1)}, u32[]{:S(2)}, u32[]{:S(2)}) collective-permute-start(bf16[400,128]{1,0:T(8,128)(2,1)S(1)} %get-tuple-element.129.refs_0_), channel_id=1, source_target_pairs={{0,2},{1,3},{2,0},{3,1},{4,5},{5,4},{6,7},{7,6},{8,10},{9,11},{10,... | collective-permute-start | bytes 307208 | tf_op jit(solution)/shard_map/ppermute | solution.py:88
  36.3 5.8 %collective-permute-start.11 = (bf16[800,128]{1,0:T(8,128)(2,1)S(1)}, bf16[800,128]{1,0:T(8,128)(2,1)S(1)}, u32[]{:S(2)}, u32[]{:S(2)}) collective-permute-start(bf16[800,128]{1,0:T(8,128)(2,1)S(1)} %get-tuple-element.127.refs_0_), channel_id=1, source_target_pairs={{0,1},{1,0},{2,3},{3,2},{4,6},{5,7},{6,4},{7,5},{8,9},{9,8},{10,11... | collective-permute-start | bytes 614408 | tf_op jit(solution)/shard_map/ppermute | solution.py:88
  44.0 8.8 %collective-permute-start.13 = (bf16[800,128]{1,0:T(8,128)(2,1)S(1)}, bf16[800,128]{1,0:T(8,128)(2,1)S(1)}, u32[]{:S(2)}, u32[]{:S(2)}) collective-permute-start(bf16[800,128]{1,0:T(8,128)(2,1)S(1)} %get-tuple-element.133.refs_0_), channel_id=1, source_target_pairs={{0,1},{1,0},{2,3},{3,2},{4,6},{5,7},{6,4},{7,5},{8,9},{9,8},{10,11... | collective-permute-start | bytes 614408 | tf_op jit(solution)/shard_map/ppermute | solution.py:88
  49.1 11.2 %collective-permute-start.19 = (bf16[1184,128]{1,0:T(8,128)(2,1)S(1)}, bf16[1184,128]{1,0:T(8,128)(2,1)S(1)}, u32[]{:S(2)}, u32[]{:S(2)}) collective-permute-start(bf16[1184,128]{1,0:T(8,128)(2,1)S(1)} %get-tuple-element.147), channel_id=1, source_target_pairs={{0,8},{4,12},{24,16},{28,20},{1,9},{5,13},{25,17},{29,21},{2,10},{... | collective-permute-start | bytes 909320 | tf_op jit(solution)/shard_map/ppermute | solution.py:469
  54.7 16.8 %collective-permute-start.21 = (bf16[1184,128]{1,0:T(8,128)(2,1)S(1)}, bf16[1184,128]{1,0:T(8,128)(2,1)S(1)}, u32[]{:S(2)}, u32[]{:S(2)}) collective-permute-start(bf16[1184,128]{1,0:T(8,128)(2,1)S(1)} %get-tuple-element.150), channel_id=1, source_target_pairs={{0,8},{4,12},{24,16},{28,20},{1,9},{5,13},{25,17},{29,21},{2,10},{... | collective-permute-start | bytes 909320 | tf_op jit(solution)/shard_map/ppermute | solution.py:469
  60.4 12.0 %collective-permute-start.20 = (bf16[1184,128]{1,0:T(8,128)(2,1)S(1)}, bf16[1184,128]{1,0:T(8,128)(2,1)S(1)}, u32[]{:S(2)}, u32[]{:S(2)}) collective-permute-start(bf16[1184,128]{1,0:T(8,128)(2,1)S(1)} %get-tuple-element.149.refs_0_), channel_id=1, source_target_pairs={{8,16},{12,20},{16,8},{20,12},{9,17},{13,21},{17,9},{21,13},{10,18... | collective-permute-start | bytes 909320 | tf_op jit(solution)/shard_map/ppermute | solution.py:474
  61.1 12.8 %collective-permute-start.18 = (bf16[1184,128]{1,0:T(8,128)(2,1)S(1)}, bf16[1184,128]{1,0:T(8,128)(2,1)S(1)}, u32[]{:S(2)}, u32[]{:S(2)}) collective-permute-start(bf16[1184,128]{1,0:T(8,128)(2,1)S(1)} %get-tuple-element.146), channel_id=1, source_target_pairs={{0,8},{4,12},{24,16},{28,20},{1,9},{5,13},{25,17},{29,21},{2,10},{... | collective-permute-start | bytes 909320 | tf_op jit(solution)/shard_map/ppermute | solution.py:469
  72.4 10.5 %collective-permute-start.23 = (bf16[1184,128]{1,0:T(8,128)(2,1)S(1)}, bf16[1184,128]{1,0:T(8,128)(2,1)S(1)}, u32[]{:S(2)}, u32[]{:S(2)}) collective-permute-start(bf16[1184,128]{1,0:T(8,128)(2,1)S(1)} %get-tuple-element.161.refs_0_), channel_id=1, source_target_pairs={{8,0},{12,4},{16,24},{20,28},{9,1},{13,5},{17,25},{21,29},{10,2},{... | collective-permute-start | bytes 909320 | tf_op jit(solution)/shard_map/ppermute | solution.py:481
  74.0 10.8 %collective-permute-start.22 = (bf16[1184,128]{1,0:T(8,128)(2,1)S(1)}, bf16[1184,128]{1,0:T(8,128)(2,1)S(1)}, u32[]{:S(2)}, u32[]{:S(2)}) collective-permute-start(bf16[1184,128]{1,0:T(8,128)(2,1)S(1)} %get-tuple-element.160.refs_0_), channel_id=1, source_target_pairs={{8,16},{12,20},{16,8},{20,12},{9,17},{13,21},{17,9},{21,13},{10,18... | collective-permute-start | bytes 909320 | tf_op jit(solution)/shard_map/ppermute | solution.py:474
  74.8 15.9 %collective-permute-start.29 = (bf16[1184,128]{1,0:T(8,128)(2,1)S(1)}, bf16[1184,128]{1,0:T(8,128)(2,1)S(1)}, u32[]{:S(2)}, u32[]{:S(2)}) collective-permute-start(bf16[1184,128]{1,0:T(8,128)(2,1)S(1)} %get-tuple-element.175.refs_0_), channel_id=1, source_target_pairs={{8,0},{12,4},{16,24},{20,28},{9,1},{13,5},{17,25},{21,29},{10,2},{... | collective-permute-start | bytes 909320 | tf_op jit(solution)/shard_map/ppermute | solution.py:481
  76.1 10.9 %collective-permute-start.25 = (bf16[400,256]{1,0:T(8,128)(2,1)S(1)}, bf16[400,256]{1,0:T(8,128)(2,1)S(1)}, u32[]{:S(2)}, u32[]{:S(2)}) collective-permute-start(bf16[400,256]{1,0:T(8,128)(2,1)S(1)} %get-tuple-element.169), channel_id=1, source_target_pairs={{0,1},{1,0},{2,3},{3,2},{4,5},{5,4},{6,7},{7,6},{8,9},{9,8},{10,11... | collective-permute-start | bytes 614408 | tf_op jit(solution)/shard_map/ppermute | solution.py:350
  76.2 10.8 %collective-permute-start.26 = (bf16[400,256]{1,0:T(8,128)(2,1)S(1)}, bf16[400,256]{1,0:T(8,128)(2,1)S(1)}, u32[]{:S(2)}, u32[]{:S(2)}) collective-permute-start(bf16[400,256]{1,0:T(8,128)(2,1)S(1)} %get-tuple-element.170), channel_id=1, source_target_pairs={{0,2},{1,3},{2,0},{3,1},{4,6},{5,7},{6,4},{7,5},{8,10},{9,11},{10,... | collective-permute-start | bytes 614408 | tf_op jit(solution)/shard_map/ppermute | solution.py:350
  82.9 6.7 %collective-permute-start.27 = (bf16[400,256]{1,0:T(8,128)(2,1)S(1)}, bf16[400,256]{1,0:T(8,128)(2,1)S(1)}, u32[]{:S(2)}, u32[]{:S(2)}) collective-permute-start(bf16[400,256]{1,0:T(8,128)(2,1)S(1)} %get-tuple-element.171), channel_id=1, source_target_pairs={{0,3},{1,2},{2,1},{3,0},{4,7},{5,6},{6,5},{7,4},{8,11},{9,10},{10,... | collective-permute-start | bytes 614408 | tf_op jit(solution)/shard_map/ppermute | solution.py:350
  84.9 10.3 %collective-permute-start.28 = (bf16[1184,128]{1,0:T(8,128)(2,1)S(1)}, bf16[1184,128]{1,0:T(8,128)(2,1)S(1)}, u32[]{:S(2)}, u32[]{:S(2)}) collective-permute-start(bf16[1184,128]{1,0:T(8,128)(2,1)S(1)} %get-tuple-element.174.refs_0_), channel_id=1, source_target_pairs={{8,0},{12,4},{16,24},{20,28},{9,1},{13,5},{17,25},{21,29},{10,2},{... | collective-permute-start | bytes 909320 | tf_op jit(solution)/shard_map/ppermute | solution.py:481
  87.0 8.4 %collective-permute-start.31 = (bf16[1184,128]{1,0:T(8,128)(2,1)S(1)}, bf16[1184,128]{1,0:T(8,128)(2,1)S(1)}, u32[]{:S(2)}, u32[]{:S(2)}) collective-permute-start(bf16[1184,128]{1,0:T(8,128)(2,1)S(1)} %get-tuple-element.181.refs_4_), channel_id=1, source_target_pairs={{0,4},{4,0},{8,12},{12,8},{16,20},{20,16},{24,28},{28,24},{1,5},{5... | collective-permute-start | bytes 909320 | tf_op jit(solution)/shard_map/ppermute | solution.py:510
  (13 other events, 44.1 us)

commit v4 on v3

--- a/solution.py
+++ b/solution.py
@@ -17,27 +17,31 @@
     return -(-columns // 8) * 8
 
 
-COSTS = {"input_grad": 0.05, "add_near_0": 0.05, "add_near_1": 0.05, "add_near_2": 0, "split_rows": 0.05, "add_far_0": 0.05, "add_far_1": 0.05, "add_far_2": 0.05, "merge_branches": 0.05, "join_channels": 0.05, "choose_0": 1, "choose_1": 0.05, "choose_2": 0.05, "weight_out_a": 0.05, "weight_out_b": 0.05, "add_cores_2": 1, "join_1": 3, "add_cores_0": 0, "add_cores_1": 0, "weight_grad_1": 0}
+COSTS = {"input_grad": 0.05, "add_near_0": 0.05, "add_near_2": 0.05, "add_near_1": 0, "split_rows": 0.05, "add_far_0": 0.05, "add_far_2": 0.05, "add_far_1": 0.05, "merge_branches": 0.05, "join_channels": 0.05, "choose_0": 0.05, "choose_2": 0.05, "choose_1": 0.05, "weight_out_a": 0.05, "weight_out_b": 0.05, "add_cores_1": 1, "join_2": 3, "add_cores_0": 0, "add_cores_2": 0, "weight_grad_2": 0, "pass_on": 0.05, "weight_out_c": 0.05}
 UNIT = 1_150_000_000
 
 
-def call(chain, kernel, ins, outs, scratch, name, in_specs=None, out_specs=None, aliases=None):
+def call(
+    chain, kernel, ins, outs, scratch, name, in_specs=None, out_specs=None, aliases=None, last=False
+):
     after = chain[-1:]
     vmem = pl.BlockSpec(memory_space=pltpu.VMEM)
     specs = list(in_specs or [vmem] * len(ins)) + [pl.BlockSpec(memory_space=pl.ANY)] * len(after)
     n, m, k = len(ins), len(after), len(outs)
 
     def body(*refs):
-        token = refs[n + m + k]
-        token[...] = jnp.zeros(token.shape, F32)
-        kernel(*refs[:n], *refs[n + m : n + m + k], *refs[n + m + k + 1 :])
-
-    *got, token = pl.pallas_call(
+        rest = refs[n + m + k :]
+        if not last:
+            rest[0][...] = jnp.zeros(rest[0].shape, F32)
+            rest = rest[1:]
+        kernel(*refs[:n], *refs[n + m : n + m + k], *rest)
+
+    got = pl.pallas_call(
         body,
         grid=(1,),
-        out_shape=(*outs, shape((8, 128), F32)),
+        out_shape=(*outs, *([] if last else [shape((8, 128), F32)])),
         in_specs=specs,
-        out_specs=(*(out_specs or [vmem] * k), vmem),
+        out_specs=(*(out_specs or [vmem] * k), *([] if last else [vmem])),
         scratch_shapes=scratch,
         name=name,
         input_output_aliases=aliases or {},
@@ -46,8 +50,10 @@
             flops=int(COSTS.get(name, 1.0) * UNIT), bytes_accessed=1024, transcendentals=0
         ),
     )(*ins, *after)
-    chain.append(token)
-    return got
+    if last:
+        return list(got)
+    chain.append(got[-1])
+    return list(got[:-1])
 
 
 def shape(dims, kind):
@@ -191,15 +197,25 @@
         act_ref[0, r] = scr[stride * r : stride * r + columns].astype(BF)
 
 
-def weight_kernel(dims, spacing, parts, mine, theirs, feat, keep, *refs):
+def corner_rows(slab, rows, stride, column):
+    return jnp.concatenate([slab[stride * r + column : stride * r + column + 1] for r in range(rows)])
+
+
+def in_slot(x, slots):
+    row = lax.broadcasted_iota(jnp.int32, (slots * x.shape[0], x.shape[1]), 0)
+    mine = row // x.shape[0] == lax.axis_index("dp")
+    return jnp.where(mine, jnp.concatenate([x] * slots), 0.0)
+
+
+def weight_kernel(dims, spacing, parts, near, mine, theirs, feat, keep, *refs):
     columns, stride = dims
     send, gstack, gpad, ghalf, full = refs
     core = lax.axis_index("dp") % 2
     total = gstack.shape[0]
     outputs = gpad.shape[1]
-    size = total // parts
     gpad[0:stride] = jnp.zeros((stride, outputs), F32)
     gpad[stride + total :] = jnp.zeros((stride, outputs), F32)
+    size = total // parts
     for q in range(parts):
         block = (mine, theirs)[2 * q // parts][...].astype(F32)
         at = q % (parts // 2) * size
@@ -207,6 +223,7 @@
         gpad[pl.ds(to, size)] = block[at : at + size]
     shifted_copies(gpad, ghalf, gstack, columns, stride, (spacing, 0, -spacing))
     step = spacing * stride
+    at = 0
     for a in range(3):
         if a == 0:
             f, g = feat[: total - step], gstack[step:]
@@ -214,20 +231,41 @@
             f, g = feat[...], gstack[...]
         else:
             f, g = feat[step:], gstack[: total - step]
+        taps = (1,) if near and a != 1 else (0, 1, 2)
+        if len(taps) == 1:
+            g = g[:, outputs : 2 * outputs]
         r = mm(f, g, 0, 0)
-        for c in range(3):
-            full[3 * a + c] = r[:, c * outputs : (c + 1) * outputs]
+        for c in range(len(taps)):
+            full[at + c] = r[:, c * outputs : (c + 1) * outputs]
+        at += len(taps)
     half = full.shape[1] // 2
-    body = 9 * half
-    own = full[:, pl.ds(pl.multiple_of(core * half, half), half)]
-    other = full[:, pl.ds(pl.multiple_of((1 - core) * half, half), half)]
+    body = at * half
+    own = full[:at, pl.ds(pl.multiple_of(core * half, half), half)]
+    other = full[:at, pl.ds(pl.multiple_of((1 - core) * half, half), half)]
     keep[:body] = own.reshape(body, outputs)
     send[:body] = other.reshape(body, outputs).astype(BF)
     total_bias = jnp.sum(gpad[...], axis=0, keepdims=True)
     row = lax.broadcasted_iota(jnp.int32, (EXTRA, outputs), 0)
     own_bias = jnp.where(row == 0, total_bias, 0.0)
-    keep[body:] = own_bias
-    send[body:] = pack_extra(own_bias)
+    keep[body : body + EXTRA] = own_bias
+    send[body : body + EXTRA] = pack_extra(own_bias)
+    if near:
+        slots = lax.axis_size("dp")
+        ends = (0, total - near * stride)
+        last = columns - 1
+        fs = [feat[e : e + near * stride].astype(F32) for e in ends]
+        gs = [gpad[stride + e : stride + e + near * stride] for e in ends]
+        at, n = body + EXTRA, near * slots
+        for a in range(2):
+            for c in range(2):
+                f = in_slot(corner_rows(fs[a], near, stride, c * last), slots)
+                g = in_slot(corner_rows(gs[1 - a], near, stride, (1 - c) * last), slots)
+                first = core == 0
+                keep[at : at + n] = jnp.where(first, f[:, :half], f[:, half:])
+                send[at : at + n] = jnp.where(first, f[:, half:], f[:, :half]).astype(BF)
+                keep[at + 4 * n : at + 5 * n] = g
+                send[at + 4 * n : at + 5 * n] = g.astype(BF)
+                at += n
 
 
 def pack_extra(x):
@@ -239,23 +277,51 @@
 
 def add_pack_kernel(body, *refs):
     ins, out_ref = refs[:-1], refs[-1]
-    end = body + EXTRA
-    total = ins[0][:end].astype(F32)
+    n = ins[0].shape[0]
+    for x in ins:
+        n = min(n, x.shape[0])
+    total = ins[0][:n].astype(F32)
     for x in ins[1:]:
-        total = total + x[:end].astype(F32)
-    out_ref[:body] = total[:body].astype(BF)
-    out_ref[body:end] = pack_extra(total[body:])
-    if out_ref.shape[0] > end:
-        out_ref[end:] = jnp.zeros((out_ref.shape[0] - end, out_ref.shape[1]), BF)
-
-
-def put_half(x, out, buf, sem, place, at, scale):
+        total = total + x[:n].astype(F32)
+    out_ref[:n] = total.astype(BF)
+    out_ref[body : body + EXTRA] = pack_extra(total[body : body + EXTRA])
+    if out_ref.shape[0] > n:
+        out_ref[n:] = jnp.zeros((out_ref.shape[0] - n, out_ref.shape[1]), BF)
+
+
+def put_half(x, near, out, buf, sems, place, at, scale):
     half, outputs = buf.shape[1:]
-    buf[...] = (x[: 9 * half].astype(F32) * scale).reshape(9, half, outputs)
     rows = pl.ds(pl.multiple_of(at * half, half), half)
-    copy = pltpu.make_async_copy(buf, out.at[place, :, rows], sem)
-    copy.start()
-    return copy
+    copies = []
+
+    def send(first, count):
+        sem = sems.at[len(copies)]
+        src, dst = buf.at[first : first + count], out.at[place, first : first + count, rows]
+        copies.append(pltpu.make_async_copy(src, dst, sem))
+        copies[-1].start()
+
+    if not near:
+        for a in range(3):
+            part = x[3 * a * half : 3 * (a + 1) * half].astype(F32) * scale
+            buf[3 * a : 3 * a + 3] = part.reshape(3, half, outputs)
+            send(3 * a, 3)
+        return copies
+    i = 0
+    for first, count in ((1, 1), (3, 3), (7, 1)):
+        part = x[i * half : (i + count) * half].astype(F32) * scale
+        buf[first : first + count] = part.reshape(count, half, outputs)
+        send(first, count)
+        i += count
+    n = near * lax.axis_size("dp")
+    start = 5 * half + EXTRA
+    f, g = x[start : start + 4 * n], x[start + 4 * n : start + 8 * n].astype(F32)
+    corner = lax.broadcasted_iota(jnp.int32, g.shape, 0) // n
+    spread = jnp.concatenate([jnp.where(corner == i, g, 0.0) for i in range(4)], axis=1)
+    r = mm(f, spread.astype(BF), 0, 0) * scale
+    for i, t in enumerate((0, 2, 6, 8)):
+        buf[t] = r[:, i * outputs : (i + 1) * outputs]
+        send(t, 1)
+    return copies
 
 
 def choose_kernel(scale, place, lined, *refs):
@@ -269,7 +335,8 @@
         return
     own, out, buf, sem = outs[-4:]
     own[...] = inner
-    put_half(inner, out, buf, sem, place, lax.axis_index("dp") % 2, scale).wait()
+    for copy in put_half(inner, 0, out, buf, sem, place, lax.axis_index("dp") % 2, scale):
+        copy.wait()
 
 
 def weight_out_kernel(scale, halves, *refs):
@@ -277,15 +344,16 @@
     out, bufs, sems = refs[-3:]
     core = lax.axis_index("dp") % 2
     copies = []
-    for i, (place, own) in enumerate(halves):
+    for i, (place, own, near) in enumerate(halves):
         at = core if own else 1 - core
-        copies.append(put_half(refs[i], out, bufs.at[i], sems.at[i], place, at, scale))
+        copies += put_half(refs[i], near, out, bufs.at[i], sems.at[i], place, at, scale)
     for copy in copies:
         copy.wait()
 
 
-def bias_kernel(scale, body, ins, out):
+def bias_kernel(scale, bodies, ins, out):
     for k, x in enumerate(ins):
+        body = bodies[k]
         total = jnp.sum(x[body : body + EXTRA].astype(F32), axis=0, keepdims=True)
         out[k : k + 1, :] = total * scale
 
@@ -319,21 +387,38 @@
 
 
 def split_rows_kernel(parts, acc, *outs):
+    size = acc.shape[0] // parts
+    if len(outs) == 3:
+        outs[0][...] = take_rows(acc, [0], size, parts).astype(BF)
+        outs[1][...] = take_rows(acc, [1], size, parts).astype(BF)
+        outs[2][...] = take_rows(acc, [2, 3], size, parts).astype(BF)
+        return
     me = lax.axis_index("space")
-    size = outs[0].shape[0]
     for b in range(parts):
         at = pl.multiple_of((me ^ b) * size, 8)
         outs[b][...] = acc[pl.ds(at, size)].astype(BF)
 
 
+def pass_on_kernel(own, got, out):
+    size = own.shape[0]
+    out[:size] = own[...]
+    out[size:] = got[size:]
+
+
 def join_kernel(dims, parts, *refs):
     rows, columns, stride = dims
-    blocks, out_ref, scr = refs[:parts], refs[parts], refs[parts + 1]
+    blocks, out_ref, scr = refs[:-2], refs[-2], refs[-1]
     me = lax.axis_index("space")
-    width = blocks[0].shape[1]
-    for b in range(parts):
-        at = pl.multiple_of((me ^ b) * width, width)
-        scr[:, pl.ds(at, width)] = blocks[b][...].astype(F32)
+    width, size = blocks[0].shape[1], scr.shape[0]
+    if len(blocks) == 3:
+        parted = [(blocks[0], 0), (blocks[2], 0), (blocks[1], 0), (blocks[2], 1)]
+        places = [owner(q, parts) for q in range(4)]
+    else:
+        parted = [(block, 0) for block in blocks]
+        places = [me ^ b for b in range(parts)]
+    for (block, n), place in zip(parted, places):
+        at = pl.multiple_of(place * width, width)
+        scr[:, pl.ds(at, width)] = block[n * size : (n + 1) * size].astype(F32)
     for r in range(rows):
         out_ref[0, r] = scr[stride * r : stride * r + columns].astype(BF)
 
@@ -366,8 +451,21 @@
     top = levels(parts)
     cores = [(i, i ^ 1) for i in range(dp)]
     half = channels // 2
-    kept_rows = 9 * half + EXTRA
-    packed = [shape((kept_rows + 16, outputs), BF)]
+    near, body, kept_rows = [], [], []
+    for spacing in dilations:
+        few = rows * parts - spacing
+        if dp == 8 and few == 4 and columns - spacing == 1 and half == outputs and size % 16 == 0:
+            near.append(few)
+            body.append(5 * half)
+            kept_rows.append(5 * half + EXTRA + 8 * few * dp)
+        else:
+            near.append(0)
+            body.append(9 * half)
+            kept_rows.append(9 * half + EXTRA)
+
+    def packed(k):
+        return [shape((kept_rows[k] + 16, outputs), BF)]
+
     chain = []
     run = functools.partial(call, chain)
 
@@ -435,11 +533,11 @@
     def weight_part(k):
         own, got = state[k]
         keep, send, stack = run(
-            functools.partial(weight_kernel, (columns, stride), dilations[k], parts),
+            functools.partial(weight_kernel, (columns, stride), dilations[k], parts, near[k]),
             [own, got, state["feat"]],
             [
-                shape((kept_rows, outputs), F32),
-                shape((kept_rows, outputs), BF),
+                shape((kept_rows[k], outputs), F32),
+                shape((kept_rows[k], outputs), BF),
                 shape((total, 3 * outputs), BF),
             ],
             [
@@ -455,8 +553,9 @@
     def line(pairs):
         return [(2 * a + c, 2 * b + c) for a, b in pairs for c in range(2)]
 
-    def add(name, ins):
-        return run(functools.partial(add_pack_kernel, 9 * half), ins, packed, [], name)[0]
+    def add(name, k, ins):
+        kernel = functools.partial(add_pack_kernel, body[k])
+        return run(kernel, ins, packed(k), [], f"{name}_{k}")[0]
 
     def add_cores(k):
         got = state["sum", k]
@@ -465,19 +564,19 @@
             groups = [[2 * i + c for i in range(dp // 2)] for c in range(2)]
             state["sum", k] = lax.psum(kept, "dp", axis_index_groups=groups)
             return
-        near = add(f"add_cores_{k}", got)
+        near = add("add_cores", k, got)
         state["sum", k] = got + [lax.ppermute(near, "dp", line([(0, 1), (3, 2)]))]
 
     def add_near(k):
         if dp == 8:
-            near = add(f"add_near_{k}", state["sum", k])
+            near = add("add_near", k, state["sum", k])
             state["sum", k] = [near, lax.ppermute(near, "dp", line([(1, 2), (2, 1)]))]
 
     def add_far(k):
         if dp != 8:
-            state["sum", k] = [add(f"round_{k}", [state["sum", k]])]
+            state["sum", k] = [add("round", k, [state["sum", k]])]
             return
-        far_sum = add(f"add_far_{k}", state["sum", k])
+        far_sum = add("add_far", k, state["sum", k])
         state["sum", k] = [far_sum, lax.ppermute(far_sum, "dp", line([(1, 0), (2, 3)]))]
 
     anywhere = pl.BlockSpec(memory_space=pl.ANY)
@@ -485,10 +584,10 @@
 
     def choose(k, last=False):
         ins = state["sum", k]
-        place, outs, scratch, specs, out_specs, aliases = None, packed, [], None, None, None
+        place, outs, scratch, specs, out_specs, aliases = None, packed(k), [], None, None, None
         if not last:
-            place, outs = k, packed + [weight_shape]
-            scratch = [vm((9, half, outputs), F32), pltpu.SemaphoreType.DMA]
+            place, outs = k, packed(k) + [weight_shape]
+            scratch = [vm((9, half, outputs), F32), pltpu.SemaphoreType.DMA((3,))]
             out_specs = [whole, anywhere]
             if "weight_grad" in state:
                 ins = ins + [state["weight_grad"]]
@@ -509,15 +608,16 @@
         state["own", k] = got[0]
         state["sum", k] = lax.ppermute(got[0], "dp", cores)
 
-    def weight_out(name, halves, with_bias=False):
+    def weight_out(name, halves, with_bias=False, last=False):
         ins = [state["own" if own else "sum", k] for k, own in halves]
+        halves = [(k, own, near[k]) for k, own in halves]
         n = len(ins)
         extra = [state["own", k] for k in range(3)] if with_bias else []
         outs = [weight_shape] + ([shape((3, outputs), F32)] if with_bias else [])
 
         def kernel(*refs):
             if with_bias:
-                bias_kernel(1.0 / dp, 9 * half, refs[n : n + 3], refs[-3])
+                bias_kernel(1.0 / dp, body, refs[n : n + 3], refs[-3])
                 refs = (*refs[: -3], *refs[-2:])
             weight_out_kernel(1.0 / dp, halves, *refs[:n], refs[-3], *refs[-2:])
 
@@ -525,11 +625,12 @@
             kernel,
             ins + extra + [state["weight_grad"]],
             outs,
-            [vm((n, 9, half, outputs), F32), pltpu.SemaphoreType.DMA((n,))],
+            [vm((n, 9, half, outputs), F32), pltpu.SemaphoreType.DMA((n, 7))],
             name,
             in_specs=[whole] * (n + len(extra)) + [anywhere],
             out_specs=[anywhere] + [whole] * (len(outs) - 1),
             aliases={n + len(extra): 0},
+            last=last,
         )
         state["weight_grad"] = got[0]
         return got[-1]
@@ -544,10 +645,22 @@
             in_specs=[far] + [whole] * 3,
         )
 
+    two_levels = False
+
     def send_back():
-        outs = [shape((size, channels), BF)] * parts
+        counts = [1, 1, 2] if two_levels else [1] * parts
+        outs = [shape((n * size, channels), BF) for n in counts]
         back = run(functools.partial(split_rows_kernel, parts), state["back"], outs, [], "split_rows")
-        state["back"] = [back[0]] + [swap(back[b], b) for b in range(1, parts)]
+        if two_levels:
+            state["back"] = [back[0], back[1], exchange(back[2], 0, parts, dp)]
+        else:
+            state["back"] = [back[0]] + [swap(back[b], b) for b in range(1, parts)]
+
+    def pass_back():
+        own, second, got = state["back"]
+        outs = [shape((2 * size, channels), BF)]
+        on = run(pass_on_kernel, [second, got], outs, [], "pass_on")[0]
+        state["back"] = [own, got, exchange(on, 1, parts, dp)]
 
     def join_back():
         state["input_grad"] = run(
@@ -564,11 +677,11 @@
             merge_kernel, acts, [shape(grad_out.shape, BF)], [], "merge_branches"
         )[0]
 
-    k0, k1, k2 = 2, 0, 1
+    k0, k1, k2 = 1, 0, 2
     run(touch_kernel, [weights], [], [], "touch_weights", in_specs=[far])
-    forward(k0, with_feat=True)
-    forward(k1)
     if top == 2:
+        forward(k0, with_feat=True)
+        forward(k1)
         reduce_step(k0, 1)
         forward(k2)
         reduce_step(k1, 1)
@@ -594,7 +707,16 @@
         add_far(k1)
         choose(k0)
         add_far(k2)
+        merge()
+        join_back()
+        choose(k1)
+        choose(k2, last=True)
+        weight_out("weight_out_a", [(k0, False), (k1, False)])
+        bias_grad = weight_out("weight_out_b", [(k2, True)], with_bias=True)
+        weight_out("weight_out_c", [(k2, False)], last=True)
     else:
+        forward(k0, with_feat=True)
+        forward(k1)
         forward(k2)
         for k in (k0, k1, k2):
             for level in range(1, top):
@@ -611,12 +733,13 @@
         add_far(k1)
         choose(k0)
         add_far(k2)
-    merge()
-    join_back()
-    choose(k1)
-    choose(k2, last=True)
-    weight_out("weight_out_a", [(k0, False), (k1, False)])
-    bias_grad = weight_out("weight_out_b", [(k2, False), (k2, True)], with_bias=True)
+        join_back()
+        merge()
+        choose(k1)
+        choose(k2, last=True)
+        weight_out("weight_out_a", [(k0, False), (k1, False)])
+        bias_grad = weight_out("weight_out_b", [(k2, True)], with_bias=True)
+        weight_out("weight_out_c", [(k2, False)], last=True)
     return state["active"], state["input_grad"], state["weight_grad"], bias_grad
 
 

time: 99 us -> 98.1 us (level)
  waiting for transfers between devices: 37 us -> 33.9 us
  starting transfers between devices: 37 us -> 38.7 us
    ppermute x3, waiting for transfers between devices: 8.71 us -> 7.31 us  [add_far(): lax.ppermute(far_sum, 'dp', line([(1, 0), (2, 3)]))]
    ppermute x12, waiting for transfers between devices: 11.6 us -> 10.4 us  [exchange(): return lax.ppermute(x, ('dp', 'space'), pairs)]
    pallas_call x35 -> x36, Pallas kernels: 22.3 us -> 22.7 us  [call(): pl.pallas_call(body, grid=(1,), out_shape=(*outs, *([] if last else [shap...]
  transfers between devices with their start and end apart: 33 -> 33, of which waited for: 17 -> 15; matrix products, arithmetic and copies ran while one was open for 0% -> 0% of each run, Pallas kernels for 19% -> 20%
where the time goes in v4:
time: 98.1 us; the launch traced here: 97.8 us
  starting transfers between devices  38.7 us (39%)
  waiting for transfers between devices  33.9 us (35%)
  Pallas kernels  22.7 us (23%)
  local copies, waits for them, and re-layouts  1.28 us (1%)
  between operations  1.21 us (1%)
    pallas_call x36, Pallas kernels, call(): pl.pallas_call(body, grid=(1,), out_shape=(*outs, *([] if last else [shap...  22.7 us
    ppermute x3, starting transfers between devices, add_cores(): state['sum', k] = got + [lax.ppermute(near, 'dp', line([(0, 1), (3, 2)]))]  12.7 us
    ppermute x12, starting transfers between devices, exchange(): return lax.ppermute(x, ('dp', 'space'), pairs)  11.8 us
    ppermute x6, waiting for transfers between devices, swap(): return lax.ppermute(x, 'space', [(i, i ^ bit) for i in range(n)])  11.7 us
    ppermute x12, waiting for transfers between devices, exchange(): return lax.ppermute(x, ('dp', 'space'), pairs)  10.4 us
    ppermute x6, starting transfers between devices, swap(): return lax.ppermute(x, 'space', [(i, i ^ bit) for i in range(n)])  7.72 us
    ppermute x3, waiting for transfers between devices, add_far(): lax.ppermute(far_sum, 'dp', line([(1, 0), (2, 3)]))  7.31 us
    ppermute x3, waiting for transfers between devices, add_cores(): state['sum', k] = got + [lax.ppermute(near, 'dp', line([(0, 1), (3, 2)]))]  4.31 us
  transfers between devices with their start and end apart: 33, of which 15 were waited for; matrix products, arithmetic and copies ran while one was open for 0% of the time, Pallas kernels for 20%

profile of v4, /device:TPU:0, one launch (start us, length us, event | category | flops | bytes accessed | tf_op | source)
XLA Modules:
  0.0 97.8 jit_solution(13619231640431211159)
XLA Ops:
  2.2 3.0 %collective-permute-start = (bf16[400,256]{1,0:T(8,128)(2,1)S(1)}, bf16[400,256]{1,0:T(8,128)(2,1)S(1)}, u32[]{:S(2)}, u32[]{:S(2)}) collective-permute-start(bf16[400,256]{1,0:T(8,128)(2,1)S(1)} %get-tuple-element.98), channel_id=1, source_target_pairs={{0,1},{1,0},{2,3},{3,2},{4,5},{5,4},{6,7},{7,6},{8,9},{9,8},{10,11... | collective-permute-start | bytes 614408 | tf_op jit(solution)/shard_map/ppermute | solution.py:435
  5.2 1.5 %collective-permute-start.1 = (bf16[400,256]{1,0:T(8,128)(2,1)S(1)}, bf16[400,256]{1,0:T(8,128)(2,1)S(1)}, u32[]{:S(2)}, u32[]{:S(2)}) collective-permute-start(bf16[400,256]{1,0:T(8,128)(2,1)S(1)} %get-tuple-element.99), channel_id=1, source_target_pairs={{0,2},{1,3},{2,0},{3,1},{4,6},{5,7},{6,4},{7,5},{8,10},{9,11},{10,... | collective-permute-start | bytes 614408 | tf_op jit(solution)/shard_map/ppermute | solution.py:435
  6.7 4.4 %collective-permute-done.refs_2_ = bf16[400,256]{1,0:T(8,128)(2,1)S(1)} collective-permute-done((bf16[400,256]{1,0:T(8,128)(2,1)S(1)}, bf16[400,256]{1,0:T(8,128)(2,1)S(1)}, u32[]{:S(2)}, u32[]{:S(2)}) %collective-permute-start) | collective-permute-done | bytes 204832 | tf_op jit(solution)/shard_map/ppermute | solution.py:435
  11.1 5.0 %collective-permute-done.1.refs_3_ = bf16[400,256]{1,0:T(8,128)(2,1)S(1)} collective-permute-done((bf16[400,256]{1,0:T(8,128)(2,1)S(1)}, bf16[400,256]{1,0:T(8,128)(2,1)S(1)}, u32[]{:S(2)}, u32[]{:S(2)}) %collective-permute-start.1) | collective-permute-done | bytes 204832 | tf_op jit(solution)/shard_map/ppermute | solution.py:435
  16.1 2.0 %forward_1.1 = (f32[800,128]{1,0:T(8,128)S(1)}, bf16[800,128]{1,0:T(8,128)(2,1)S(1)}, bf16[1600,256]{1,0:T(8,128)(2,1)S(1)}, f32[8,128]{1,0:T(8,128)S(1)}) custom-call(bf16[3,9,256,128]{3,2,1,0:T(8,128)(2,1)S(1)} %copy-done, bf16[400,256]{1,0:T(8,128)(2,1)S(1)} %get-tuple-element.97.refs_1_, bf16[400,256]{1,0:T(8,128)(2,1)S(1)} %collective-permute-done.refs_2_, ...), custom_call_target="tpu_custom_call" | custom-call | flops 1150000000 | bytes 1024 | tf_op jit(solution)/shard_map/forward_1/pallas_call | solution.py:39
  19.4 2.5 %forward_0.1 = (f32[800,128]{1,0:T(8,128)S(1)}, bf16[800,128]{1,0:T(8,128)(2,1)S(1)}, f32[8,128]{1,0:T(8,128)S(1)}) custom-call(bf16[3,9,256,128]{3,2,1,0:T(8,128)(2,1)S(1)} %copy-done, bf16[400,256]{1,0:T(8,128)(2,1)S(1)} %get-tuple-element.97.refs_1_, bf16[400,256]{1,0:T(8,128)(2,1)S(1)} %collective-permute-done.refs_2_, ...), custom_call_target="tpu_custom_call" | custom-call | flops 1150000000 | bytes 1024 | tf_op jit(solution)/shard_map/forward_0/pallas_call | solution.py:39
  23.9 2.2 %collective-permute-start.7 = (bf16[400,128]{1,0:T(8,128)(2,1)S(1)}, bf16[400,128]{1,0:T(8,128)(2,1)S(1)}, u32[]{:S(2)}, u32[]{:S(2)}) collective-permute-start(bf16[400,128]{1,0:T(8,128)(2,1)S(1)} %get-tuple-element.115), channel_id=1, source_target_pairs={{0,2},{1,3},{2,0},{3,1},{4,5},{5,4},{6,7},{7,6},{8,10},{9,11},{10,... | collective-permute-start | bytes 307208 | tf_op jit(solution)/shard_map/ppermute | solution.py:94
  26.1 1.6 %forward_2.1 = (f32[800,128]{1,0:T(8,128)S(1)}, bf16[800,128]{1,0:T(8,128)(2,1)S(1)}, f32[8,128]{1,0:T(8,128)S(1)}) custom-call(bf16[3,9,256,128]{3,2,1,0:T(8,128)(2,1)S(1)} %copy-done, bf16[400,256]{1,0:T(8,128)(2,1)S(1)} %get-tuple-element.97.refs_1_, bf16[400,256]{1,0:T(8,128)(2,1)S(1)} %collective-permute-done.refs_2_, ...), custom_call_target="tpu_custom_call" | custom-call | flops 1150000000 | bytes 1024 | tf_op jit(solution)/shard_map/forward_2/pallas_call | solution.py:39
  31.2 2.6 %collective-permute-done.6.refs_1_ = bf16[800,128]{1,0:T(8,128)(2,1)S(1)} collective-permute-done((bf16[800,128]{1,0:T(8,128)(2,1)S(1)}, bf16[800,128]{1,0:T(8,128)(2,1)S(1)}, u32[]{:S(2)}, u32[]{:S(2)}) %collective-permute-start.6) | collective-permute-done | bytes 204832 | tf_op jit(solution)/shard_map/ppermute | solution.py:94
  34.4 1.8 %collective-permute-start.12 = (bf16[400,128]{1,0:T(8,128)(2,1)S(1)}, bf16[400,128]{1,0:T(8,128)(2,1)S(1)}, u32[]{:S(2)}, u32[]{:S(2)}) collective-permute-start(bf16[400,128]{1,0:T(8,128)(2,1)S(1)} %get-tuple-element.130.refs_0_), channel_id=1, source_target_pairs={{0,2},{1,3},{2,0},{3,1},{4,5},{5,4},{6,7},{7,6},{8,10},{9,11},{10,... | collective-permute-start | bytes 307208 | tf_op jit(solution)/shard_map/ppermute | solution.py:94
  36.8 2.2 %collective-permute-done.8.refs_1_ = bf16[400,128]{1,0:T(8,128)(2,1)S(1)} collective-permute-done((bf16[400,128]{1,0:T(8,128)(2,1)S(1)}, bf16[400,128]{1,0:T(8,128)(2,1)S(1)}, u32[]{:S(2)}, u32[]{:S(2)}) %collective-permute-start.8) | collective-permute-done | bytes 102432 | tf_op jit(solution)/shard_map/ppermute | solution.py:94
  42.1 1.6 %weight_grad_1.1 = (f32[1168,128]{1,0:T(8,128)S(1)}, bf16[1168,128]{1,0:T(8,128)(2,1)S(1)}, bf16[1600,384]{1,0:T(8,128)(2,1)S(1)}, f32[8,128]{1,0:T(8,128)S(1)}) custom-call(bf16[800,128]{1,0:T(8,128)(2,1)S(1)} %get-tuple-element.128.refs_0_, bf16[800,128]{1,0:T(8,128)(2,1)S(1)} %collective-permute-done.11.refs_1_, ...), custom_call_target="tpu_custom_call" | custom-call | flops 1150000000 | bytes 1024 | tf_op jit(solution)/shard_map/weight_grad_1/pallas_call | solution.py:39
  45.4 1.7 %collective-permute-done.14.refs_1_ = bf16[800,128]{1,0:T(8,128)(2,1)S(1)} collective-permute-done((bf16[800,128]{1,0:T(8,128)(2,1)S(1)}, bf16[800,128]{1,0:T(8,128)(2,1)S(1)}, u32[]{:S(2)}, u32[]{:S(2)}) %collective-permute-start.14) | collective-permute-done | bytes 204832 | tf_op jit(solution)/shard_map/ppermute | solution.py:94
  47.0 1.9 %weight_grad_0.1 = (f32[1168,128]{1,0:T(8,128)S(1)}, bf16[1168,128]{1,0:T(8,128)(2,1)S(1)}, bf16[1600,384]{1,0:T(8,128)(2,1)S(1)}, f32[8,128]{1,0:T(8,128)S(1)}) custom-call(bf16[800,128]{1,0:T(8,128)(2,1)S(1)} %get-tuple-element.135.refs_0_, bf16[800,128]{1,0:T(8,128)(2,1)S(1)} %collective-permute-done.14.refs_1_, ...), custom_call_target="tpu_custom_call" | custom-call | flops 1150000000 | bytes 1024 | tf_op jit(solution)/shard_map/weight_grad_0/pallas_call | solution.py:39
  49.0 3.8 %collective-permute-start.19 = (bf16[1184,128]{1,0:T(8,128)(2,1)S(1)}, bf16[1184,128]{1,0:T(8,128)(2,1)S(1)}, u32[]{:S(2)}, u32[]{:S(2)}) collective-permute-start(bf16[1184,128]{1,0:T(8,128)(2,1)S(1)} %get-tuple-element.148), channel_id=1, source_target_pairs={{0,8},{4,12},{24,16},{28,20},{1,9},{5,13},{25,17},{29,21},{2,10},{... | collective-permute-start | bytes 909320 | tf_op jit(solution)/shard_map/ppermute | solution.py:568
  54.3 1.6 %collective-permute-start.21 = (bf16[1184,128]{1,0:T(8,128)(2,1)S(1)}, bf16[1184,128]{1,0:T(8,128)(2,1)S(1)}, u32[]{:S(2)}, u32[]{:S(2)}) collective-permute-start(bf16[1184,128]{1,0:T(8,128)(2,1)S(1)} %get-tuple-element.151), channel_id=1, source_target_pairs={{0,8},{4,12},{24,16},{28,20},{1,9},{5,13},{25,17},{29,21},{2,10},{... | collective-permute-start | bytes 909320 | tf_op jit(solution)/shard_map/ppermute | solution.py:568
  55.9 4.3 %collective-permute-done.19.refs_2_ = bf16[1184,128]{1,0:T(8,128)(2,1)S(1)} collective-permute-done((bf16[1184,128]{1,0:T(8,128)(2,1)S(1)}, bf16[1184,128]{1,0:T(8,128)(2,1)S(1)}, u32[]{:S(2)}, u32[]{:S(2)}) %collective-permute-start.19) | collective-permute-done | bytes 303136 | tf_op jit(solution)/shard_map/ppermute | solution.py:568
  61.1 7.4 %collective-permute-start.18 = (bf16[928,128]{1,0:T(8,128)(2,1)S(1)}, bf16[928,128]{1,0:T(8,128)(2,1)S(1)}, u32[]{:S(2)}, u32[]{:S(2)}) collective-permute-start(bf16[928,128]{1,0:T(8,128)(2,1)S(1)} %get-tuple-element.147), channel_id=1, source_target_pairs={{0,8},{4,12},{24,16},{28,20},{1,9},{5,13},{25,17},{29,21},{2,10},{... | collective-permute-start | bytes 712712 | tf_op jit(solution)/shard_map/ppermute | solution.py:568
  68.4 2.9 %input_grad.1 = (f32[1600,256]{1,0:T(8,128)S(1)}, f32[8,128]{1,0:T(8,128)S(1)}) custom-call(bf16[3,9,256,128]{3,2,1,0:T(8,128)(2,1)S(1)} %copy-done, bf16[1600,384]{1,0:T(8,128)(2,1)S(1)} %get-tuple-element.152.refs_1_, bf16[1600,384]{1,0:T(8,128)(2,1)S(1)} %get-tuple-element.153.refs_2_, bf16[1600,384]{1,0:T(8,128)(2,1)S(1)} %get-tuple-element.154.refs_3_, ...), custom_call_target="tpu_custom_call" | custom-call | flops 57500000 | bytes 1024 | tf_op jit(solution)/shard_map/input_grad/pallas_call | solution.py:39
  76.2 1.5 %collective-permute-start.26 = (bf16[400,256]{1,0:T(8,128)(2,1)S(1)}, bf16[400,256]{1,0:T(8,128)(2,1)S(1)}, u32[]{:S(2)}, u32[]{:S(2)}) collective-permute-start(bf16[400,256]{1,0:T(8,128)(2,1)S(1)} %get-tuple-element.171), channel_id=1, source_target_pairs={{0,2},{1,3},{2,0},{3,1},{4,6},{5,7},{6,4},{7,5},{8,10},{9,11},{10,... | collective-permute-start | bytes 614408 | tf_op jit(solution)/shard_map/ppermute | solution.py:435
  77.7 5.1 %collective-permute-done.23.refs_1_ = bf16[1184,128]{1,0:T(8,128)(2,1)S(1)} collective-permute-done((bf16[1184,128]{1,0:T(8,128)(2,1)S(1)}, bf16[1184,128]{1,0:T(8,128)(2,1)S(1)}, u32[]{:S(2)}, u32[]{:S(2)}) %collective-permute-start.23) | collective-permute-done | bytes 303136 | tf_op jit(solution)/shard_map/ppermute | solution.py:580
  87.2 2.3 %collective-permute-done.27.refs_3_ = bf16[400,256]{1,0:T(8,128)(2,1)S(1)} collective-permute-done((bf16[400,256]{1,0:T(8,128)(2,1)S(1)}, bf16[400,256]{1,0:T(8,128)(2,1)S(1)}, u32[]{:S(2)}, u32[]{:S(2)}) %collective-permute-start.27) | collective-permute-done | bytes 204832 | tf_op jit(solution)/shard_map/ppermute | solution.py:435
  91.6 2.2 %collective-permute-done.28.refs_1_ = bf16[928,128]{1,0:T(8,128)(2,1)S(1)} collective-permute-done((bf16[928,128]{1,0:T(8,128)(2,1)S(1)}, bf16[928,128]{1,0:T(8,128)(2,1)S(1)}, u32[]{:S(2)}, u32[]{:S(2)}) %collective-permute-start.28) | collective-permute-done | bytes 237600 | tf_op jit(solution)/shard_map/ppermute | solution.py:580
  95.1 1.5 %weight_out_b.1 = (f32[3,9,256,128]{3,2,1,0:T(8,128)}, f32[3,128]{1,0:T(4,128)}, f32[8,128]{1,0:T(8,128)S(1)}) custom-call(bf16[928,128]{1,0:T(8,128)(2,1)S(1)} %get-tuple-element.180.refs_0_.refs_3_, bf16[1184,128]{1,0:T(8,128)(2,1)S(1)} %get-tuple-element.181.refs_1_, ...), custom_call_target="tpu_custom_call", output_to_operand_aliasing={{0}: (4, {})} | custom-call | flops 57500000 | bytes 1024 | tf_op jit(solution)/shard_map/weight_out_b/pallas_call | solution.py:39
  (86 shorter events, 30.1 us)
Async XLA Ops:
  2.2 8.9 %collective-permute-start = (bf16[400,256]{1,0:T(8,128)(2,1)S(1)}, bf16[400,256]{1,0:T(8,128)(2,1)S(1)}, u32[]{:S(2)}, u32[]{:S(2)}) collective-permute-start(bf16[400,256]{1,0:T(8,128)(2,1)S(1)} %get-tuple-element.98), channel_id=1, source_target_pairs={{0,1},{1,0},{2,3},{3,2},{4,5},{5,4},{6,7},{7,6},{8,9},{9,8},{10,11... | collective-permute-start | bytes 614408 | tf_op jit(solution)/shard_map/ppermute | solution.py:435
  5.2 10.9 %collective-permute-start.1 = (bf16[400,256]{1,0:T(8,128)(2,1)S(1)}, bf16[400,256]{1,0:T(8,128)(2,1)S(1)}, u32[]{:S(2)}, u32[]{:S(2)}) collective-permute-start(bf16[400,256]{1,0:T(8,128)(2,1)S(1)} %get-tuple-element.99), channel_id=1, source_target_pairs={{0,2},{1,3},{2,0},{3,1},{4,6},{5,7},{6,4},{7,5},{8,10},{9,11},{10,... | collective-permute-start | bytes 614408 | tf_op jit(solution)/shard_map/ppermute | solution.py:435
  6.7 9.4 %collective-permute-start.2 = (bf16[400,256]{1,0:T(8,128)(2,1)S(1)}, bf16[400,256]{1,0:T(8,128)(2,1)S(1)}, u32[]{:S(2)}, u32[]{:S(2)}) collective-permute-start(bf16[400,256]{1,0:T(8,128)(2,1)S(1)} %get-tuple-element.100), channel_id=1, source_target_pairs={{0,3},{1,2},{2,1},{3,0},{4,7},{5,6},{6,5},{7,4},{8,11},{9,10},{10,... | collective-permute-start | bytes 614408 | tf_op jit(solution)/shard_map/ppermute | solution.py:435
  18.1 5.8 %collective-permute-start.4 = (bf16[800,128]{1,0:T(8,128)(2,1)S(1)}, bf16[800,128]{1,0:T(8,128)(2,1)S(1)}, u32[]{:S(2)}, u32[]{:S(2)}) collective-permute-start(bf16[800,128]{1,0:T(8,128)(2,1)S(1)} %get-tuple-element.106), channel_id=1, source_target_pairs={{0,1},{1,0},{2,3},{3,2},{4,6},{5,7},{6,4},{7,5},{8,9},{9,8},{10,11... | collective-permute-start | bytes 614408 | tf_op jit(solution)/shard_map/ppermute | solution.py:94
  21.8 6.0 %collective-permute-start.3 = (bf16[800,128]{1,0:T(8,128)(2,1)S(1)}, bf16[800,128]{1,0:T(8,128)(2,1)S(1)}, u32[]{:S(2)}, u32[]{:S(2)}) collective-permute-start(bf16[800,128]{1,0:T(8,128)(2,1)S(1)} %get-tuple-element.104), channel_id=1, source_target_pairs={{0,1},{1,0},{2,3},{3,2},{4,6},{5,7},{6,4},{7,5},{8,9},{9,8},{10,11... | collective-permute-start | bytes 614408 | tf_op jit(solution)/shard_map/ppermute | solution.py:94
  23.9 5.9 %collective-permute-start.7 = (bf16[400,128]{1,0:T(8,128)(2,1)S(1)}, bf16[400,128]{1,0:T(8,128)(2,1)S(1)}, u32[]{:S(2)}, u32[]{:S(2)}) collective-permute-start(bf16[400,128]{1,0:T(8,128)(2,1)S(1)} %get-tuple-element.115), channel_id=1, source_target_pairs={{0,2},{1,3},{2,0},{3,1},{4,5},{5,4},{6,7},{7,6},{8,10},{9,11},{10,... | collective-permute-start | bytes 307208 | tf_op jit(solution)/shard_map/ppermute | solution.py:94
  27.7 6.1 %collective-permute-start.6 = (bf16[800,128]{1,0:T(8,128)(2,1)S(1)}, bf16[800,128]{1,0:T(8,128)(2,1)S(1)}, u32[]{:S(2)}, u32[]{:S(2)}) collective-permute-start(bf16[800,128]{1,0:T(8,128)(2,1)S(1)} %get-tuple-element.113), channel_id=1, source_target_pairs={{0,1},{1,0},{2,3},{3,2},{4,6},{5,7},{6,4},{7,5},{8,9},{9,8},{10,11... | collective-permute-start | bytes 614408 | tf_op jit(solution)/shard_map/ppermute | solution.py:94
  27.9 6.4 %collective-permute-start.5 = (bf16[400,128]{1,0:T(8,128)(2,1)S(1)}, bf16[400,128]{1,0:T(8,128)(2,1)S(1)}, u32[]{:S(2)}, u32[]{:S(2)}) collective-permute-start(bf16[400,128]{1,0:T(8,128)(2,1)S(1)} %get-tuple-element.111), channel_id=1, source_target_pairs={{0,2},{1,3},{2,0},{3,1},{4,5},{5,4},{6,7},{7,6},{8,10},{9,11},{10,... | collective-permute-start | bytes 307208 | tf_op jit(solution)/shard_map/ppermute | solution.py:94
  30.0 6.2 %collective-permute-start.9 = (bf16[400,128]{1,0:T(8,128)(2,1)S(1)}, bf16[400,128]{1,0:T(8,128)(2,1)S(1)}, u32[]{:S(2)}, u32[]{:S(2)}) collective-permute-start(bf16[400,128]{1,0:T(8,128)(2,1)S(1)} %get-tuple-element.123.refs_0_), channel_id=1, source_target_pairs={{0,2},{1,3},{2,0},{3,1},{4,5},{5,4},{6,7},{7,6},{8,10},{9,11},{10,... | collective-permute-start | bytes 307208 | tf_op jit(solution)/shard_map/ppermute | solution.py:94
  34.4 6.8 %collective-permute-start.12 = (bf16[400,128]{1,0:T(8,128)(2,1)S(1)}, bf16[400,128]{1,0:T(8,128)(2,1)S(1)}, u32[]{:S(2)}, u32[]{:S(2)}) collective-permute-start(bf16[400,128]{1,0:T(8,128)(2,1)S(1)} %get-tuple-element.130.refs_0_), channel_id=1, source_target_pairs={{0,2},{1,3},{2,0},{3,1},{4,5},{5,4},{6,7},{7,6},{8,10},{9,11},{10,... | collective-permute-start | bytes 307208 | tf_op jit(solution)/shard_map/ppermute | solution.py:94
  36.2 5.8 %collective-permute-start.11 = (bf16[800,128]{1,0:T(8,128)(2,1)S(1)}, bf16[800,128]{1,0:T(8,128)(2,1)S(1)}, u32[]{:S(2)}, u32[]{:S(2)}) collective-permute-start(bf16[800,128]{1,0:T(8,128)(2,1)S(1)} %get-tuple-element.128.refs_0_), channel_id=1, source_target_pairs={{0,1},{1,0},{2,3},{3,2},{4,6},{5,7},{6,4},{7,5},{8,9},{9,8},{10,11... | collective-permute-start | bytes 614408 | tf_op jit(solution)/shard_map/ppermute | solution.py:94
  43.9 8.9 %collective-permute-start.13 = (bf16[800,128]{1,0:T(8,128)(2,1)S(1)}, bf16[800,128]{1,0:T(8,128)(2,1)S(1)}, u32[]{:S(2)}, u32[]{:S(2)}) collective-permute-start(bf16[800,128]{1,0:T(8,128)(2,1)S(1)} %get-tuple-element.134.refs_0_), channel_id=1, source_target_pairs={{0,1},{1,0},{2,3},{3,2},{4,6},{5,7},{6,4},{7,5},{8,9},{9,8},{10,11... | collective-permute-start | bytes 614408 | tf_op jit(solution)/shard_map/ppermute | solution.py:94
  49.0 11.2 %collective-permute-start.19 = (bf16[1184,128]{1,0:T(8,128)(2,1)S(1)}, bf16[1184,128]{1,0:T(8,128)(2,1)S(1)}, u32[]{:S(2)}, u32[]{:S(2)}) collective-permute-start(bf16[1184,128]{1,0:T(8,128)(2,1)S(1)} %get-tuple-element.148), channel_id=1, source_target_pairs={{0,8},{4,12},{24,16},{28,20},{1,9},{5,13},{25,17},{29,21},{2,10},{... | collective-permute-start | bytes 909320 | tf_op jit(solution)/shard_map/ppermute | solution.py:568
  54.3 17.2 %collective-permute-start.21 = (bf16[1184,128]{1,0:T(8,128)(2,1)S(1)}, bf16[1184,128]{1,0:T(8,128)(2,1)S(1)}, u32[]{:S(2)}, u32[]{:S(2)}) collective-permute-start(bf16[1184,128]{1,0:T(8,128)(2,1)S(1)} %get-tuple-element.151), channel_id=1, source_target_pairs={{0,8},{4,12},{24,16},{28,20},{1,9},{5,13},{25,17},{29,21},{2,10},{... | collective-permute-start | bytes 909320 | tf_op jit(solution)/shard_map/ppermute | solution.py:568
  60.4 11.9 %collective-permute-start.20 = (bf16[1184,128]{1,0:T(8,128)(2,1)S(1)}, bf16[1184,128]{1,0:T(8,128)(2,1)S(1)}, u32[]{:S(2)}, u32[]{:S(2)}) collective-permute-start(bf16[1184,128]{1,0:T(8,128)(2,1)S(1)} %get-tuple-element.150.refs_0_), channel_id=1, source_target_pairs={{8,16},{12,20},{16,8},{20,12},{9,17},{13,21},{17,9},{21,13},{10,18... | collective-permute-start | bytes 909320 | tf_op jit(solution)/shard_map/ppermute | solution.py:573
  61.1 12.6 %collective-permute-start.18 = (bf16[928,128]{1,0:T(8,128)(2,1)S(1)}, bf16[928,128]{1,0:T(8,128)(2,1)S(1)}, u32[]{:S(2)}, u32[]{:S(2)}) collective-permute-start(bf16[928,128]{1,0:T(8,128)(2,1)S(1)} %get-tuple-element.147), channel_id=1, source_target_pairs={{0,8},{4,12},{24,16},{28,20},{1,9},{5,13},{25,17},{29,21},{2,10},{... | collective-permute-start | bytes 712712 | tf_op jit(solution)/shard_map/ppermute | solution.py:568
  72.4 10.5 %collective-permute-start.23 = (bf16[1184,128]{1,0:T(8,128)(2,1)S(1)}, bf16[1184,128]{1,0:T(8,128)(2,1)S(1)}, u32[]{:S(2)}, u32[]{:S(2)}) collective-permute-start(bf16[1184,128]{1,0:T(8,128)(2,1)S(1)} %get-tuple-element.162.refs_0_), channel_id=1, source_target_pairs={{8,0},{12,4},{16,24},{20,28},{9,1},{13,5},{17,25},{21,29},{10,2},{... | collective-permute-start | bytes 909320 | tf_op jit(solution)/shard_map/ppermute | solution.py:580
  73.8 11.2 %collective-permute-start.22 = (bf16[928,128]{1,0:T(8,128)(2,1)S(1)}, bf16[928,128]{1,0:T(8,128)(2,1)S(1)}, u32[]{:S(2)}, u32[]{:S(2)}) collective-permute-start(bf16[928,128]{1,0:T(8,128)(2,1)S(1)} %get-tuple-element.161.refs_0_), channel_id=1, source_target_pairs={{8,16},{12,20},{16,8},{20,12},{9,17},{13,21},{17,9},{21,13},{10,18... | collective-permute-start | bytes 712712 | tf_op jit(solution)/shard_map/ppermute | solution.py:573
  74.5 16.1 %collective-permute-start.29 = (bf16[1184,128]{1,0:T(8,128)(2,1)S(1)}, bf16[1184,128]{1,0:T(8,128)(2,1)S(1)}, u32[]{:S(2)}, u32[]{:S(2)}) collective-permute-start(bf16[1184,128]{1,0:T(8,128)(2,1)S(1)} %get-tuple-element.176.refs_0_), channel_id=1, source_target_pairs={{8,0},{12,4},{16,24},{20,28},{9,1},{13,5},{17,25},{21,29},{10,2},{... | collective-permute-start | bytes 909320 | tf_op jit(solution)/shard_map/ppermute | solution.py:580
  75.8 11.3 %collective-permute-start.25 = (bf16[400,256]{1,0:T(8,128)(2,1)S(1)}, bf16[400,256]{1,0:T(8,128)(2,1)S(1)}, u32[]{:S(2)}, u32[]{:S(2)}) collective-permute-start(bf16[400,256]{1,0:T(8,128)(2,1)S(1)} %get-tuple-element.170), channel_id=1, source_target_pairs={{0,1},{1,0},{2,3},{3,2},{4,5},{5,4},{6,7},{7,6},{8,9},{9,8},{10,11... | collective-permute-start | bytes 614408 | tf_op jit(solution)/shard_map/ppermute | solution.py:435
  76.2 11.0 %collective-permute-start.26 = (bf16[400,256]{1,0:T(8,128)(2,1)S(1)}, bf16[400,256]{1,0:T(8,128)(2,1)S(1)}, u32[]{:S(2)}, u32[]{:S(2)}) collective-permute-start(bf16[400,256]{1,0:T(8,128)(2,1)S(1)} %get-tuple-element.171), channel_id=1, source_target_pairs={{0,2},{1,3},{2,0},{3,1},{4,6},{5,7},{6,4},{7,5},{8,10},{9,11},{10,... | collective-permute-start | bytes 614408 | tf_op jit(solution)/shard_map/ppermute | solution.py:435
  82.8 6.7 %collective-permute-start.27 = (bf16[400,256]{1,0:T(8,128)(2,1)S(1)}, bf16[400,256]{1,0:T(8,128)(2,1)S(1)}, u32[]{:S(2)}, u32[]{:S(2)}) collective-permute-start(bf16[400,256]{1,0:T(8,128)(2,1)S(1)} %get-tuple-element.172), channel_id=1, source_target_pairs={{0,3},{1,2},{2,1},{3,0},{4,7},{5,6},{6,5},{7,4},{8,11},{9,10},{10,... | collective-permute-start | bytes 614408 | tf_op jit(solution)/shard_map/ppermute | solution.py:435
  85.1 8.7 %collective-permute-start.28 = (bf16[928,128]{1,0:T(8,128)(2,1)S(1)}, bf16[928,128]{1,0:T(8,128)(2,1)S(1)}, u32[]{:S(2)}, u32[]{:S(2)}) collective-permute-start(bf16[928,128]{1,0:T(8,128)(2,1)S(1)} %get-tuple-element.175.refs_0_), channel_id=1, source_target_pairs={{8,0},{12,4},{16,24},{20,28},{9,1},{13,5},{17,25},{21,29},{10,2},{... | collective-permute-start | bytes 712712 | tf_op jit(solution)/shard_map/ppermute | solution.py:580
  87.2 6.8 %collective-permute-start.31 = (bf16[1184,128]{1,0:T(8,128)(2,1)S(1)}, bf16[1184,128]{1,0:T(8,128)(2,1)S(1)}, u32[]{:S(2)}, u32[]{:S(2)}) collective-permute-start(bf16[1184,128]{1,0:T(8,128)(2,1)S(1)} %get-tuple-element.182.refs_2_), channel_id=1, source_target_pairs={{0,4},{4,0},{8,12},{12,8},{16,20},{20,16},{24,28},{28,24},{1,5},{5... | collective-permute-start | bytes 909320 | tf_op jit(solution)/shard_map/ppermute | solution.py:609
  (13 other events, 47.5 us)

commit v5 on v4

--- a/solution.py
+++ b/solution.py
@@ -17,7 +17,7 @@
     return -(-columns // 8) * 8
 
 
-COSTS = {"input_grad": 0.05, "add_near_0": 0.05, "add_near_2": 0.05, "add_near_1": 0, "split_rows": 0.05, "add_far_0": 0.05, "add_far_2": 0.05, "add_far_1": 0.05, "merge_branches": 0.05, "join_channels": 0.05, "choose_0": 0.05, "choose_2": 0.05, "choose_1": 0.05, "weight_out_a": 0.05, "weight_out_b": 0.05, "add_cores_1": 1, "join_2": 3, "add_cores_0": 0, "add_cores_2": 0, "weight_grad_2": 0, "pass_on": 0.05, "weight_out_c": 0.05}
+COSTS = {"input_grad": 0.05, "add_near_0": 0.05, "add_near_2": 1, "add_near_1": 1, "split_rows": 0.05, "add_far_0": 0.05, "add_far_2": 0.05, "add_far_1": 0.05, "merge_branches": 0.05, "join_channels": 0.05, "choose_0": 0.05, "choose_2": 0.05, "choose_1": 0.05, "weight_out_a": 0.05, "weight_out_b": 0.05, "add_cores_1": 1, "join_2": 3, "add_cores_0": 0, "add_cores_2": 0, "weight_grad_2": 0, "pass_on": 0.05, "weight_out_c": 0.05}
 UNIT = 1_150_000_000
 
 
@@ -351,11 +351,14 @@
         copy.wait()
 
 
-def bias_kernel(scale, bodies, ins, out):
+def bias_kernel(scale, bodies, ins, out, buf, sem):
     for k, x in enumerate(ins):
         body = bodies[k]
         total = jnp.sum(x[body : body + EXTRA].astype(F32), axis=0, keepdims=True)
-        out[k : k + 1, :] = total * scale
+        buf[k : k + 1, :] = total * scale
+    copy = pltpu.make_async_copy(buf, out, sem)
+    copy.start()
+    return copy
 
 
 def touch_kernel(w_ref):
@@ -615,20 +618,28 @@
         extra = [state["own", k] for k in range(3)] if with_bias else []
         outs = [weight_shape] + ([shape((3, outputs), F32)] if with_bias else [])
 
+        scratch = [vm((n, 9, half, outputs), F32), pltpu.SemaphoreType.DMA((n, 7))]
+        if with_bias:
+            scratch += [vm((3, outputs), F32), pltpu.SemaphoreType.DMA]
+
         def kernel(*refs):
+            main = functools.partial(weight_out_kernel, 1.0 / dp, halves, *refs[:n])
             if with_bias:
-                bias_kernel(1.0 / dp, body, refs[n : n + 3], refs[-3])
-                refs = (*refs[: -3], *refs[-2:])
-            weight_out_kernel(1.0 / dp, halves, *refs[:n], refs[-3], *refs[-2:])
+                out, bias_out, bufs, sems, buf, sem = refs[-6:]
+                copy = bias_kernel(1.0 / dp, body, refs[n : n + 3], bias_out, buf, sem)
+                main(out, bufs, sems)
+                copy.wait()
+            else:
+                main(*refs[-3:])
 
         got = run(
             kernel,
             ins + extra + [state["weight_grad"]],
             outs,
-            [vm((n, 9, half, outputs), F32), pltpu.SemaphoreType.DMA((n, 7))],
+            scratch,
             name,
             in_specs=[whole] * (n + len(extra)) + [anywhere],
-            out_specs=[anywhere] + [whole] * (len(outs) - 1),
+            out_specs=[anywhere] * len(outs),
             aliases={n + len(extra): 0},
             last=last,
         )

time: 98.1 us -> 93.2 us (0.950)
  waiting for transfers between devices: 33.9 us -> 28 us
  starting transfers between devices: 38.7 us -> 40.2 us
    ppermute x3, waiting for transfers between devices: 4.31 us -> 1.14 us  [add_cores(): state['sum', k] = got + [lax.ppermute(near, 'dp', line([(0, 1), (3, 2)]))]]
    ppermute x12, waiting for transfers between devices: 10.4 us -> 8.76 us  [exchange(): return lax.ppermute(x, ('dp', 'space'), pairs)]
  transfers between devices with their start and end apart: 33 -> 33, of which waited for: 15 -> 14; matrix products, arithmetic and copies ran while one was open for 0% -> 0% of each run, Pallas kernels for 20% -> 20%
where the time goes in v5:
time: 93.2 us; the launch traced here: 92.7 us
  starting transfers between devices  40.2 us (43%)
  waiting for transfers between devices  28 us (30%)
  Pallas kernels  22.1 us (24%)
  local copies, waits for them, and re-layouts  1.28 us (1%)
  between operations  1.21 us (1%)
    pallas_call x36, Pallas kernels, call(): pl.pallas_call(body, grid=(1,), out_shape=(*outs, *([] if last else [shap...  22.1 us
    ppermute x3, starting transfers between devices, add_cores(): state['sum', k] = got + [lax.ppermute(near, 'dp', line([(0, 1), (3, 2)]))]  13 us
    ppermute x12, starting transfers between devices, exchange(): return lax.ppermute(x, ('dp', 'space'), pairs)  11.8 us
    ppermute x6, waiting for transfers between devices, swap(): return lax.ppermute(x, 'space', [(i, i ^ bit) for i in range(n)])  11.3 us
    ppermute x12, waiting for transfers between devices, exchange(): return lax.ppermute(x, ('dp', 'space'), pairs)  8.76 us
    ppermute x6, starting transfers between devices, swap(): return lax.ppermute(x, 'space', [(i, i ^ bit) for i in range(n)])  8.62 us
    ppermute x3, waiting for transfers between devices, add_far(): lax.ppermute(far_sum, 'dp', line([(1, 0), (2, 3)]))  6.6 us
    ppermute x3, starting transfers between devices, add_far(): lax.ppermute(far_sum, 'dp', line([(1, 0), (2, 3)]))  3.88 us
  transfers between devices with their start and end apart: 33, of which 14 were waited for; matrix products, arithmetic and copies ran while one was open for 0% of the time, Pallas kernels for 20%

profile of v5, /device:TPU:0, one launch (start us, length us, event | category | flops | bytes accessed | tf_op | source)
XLA Modules:
  0.0 92.7 jit_solution(8278796123922077032)
XLA Ops:
  2.2 3.0 %collective-permute-start = (bf16[400,256]{1,0:T(8,128)(2,1)S(1)}, bf16[400,256]{1,0:T(8,128)(2,1)S(1)}, u32[]{:S(2)}, u32[]{:S(2)}) collective-permute-start(bf16[400,256]{1,0:T(8,128)(2,1)S(1)} %get-tuple-element.98), channel_id=1, source_target_pairs={{0,1},{1,0},{2,3},{3,2},{4,5},{5,4},{6,7},{7,6},{8,9},{9,8},{10,11... | collective-permute-start | bytes 614408 | tf_op jit(solution)/shard_map/ppermute | solution.py:438
  5.2 1.5 %collective-permute-start.1 = (bf16[400,256]{1,0:T(8,128)(2,1)S(1)}, bf16[400,256]{1,0:T(8,128)(2,1)S(1)}, u32[]{:S(2)}, u32[]{:S(2)}) collective-permute-start(bf16[400,256]{1,0:T(8,128)(2,1)S(1)} %get-tuple-element.99), channel_id=1, source_target_pairs={{0,2},{1,3},{2,0},{3,1},{4,6},{5,7},{6,4},{7,5},{8,10},{9,11},{10,... | collective-permute-start | bytes 614408 | tf_op jit(solution)/shard_map/ppermute | solution.py:438
  6.7 4.4 %collective-permute-done.refs_2_ = bf16[400,256]{1,0:T(8,128)(2,1)S(1)} collective-permute-done((bf16[400,256]{1,0:T(8,128)(2,1)S(1)}, bf16[400,256]{1,0:T(8,128)(2,1)S(1)}, u32[]{:S(2)}, u32[]{:S(2)}) %collective-permute-start) | collective-permute-done | bytes 204832 | tf_op jit(solution)/shard_map/ppermute | solution.py:438
  11.1 5.0 %collective-permute-done.1.refs_3_ = bf16[400,256]{1,0:T(8,128)(2,1)S(1)} collective-permute-done((bf16[400,256]{1,0:T(8,128)(2,1)S(1)}, bf16[400,256]{1,0:T(8,128)(2,1)S(1)}, u32[]{:S(2)}, u32[]{:S(2)}) %collective-permute-start.1) | collective-permute-done | bytes 204832 | tf_op jit(solution)/shard_map/ppermute | solution.py:438
  16.1 2.0 %forward_1.1 = (f32[800,128]{1,0:T(8,128)S(1)}, bf16[800,128]{1,0:T(8,128)(2,1)S(1)}, bf16[1600,256]{1,0:T(8,128)(2,1)S(1)}, f32[8,128]{1,0:T(8,128)S(1)}) custom-call(bf16[3,9,256,128]{3,2,1,0:T(8,128)(2,1)S(1)} %copy-done, bf16[400,256]{1,0:T(8,128)(2,1)S(1)} %get-tuple-element.97.refs_1_, bf16[400,256]{1,0:T(8,128)(2,1)S(1)} %collective-permute-done.refs_2_, ...), custom_call_target="tpu_custom_call" | custom-call | flops 1150000000 | bytes 1024 | tf_op jit(solution)/shard_map/forward_1/pallas_call | solution.py:39
  18.1 1.3 %collective-permute-start.4 = (bf16[800,128]{1,0:T(8,128)(2,1)S(1)}, bf16[800,128]{1,0:T(8,128)(2,1)S(1)}, u32[]{:S(2)}, u32[]{:S(2)}) collective-permute-start(bf16[800,128]{1,0:T(8,128)(2,1)S(1)} %get-tuple-element.106), channel_id=1, source_target_pairs={{0,1},{1,0},{2,3},{3,2},{4,6},{5,7},{6,4},{7,5},{8,9},{9,8},{10,11... | collective-permute-start | bytes 614408 | tf_op jit(solution)/shard_map/ppermute | solution.py:94
  19.4 2.5 %forward_0.1 = (f32[800,128]{1,0:T(8,128)S(1)}, bf16[800,128]{1,0:T(8,128)(2,1)S(1)}, f32[8,128]{1,0:T(8,128)S(1)}) custom-call(bf16[3,9,256,128]{3,2,1,0:T(8,128)(2,1)S(1)} %copy-done, bf16[400,256]{1,0:T(8,128)(2,1)S(1)} %get-tuple-element.97.refs_1_, bf16[400,256]{1,0:T(8,128)(2,1)S(1)} %collective-permute-done.refs_2_, ...), custom_call_target="tpu_custom_call" | custom-call | flops 1150000000 | bytes 1024 | tf_op jit(solution)/shard_map/forward_0/pallas_call | solution.py:39
  23.9 2.2 %collective-permute-start.7 = (bf16[400,128]{1,0:T(8,128)(2,1)S(1)}, bf16[400,128]{1,0:T(8,128)(2,1)S(1)}, u32[]{:S(2)}, u32[]{:S(2)}) collective-permute-start(bf16[400,128]{1,0:T(8,128)(2,1)S(1)} %get-tuple-element.115), channel_id=1, source_target_pairs={{0,2},{1,3},{2,0},{3,1},{4,5},{5,4},{6,7},{7,6},{8,10},{9,11},{10,... | collective-permute-start | bytes 307208 | tf_op jit(solution)/shard_map/ppermute | solution.py:94
  26.1 1.6 %forward_2.1 = (f32[800,128]{1,0:T(8,128)S(1)}, bf16[800,128]{1,0:T(8,128)(2,1)S(1)}, f32[8,128]{1,0:T(8,128)S(1)}) custom-call(bf16[3,9,256,128]{3,2,1,0:T(8,128)(2,1)S(1)} %copy-done, bf16[400,256]{1,0:T(8,128)(2,1)S(1)} %get-tuple-element.97.refs_1_, bf16[400,256]{1,0:T(8,128)(2,1)S(1)} %collective-permute-done.refs_2_, ...), custom_call_target="tpu_custom_call" | custom-call | flops 1150000000 | bytes 1024 | tf_op jit(solution)/shard_map/forward_2/pallas_call | solution.py:39
  31.2 2.7 %collective-permute-done.6.refs_1_ = bf16[800,128]{1,0:T(8,128)(2,1)S(1)} collective-permute-done((bf16[800,128]{1,0:T(8,128)(2,1)S(1)}, bf16[800,128]{1,0:T(8,128)(2,1)S(1)}, u32[]{:S(2)}, u32[]{:S(2)}) %collective-permute-start.6) | collective-permute-done | bytes 204832 | tf_op jit(solution)/shard_map/ppermute | solution.py:94
  34.4 1.8 %collective-permute-start.12 = (bf16[400,128]{1,0:T(8,128)(2,1)S(1)}, bf16[400,128]{1,0:T(8,128)(2,1)S(1)}, u32[]{:S(2)}, u32[]{:S(2)}) collective-permute-start(bf16[400,128]{1,0:T(8,128)(2,1)S(1)} %get-tuple-element.130.refs_0_), channel_id=1, source_target_pairs={{0,2},{1,3},{2,0},{3,1},{4,5},{5,4},{6,7},{7,6},{8,10},{9,11},{10,... | collective-permute-start | bytes 307208 | tf_op jit(solution)/shard_map/ppermute | solution.py:94
  36.8 2.2 %collective-permute-done.8.refs_1_ = bf16[400,128]{1,0:T(8,128)(2,1)S(1)} collective-permute-done((bf16[400,128]{1,0:T(8,128)(2,1)S(1)}, bf16[400,128]{1,0:T(8,128)(2,1)S(1)}, u32[]{:S(2)}, u32[]{:S(2)}) %collective-permute-start.8) | collective-permute-done | bytes 102432 | tf_op jit(solution)/shard_map/ppermute | solution.py:94
  39.9 1.3 %collective-permute-done.12.refs_1_ = bf16[400,128]{1,0:T(8,128)(2,1)S(1)} collective-permute-done((bf16[400,128]{1,0:T(8,128)(2,1)S(1)}, bf16[400,128]{1,0:T(8,128)(2,1)S(1)}, u32[]{:S(2)}, u32[]{:S(2)}) %collective-permute-start.12) | collective-permute-done | bytes 102432 | tf_op jit(solution)/shard_map/ppermute | solution.py:94
  42.1 1.6 %weight_grad_1.1 = (f32[1168,128]{1,0:T(8,128)S(1)}, bf16[1168,128]{1,0:T(8,128)(2,1)S(1)}, bf16[1600,384]{1,0:T(8,128)(2,1)S(1)}, f32[8,128]{1,0:T(8,128)S(1)}) custom-call(bf16[800,128]{1,0:T(8,128)(2,1)S(1)} %get-tuple-element.128.refs_0_, bf16[800,128]{1,0:T(8,128)(2,1)S(1)} %collective-permute-done.11.refs_1_, ...), custom_call_target="tpu_custom_call" | custom-call | flops 1150000000 | bytes 1024 | tf_op jit(solution)/shard_map/weight_grad_1/pallas_call | solution.py:39
  45.4 3.7 %collective-permute-start.19 = (bf16[1184,128]{1,0:T(8,128)(2,1)S(1)}, bf16[1184,128]{1,0:T(8,128)(2,1)S(1)}, u32[]{:S(2)}, u32[]{:S(2)}) collective-permute-start(bf16[1184,128]{1,0:T(8,128)(2,1)S(1)} %get-tuple-element.148), channel_id=1, source_target_pairs={{0,8},{4,12},{24,16},{28,20},{1,9},{5,13},{25,17},{29,21},{2,10},{... | collective-permute-start | bytes 909320 | tf_op jit(solution)/shard_map/ppermute | solution.py:571
  49.0 1.9 %weight_grad_0.1 = (f32[1168,128]{1,0:T(8,128)S(1)}, bf16[1168,128]{1,0:T(8,128)(2,1)S(1)}, bf16[1600,384]{1,0:T(8,128)(2,1)S(1)}, f32[8,128]{1,0:T(8,128)S(1)}) custom-call(bf16[800,128]{1,0:T(8,128)(2,1)S(1)} %get-tuple-element.135.refs_0_, bf16[800,128]{1,0:T(8,128)(2,1)S(1)} %collective-permute-done.14.refs_1_, ...), custom_call_target="tpu_custom_call" | custom-call | flops 1150000000 | bytes 1024 | tf_op jit(solution)/shard_map/weight_grad_0/pallas_call | solution.py:39
  52.8 2.0 %collective-permute-start.21 = (bf16[1184,128]{1,0:T(8,128)(2,1)S(1)}, bf16[1184,128]{1,0:T(8,128)(2,1)S(1)}, u32[]{:S(2)}, u32[]{:S(2)}) collective-permute-start(bf16[1184,128]{1,0:T(8,128)(2,1)S(1)} %get-tuple-element.151), channel_id=1, source_target_pairs={{0,8},{4,12},{24,16},{28,20},{1,9},{5,13},{25,17},{29,21},{2,10},{... | collective-permute-start | bytes 909320 | tf_op jit(solution)/shard_map/ppermute | solution.py:571
  56.8 7.4 %collective-permute-start.18 = (bf16[928,128]{1,0:T(8,128)(2,1)S(1)}, bf16[928,128]{1,0:T(8,128)(2,1)S(1)}, u32[]{:S(2)}, u32[]{:S(2)}) collective-permute-start(bf16[928,128]{1,0:T(8,128)(2,1)S(1)} %get-tuple-element.147), channel_id=1, source_target_pairs={{0,8},{4,12},{24,16},{28,20},{1,9},{5,13},{25,17},{29,21},{2,10},{... | collective-permute-start | bytes 712712 | tf_op jit(solution)/shard_map/ppermute | solution.py:571
  64.2 2.9 %input_grad.1 = (f32[1600,256]{1,0:T(8,128)S(1)}, f32[8,128]{1,0:T(8,128)S(1)}) custom-call(bf16[3,9,256,128]{3,2,1,0:T(8,128)(2,1)S(1)} %copy-done, bf16[1600,384]{1,0:T(8,128)(2,1)S(1)} %get-tuple-element.152.refs_1_, bf16[1600,384]{1,0:T(8,128)(2,1)S(1)} %get-tuple-element.153.refs_2_, bf16[1600,384]{1,0:T(8,128)(2,1)S(1)} %get-tuple-element.154.refs_3_, ...), custom_call_target="tpu_custom_call" | custom-call | flops 57500000 | bytes 1024 | tf_op jit(solution)/shard_map/input_grad/pallas_call | solution.py:39
  71.6 1.6 %collective-permute-start.25 = (bf16[400,256]{1,0:T(8,128)(2,1)S(1)}, bf16[400,256]{1,0:T(8,128)(2,1)S(1)}, u32[]{:S(2)}, u32[]{:S(2)}) collective-permute-start(bf16[400,256]{1,0:T(8,128)(2,1)S(1)} %get-tuple-element.170), channel_id=1, source_target_pairs={{0,1},{1,0},{2,3},{3,2},{4,5},{5,4},{6,7},{7,6},{8,9},{9,8},{10,11... | collective-permute-start | bytes 614408 | tf_op jit(solution)/shard_map/ppermute | solution.py:438
  73.9 4.6 %collective-permute-done.23.refs_1_ = bf16[1184,128]{1,0:T(8,128)(2,1)S(1)} collective-permute-done((bf16[1184,128]{1,0:T(8,128)(2,1)S(1)}, bf16[1184,128]{1,0:T(8,128)(2,1)S(1)}, u32[]{:S(2)}, u32[]{:S(2)}) %collective-permute-start.23) | collective-permute-done | bytes 303136 | tf_op jit(solution)/shard_map/ppermute | solution.py:583
  78.6 1.7 %collective-permute-start.27 = (bf16[400,256]{1,0:T(8,128)(2,1)S(1)}, bf16[400,256]{1,0:T(8,128)(2,1)S(1)}, u32[]{:S(2)}, u32[]{:S(2)}) collective-permute-start(bf16[400,256]{1,0:T(8,128)(2,1)S(1)} %get-tuple-element.172), channel_id=1, source_target_pairs={{0,3},{1,2},{2,1},{3,0},{4,7},{5,6},{6,5},{7,4},{8,11},{9,10},{10,... | collective-permute-start | bytes 614408 | tf_op jit(solution)/shard_map/ppermute | solution.py:438
  83.4 1.9 %collective-permute-done.27.refs_3_ = bf16[400,256]{1,0:T(8,128)(2,1)S(1)} collective-permute-done((bf16[400,256]{1,0:T(8,128)(2,1)S(1)}, bf16[400,256]{1,0:T(8,128)(2,1)S(1)}, u32[]{:S(2)}, u32[]{:S(2)}) %collective-permute-start.27) | collective-permute-done | bytes 204832 | tf_op jit(solution)/shard_map/ppermute | solution.py:438
  87.3 2.0 %collective-permute-done.28.refs_1_ = bf16[928,128]{1,0:T(8,128)(2,1)S(1)} collective-permute-done((bf16[928,128]{1,0:T(8,128)(2,1)S(1)}, bf16[928,128]{1,0:T(8,128)(2,1)S(1)}, u32[]{:S(2)}, u32[]{:S(2)}) %collective-permute-start.28) | collective-permute-done | bytes 237600 | tf_op jit(solution)/shard_map/ppermute | solution.py:583
  (86 shorter events, 28.9 us)
Async XLA Ops:
  2.2 8.9 %collective-permute-start = (bf16[400,256]{1,0:T(8,128)(2,1)S(1)}, bf16[400,256]{1,0:T(8,128)(2,1)S(1)}, u32[]{:S(2)}, u32[]{:S(2)}) collective-permute-start(bf16[400,256]{1,0:T(8,128)(2,1)S(1)} %get-tuple-element.98), channel_id=1, source_target_pairs={{0,1},{1,0},{2,3},{3,2},{4,5},{5,4},{6,7},{7,6},{8,9},{9,8},{10,11... | collective-permute-start | bytes 614408 | tf_op jit(solution)/shard_map/ppermute | solution.py:438
  5.2 10.9 %collective-permute-start.1 = (bf16[400,256]{1,0:T(8,128)(2,1)S(1)}, bf16[400,256]{1,0:T(8,128)(2,1)S(1)}, u32[]{:S(2)}, u32[]{:S(2)}) collective-permute-start(bf16[400,256]{1,0:T(8,128)(2,1)S(1)} %get-tuple-element.99), channel_id=1, source_target_pairs={{0,2},{1,3},{2,0},{3,1},{4,6},{5,7},{6,4},{7,5},{8,10},{9,11},{10,... | collective-permute-start | bytes 614408 | tf_op jit(solution)/shard_map/ppermute | solution.py:438
  6.7 9.4 %collective-permute-start.2 = (bf16[400,256]{1,0:T(8,128)(2,1)S(1)}, bf16[400,256]{1,0:T(8,128)(2,1)S(1)}, u32[]{:S(2)}, u32[]{:S(2)}) collective-permute-start(bf16[400,256]{1,0:T(8,128)(2,1)S(1)} %get-tuple-element.100), channel_id=1, source_target_pairs={{0,3},{1,2},{2,1},{3,0},{4,7},{5,6},{6,5},{7,4},{8,11},{9,10},{10,... | collective-permute-start | bytes 614408 | tf_op jit(solution)/shard_map/ppermute | solution.py:438
  18.1 5.8 %collective-permute-start.4 = (bf16[800,128]{1,0:T(8,128)(2,1)S(1)}, bf16[800,128]{1,0:T(8,128)(2,1)S(1)}, u32[]{:S(2)}, u32[]{:S(2)}) collective-permute-start(bf16[800,128]{1,0:T(8,128)(2,1)S(1)} %get-tuple-element.106), channel_id=1, source_target_pairs={{0,1},{1,0},{2,3},{3,2},{4,6},{5,7},{6,4},{7,5},{8,9},{9,8},{10,11... | collective-permute-start | bytes 614408 | tf_op jit(solution)/shard_map/ppermute | solution.py:94
  21.8 6.0 %collective-permute-start.3 = (bf16[800,128]{1,0:T(8,128)(2,1)S(1)}, bf16[800,128]{1,0:T(8,128)(2,1)S(1)}, u32[]{:S(2)}, u32[]{:S(2)}) collective-permute-start(bf16[800,128]{1,0:T(8,128)(2,1)S(1)} %get-tuple-element.104), channel_id=1, source_target_pairs={{0,1},{1,0},{2,3},{3,2},{4,6},{5,7},{6,4},{7,5},{8,9},{9,8},{10,11... | collective-permute-start | bytes 614408 | tf_op jit(solution)/shard_map/ppermute | solution.py:94
  23.9 5.9 %collective-permute-start.7 = (bf16[400,128]{1,0:T(8,128)(2,1)S(1)}, bf16[400,128]{1,0:T(8,128)(2,1)S(1)}, u32[]{:S(2)}, u32[]{:S(2)}) collective-permute-start(bf16[400,128]{1,0:T(8,128)(2,1)S(1)} %get-tuple-element.115), channel_id=1, source_target_pairs={{0,2},{1,3},{2,0},{3,1},{4,5},{5,4},{6,7},{7,6},{8,10},{9,11},{10,... | collective-permute-start | bytes 307208 | tf_op jit(solution)/shard_map/ppermute | solution.py:94
  27.7 6.1 %collective-permute-start.6 = (bf16[800,128]{1,0:T(8,128)(2,1)S(1)}, bf16[800,128]{1,0:T(8,128)(2,1)S(1)}, u32[]{:S(2)}, u32[]{:S(2)}) collective-permute-start(bf16[800,128]{1,0:T(8,128)(2,1)S(1)} %get-tuple-element.113), channel_id=1, source_target_pairs={{0,1},{1,0},{2,3},{3,2},{4,6},{5,7},{6,4},{7,5},{8,9},{9,8},{10,11... | collective-permute-start | bytes 614408 | tf_op jit(solution)/shard_map/ppermute | solution.py:94
  27.9 6.4 %collective-permute-start.5 = (bf16[400,128]{1,0:T(8,128)(2,1)S(1)}, bf16[400,128]{1,0:T(8,128)(2,1)S(1)}, u32[]{:S(2)}, u32[]{:S(2)}) collective-permute-start(bf16[400,128]{1,0:T(8,128)(2,1)S(1)} %get-tuple-element.111), channel_id=1, source_target_pairs={{0,2},{1,3},{2,0},{3,1},{4,5},{5,4},{6,7},{7,6},{8,10},{9,11},{10,... | collective-permute-start | bytes 307208 | tf_op jit(solution)/shard_map/ppermute | solution.py:94
  30.0 6.2 %collective-permute-start.9 = (bf16[400,128]{1,0:T(8,128)(2,1)S(1)}, bf16[400,128]{1,0:T(8,128)(2,1)S(1)}, u32[]{:S(2)}, u32[]{:S(2)}) collective-permute-start(bf16[400,128]{1,0:T(8,128)(2,1)S(1)} %get-tuple-element.123.refs_0_), channel_id=1, source_target_pairs={{0,2},{1,3},{2,0},{3,1},{4,5},{5,4},{6,7},{7,6},{8,10},{9,11},{10,... | collective-permute-start | bytes 307208 | tf_op jit(solution)/shard_map/ppermute | solution.py:94
  34.4 6.8 %collective-permute-start.12 = (bf16[400,128]{1,0:T(8,128)(2,1)S(1)}, bf16[400,128]{1,0:T(8,128)(2,1)S(1)}, u32[]{:S(2)}, u32[]{:S(2)}) collective-permute-start(bf16[400,128]{1,0:T(8,128)(2,1)S(1)} %get-tuple-element.130.refs_0_), channel_id=1, source_target_pairs={{0,2},{1,3},{2,0},{3,1},{4,5},{5,4},{6,7},{7,6},{8,10},{9,11},{10,... | collective-permute-start | bytes 307208 | tf_op jit(solution)/shard_map/ppermute | solution.py:94
  41.2 7.8 %collective-permute-start.14 = (bf16[800,128]{1,0:T(8,128)(2,1)S(1)}, bf16[800,128]{1,0:T(8,128)(2,1)S(1)}, u32[]{:S(2)}, u32[]{:S(2)}) collective-permute-start(bf16[800,128]{1,0:T(8,128)(2,1)S(1)} %get-tuple-element.135.refs_0_), channel_id=1, source_target_pairs={{0,1},{1,0},{2,3},{3,2},{4,6},{5,7},{6,4},{7,5},{8,9},{9,8},{10,11... | collective-permute-start | bytes 614408 | tf_op jit(solution)/shard_map/ppermute | solution.py:94
  43.9 7.1 %collective-permute-start.13 = (bf16[800,128]{1,0:T(8,128)(2,1)S(1)}, bf16[800,128]{1,0:T(8,128)(2,1)S(1)}, u32[]{:S(2)}, u32[]{:S(2)}) collective-permute-start(bf16[800,128]{1,0:T(8,128)(2,1)S(1)} %get-tuple-element.134.refs_0_), channel_id=1, source_target_pairs={{0,1},{1,0},{2,3},{3,2},{4,6},{5,7},{6,4},{7,5},{8,9},{9,8},{10,11... | collective-permute-start | bytes 614408 | tf_op jit(solution)/shard_map/ppermute | solution.py:94
  45.4 10.7 %collective-permute-start.19 = (bf16[1184,128]{1,0:T(8,128)(2,1)S(1)}, bf16[1184,128]{1,0:T(8,128)(2,1)S(1)}, u32[]{:S(2)}, u32[]{:S(2)}) collective-permute-start(bf16[1184,128]{1,0:T(8,128)(2,1)S(1)} %get-tuple-element.148), channel_id=1, source_target_pairs={{0,8},{4,12},{24,16},{28,20},{1,9},{5,13},{25,17},{29,21},{2,10},{... | collective-permute-start | bytes 909320 | tf_op jit(solution)/shard_map/ppermute | solution.py:571
  52.8 14.4 %collective-permute-start.21 = (bf16[1184,128]{1,0:T(8,128)(2,1)S(1)}, bf16[1184,128]{1,0:T(8,128)(2,1)S(1)}, u32[]{:S(2)}, u32[]{:S(2)}) collective-permute-start(bf16[1184,128]{1,0:T(8,128)(2,1)S(1)} %get-tuple-element.151), channel_id=1, source_target_pairs={{0,8},{4,12},{24,16},{28,20},{1,9},{5,13},{25,17},{29,21},{2,10},{... | collective-permute-start | bytes 909320 | tf_op jit(solution)/shard_map/ppermute | solution.py:571
  56.1 11.9 %collective-permute-start.20 = (bf16[1184,128]{1,0:T(8,128)(2,1)S(1)}, bf16[1184,128]{1,0:T(8,128)(2,1)S(1)}, u32[]{:S(2)}, u32[]{:S(2)}) collective-permute-start(bf16[1184,128]{1,0:T(8,128)(2,1)S(1)} %get-tuple-element.150.refs_0_), channel_id=1, source_target_pairs={{8,16},{12,20},{16,8},{20,12},{9,17},{13,21},{17,9},{21,13},{10,18... | collective-permute-start | bytes 909320 | tf_op jit(solution)/shard_map/ppermute | solution.py:576
  56.8 12.6 %collective-permute-start.18 = (bf16[928,128]{1,0:T(8,128)(2,1)S(1)}, bf16[928,128]{1,0:T(8,128)(2,1)S(1)}, u32[]{:S(2)}, u32[]{:S(2)}) collective-permute-start(bf16[928,128]{1,0:T(8,128)(2,1)S(1)} %get-tuple-element.147), channel_id=1, source_target_pairs={{0,8},{4,12},{24,16},{28,20},{1,9},{5,13},{25,17},{29,21},{2,10},{... | collective-permute-start | bytes 712712 | tf_op jit(solution)/shard_map/ppermute | solution.py:571
  68.1 10.5 %collective-permute-start.23 = (bf16[1184,128]{1,0:T(8,128)(2,1)S(1)}, bf16[1184,128]{1,0:T(8,128)(2,1)S(1)}, u32[]{:S(2)}, u32[]{:S(2)}) collective-permute-start(bf16[1184,128]{1,0:T(8,128)(2,1)S(1)} %get-tuple-element.162.refs_0_), channel_id=1, source_target_pairs={{8,0},{12,4},{16,24},{20,28},{9,1},{13,5},{17,25},{21,29},{10,2},{... | collective-permute-start | bytes 909320 | tf_op jit(solution)/shard_map/ppermute | solution.py:583
  69.5 11.7 %collective-permute-start.22 = (bf16[928,128]{1,0:T(8,128)(2,1)S(1)}, bf16[928,128]{1,0:T(8,128)(2,1)S(1)}, u32[]{:S(2)}, u32[]{:S(2)}) collective-permute-start(bf16[928,128]{1,0:T(8,128)(2,1)S(1)} %get-tuple-element.161.refs_0_), channel_id=1, source_target_pairs={{8,16},{12,20},{16,8},{20,12},{9,17},{13,21},{17,9},{21,13},{10,18... | collective-permute-start | bytes 712712 | tf_op jit(solution)/shard_map/ppermute | solution.py:576
  70.3 16.1 %collective-permute-start.29 = (bf16[1184,128]{1,0:T(8,128)(2,1)S(1)}, bf16[1184,128]{1,0:T(8,128)(2,1)S(1)}, u32[]{:S(2)}, u32[]{:S(2)}) collective-permute-start(bf16[1184,128]{1,0:T(8,128)(2,1)S(1)} %get-tuple-element.176.refs_0_), channel_id=1, source_target_pairs={{8,0},{12,4},{16,24},{20,28},{9,1},{13,5},{17,25},{21,29},{10,2},{... | collective-permute-start | bytes 909320 | tf_op jit(solution)/shard_map/ppermute | solution.py:583
  71.6 11.8 %collective-permute-start.25 = (bf16[400,256]{1,0:T(8,128)(2,1)S(1)}, bf16[400,256]{1,0:T(8,128)(2,1)S(1)}, u32[]{:S(2)}, u32[]{:S(2)}) collective-permute-start(bf16[400,256]{1,0:T(8,128)(2,1)S(1)} %get-tuple-element.170), channel_id=1, source_target_pairs={{0,1},{1,0},{2,3},{3,2},{4,5},{5,4},{6,7},{7,6},{8,9},{9,8},{10,11... | collective-permute-start | bytes 614408 | tf_op jit(solution)/shard_map/ppermute | solution.py:438
  73.2 10.1 %collective-permute-start.26 = (bf16[400,256]{1,0:T(8,128)(2,1)S(1)}, bf16[400,256]{1,0:T(8,128)(2,1)S(1)}, u32[]{:S(2)}, u32[]{:S(2)}) collective-permute-start(bf16[400,256]{1,0:T(8,128)(2,1)S(1)} %get-tuple-element.171), channel_id=1, source_target_pairs={{0,2},{1,3},{2,0},{3,1},{4,6},{5,7},{6,4},{7,5},{8,10},{9,11},{10,... | collective-permute-start | bytes 614408 | tf_op jit(solution)/shard_map/ppermute | solution.py:438
  78.6 6.7 %collective-permute-start.27 = (bf16[400,256]{1,0:T(8,128)(2,1)S(1)}, bf16[400,256]{1,0:T(8,128)(2,1)S(1)}, u32[]{:S(2)}, u32[]{:S(2)}) collective-permute-start(bf16[400,256]{1,0:T(8,128)(2,1)S(1)} %get-tuple-element.172), channel_id=1, source_target_pairs={{0,3},{1,2},{2,1},{3,0},{4,7},{5,6},{6,5},{7,4},{8,11},{9,10},{10,... | collective-permute-start | bytes 614408 | tf_op jit(solution)/shard_map/ppermute | solution.py:438
  81.3 8.0 %collective-permute-start.28 = (bf16[928,128]{1,0:T(8,128)(2,1)S(1)}, bf16[928,128]{1,0:T(8,128)(2,1)S(1)}, u32[]{:S(2)}, u32[]{:S(2)}) collective-permute-start(bf16[928,128]{1,0:T(8,128)(2,1)S(1)} %get-tuple-element.175.refs_0_), channel_id=1, source_target_pairs={{8,0},{12,4},{16,24},{20,28},{9,1},{13,5},{17,25},{21,29},{10,2},{... | collective-permute-start | bytes 712712 | tf_op jit(solution)/shard_map/ppermute | solution.py:583
  83.4 6.1 %collective-permute-start.31 = (bf16[1184,128]{1,0:T(8,128)(2,1)S(1)}, bf16[1184,128]{1,0:T(8,128)(2,1)S(1)}, u32[]{:S(2)}, u32[]{:S(2)}) collective-permute-start(bf16[1184,128]{1,0:T(8,128)(2,1)S(1)} %get-tuple-element.182.refs_2_), channel_id=1, source_target_pairs={{0,4},{4,0},{8,12},{12,8},{16,20},{20,16},{24,28},{28,24},{1,5},{5... | collective-permute-start | bytes 909320 | tf_op jit(solution)/shard_map/ppermute | solution.py:612
  (13 other events, 43.9 us)

commit v6 on v5

--- a/solution.py
+++ b/solution.py
@@ -467,7 +467,7 @@
             kept_rows.append(9 * half + EXTRA)
 
     def packed(k):
-        return [shape((kept_rows[k] + 16, outputs), BF)]
+        return [shape((kept_rows[k] + (0 if near[k] else 16), outputs), BF)]
 
     chain = []
     run = functools.partial(call, chain)

time: 93.2 us -> 93.2 us (level)
  no operation moved by 1% of the time
where the time goes in v6:
time: 93.2 us; the launch traced here: 92.7 us
  starting transfers between devices  40.2 us (43%)
  waiting for transfers between devices  27.9 us (30%)
  Pallas kernels  22.1 us (24%)
  local copies, waits for them, and re-layouts  1.28 us (1%)
  between operations  1.21 us (1%)
    pallas_call x36, Pallas kernels, call(): pl.pallas_call(body, grid=(1,), out_shape=(*outs, *([] if last else [shap...  22.1 us
    ppermute x3, starting transfers between devices, add_cores(): state['sum', k] = got + [lax.ppermute(near, 'dp', line([(0, 1), (3, 2)]))]  13 us
    ppermute x12, starting transfers between devices, exchange(): return lax.ppermute(x, ('dp', 'space'), pairs)  11.8 us
    ppermute x6, waiting for transfers between devices, swap(): return lax.ppermute(x, 'space', [(i, i ^ bit) for i in range(n)])  11.3 us
    ppermute x12, waiting for transfers between devices, exchange(): return lax.ppermute(x, ('dp', 'space'), pairs)  8.76 us
    ppermute x6, starting transfers between devices, swap(): return lax.ppermute(x, 'space', [(i, i ^ bit) for i in range(n)])  8.62 us
    ppermute x3, waiting for transfers between devices, add_far(): lax.ppermute(far_sum, 'dp', line([(1, 0), (2, 3)]))  6.56 us
    ppermute x3, starting transfers between devices, add_far(): lax.ppermute(far_sum, 'dp', line([(1, 0), (2, 3)]))  3.88 us
  transfers between devices with their start and end apart: 33, of which 14 were waited for; matrix products, arithmetic and copies ran while one was open for 0% of the time, Pallas kernels for 20%

profile of v6, /device:TPU:0, one launch (start us, length us, event | category | flops | bytes accessed | tf_op | source)
XLA Modules:
  0.0 92.7 jit_solution(3099057268507759277)
XLA Ops:
  2.2 3.0 %collective-permute-start = (bf16[400,256]{1,0:T(8,128)(2,1)S(1)}, bf16[400,256]{1,0:T(8,128)(2,1)S(1)}, u32[]{:S(2)}, u32[]{:S(2)}) collective-permute-start(bf16[400,256]{1,0:T(8,128)(2,1)S(1)} %get-tuple-element.98), channel_id=1, source_target_pairs={{0,1},{1,0},{2,3},{3,2},{4,5},{5,4},{6,7},{7,6},{8,9},{9,8},{10,11... | collective-permute-start | bytes 614408 | tf_op jit(solution)/shard_map/ppermute | solution.py:438
  5.2 1.5 %collective-permute-start.1 = (bf16[400,256]{1,0:T(8,128)(2,1)S(1)}, bf16[400,256]{1,0:T(8,128)(2,1)S(1)}, u32[]{:S(2)}, u32[]{:S(2)}) collective-permute-start(bf16[400,256]{1,0:T(8,128)(2,1)S(1)} %get-tuple-element.99), channel_id=1, source_target_pairs={{0,2},{1,3},{2,0},{3,1},{4,6},{5,7},{6,4},{7,5},{8,10},{9,11},{10,... | collective-permute-start | bytes 614408 | tf_op jit(solution)/shard_map/ppermute | solution.py:438
  6.7 4.4 %collective-permute-done.refs_2_ = bf16[400,256]{1,0:T(8,128)(2,1)S(1)} collective-permute-done((bf16[400,256]{1,0:T(8,128)(2,1)S(1)}, bf16[400,256]{1,0:T(8,128)(2,1)S(1)}, u32[]{:S(2)}, u32[]{:S(2)}) %collective-permute-start) | collective-permute-done | bytes 204832 | tf_op jit(solution)/shard_map/ppermute | solution.py:438
  11.1 5.0 %collective-permute-done.1.refs_3_ = bf16[400,256]{1,0:T(8,128)(2,1)S(1)} collective-permute-done((bf16[400,256]{1,0:T(8,128)(2,1)S(1)}, bf16[400,256]{1,0:T(8,128)(2,1)S(1)}, u32[]{:S(2)}, u32[]{:S(2)}) %collective-permute-start.1) | collective-permute-done | bytes 204832 | tf_op jit(solution)/shard_map/ppermute | solution.py:438
  16.1 2.0 %forward_1.1 = (f32[800,128]{1,0:T(8,128)S(1)}, bf16[800,128]{1,0:T(8,128)(2,1)S(1)}, bf16[1600,256]{1,0:T(8,128)(2,1)S(1)}, f32[8,128]{1,0:T(8,128)S(1)}) custom-call(bf16[3,9,256,128]{3,2,1,0:T(8,128)(2,1)S(1)} %copy-done, bf16[400,256]{1,0:T(8,128)(2,1)S(1)} %get-tuple-element.97.refs_1_, bf16[400,256]{1,0:T(8,128)(2,1)S(1)} %collective-permute-done.refs_2_, ...), custom_call_target="tpu_custom_call" | custom-call | flops 1150000000 | bytes 1024 | tf_op jit(solution)/shard_map/forward_1/pallas_call | solution.py:39
  18.1 1.3 %collective-permute-start.4 = (bf16[800,128]{1,0:T(8,128)(2,1)S(1)}, bf16[800,128]{1,0:T(8,128)(2,1)S(1)}, u32[]{:S(2)}, u32[]{:S(2)}) collective-permute-start(bf16[800,128]{1,0:T(8,128)(2,1)S(1)} %get-tuple-element.106), channel_id=1, source_target_pairs={{0,1},{1,0},{2,3},{3,2},{4,6},{5,7},{6,4},{7,5},{8,9},{9,8},{10,11... | collective-permute-start | bytes 614408 | tf_op jit(solution)/shard_map/ppermute | solution.py:94
  19.4 2.5 %forward_0.1 = (f32[800,128]{1,0:T(8,128)S(1)}, bf16[800,128]{1,0:T(8,128)(2,1)S(1)}, f32[8,128]{1,0:T(8,128)S(1)}) custom-call(bf16[3,9,256,128]{3,2,1,0:T(8,128)(2,1)S(1)} %copy-done, bf16[400,256]{1,0:T(8,128)(2,1)S(1)} %get-tuple-element.97.refs_1_, bf16[400,256]{1,0:T(8,128)(2,1)S(1)} %collective-permute-done.refs_2_, ...), custom_call_target="tpu_custom_call" | custom-call | flops 1150000000 | bytes 1024 | tf_op jit(solution)/shard_map/forward_0/pallas_call | solution.py:39
  23.9 2.2 %collective-permute-start.7 = (bf16[400,128]{1,0:T(8,128)(2,1)S(1)}, bf16[400,128]{1,0:T(8,128)(2,1)S(1)}, u32[]{:S(2)}, u32[]{:S(2)}) collective-permute-start(bf16[400,128]{1,0:T(8,128)(2,1)S(1)} %get-tuple-element.115), channel_id=1, source_target_pairs={{0,2},{1,3},{2,0},{3,1},{4,5},{5,4},{6,7},{7,6},{8,10},{9,11},{10,... | collective-permute-start | bytes 307208 | tf_op jit(solution)/shard_map/ppermute | solution.py:94
  26.1 1.6 %forward_2.1 = (f32[800,128]{1,0:T(8,128)S(1)}, bf16[800,128]{1,0:T(8,128)(2,1)S(1)}, f32[8,128]{1,0:T(8,128)S(1)}) custom-call(bf16[3,9,256,128]{3,2,1,0:T(8,128)(2,1)S(1)} %copy-done, bf16[400,256]{1,0:T(8,128)(2,1)S(1)} %get-tuple-element.97.refs_1_, bf16[400,256]{1,0:T(8,128)(2,1)S(1)} %collective-permute-done.refs_2_, ...), custom_call_target="tpu_custom_call" | custom-call | flops 1150000000 | bytes 1024 | tf_op jit(solution)/shard_map/forward_2/pallas_call | solution.py:39
  31.2 2.7 %collective-permute-done.6.refs_1_ = bf16[800,128]{1,0:T(8,128)(2,1)S(1)} collective-permute-done((bf16[800,128]{1,0:T(8,128)(2,1)S(1)}, bf16[800,128]{1,0:T(8,128)(2,1)S(1)}, u32[]{:S(2)}, u32[]{:S(2)}) %collective-permute-start.6) | collective-permute-done | bytes 204832 | tf_op jit(solution)/shard_map/ppermute | solution.py:94
  34.4 1.8 %collective-permute-start.12 = (bf16[400,128]{1,0:T(8,128)(2,1)S(1)}, bf16[400,128]{1,0:T(8,128)(2,1)S(1)}, u32[]{:S(2)}, u32[]{:S(2)}) collective-permute-start(bf16[400,128]{1,0:T(8,128)(2,1)S(1)} %get-tuple-element.130.refs_0_), channel_id=1, source_target_pairs={{0,2},{1,3},{2,0},{3,1},{4,5},{5,4},{6,7},{7,6},{8,10},{9,11},{10,... | collective-permute-start | bytes 307208 | tf_op jit(solution)/shard_map/ppermute | solution.py:94
  36.8 2.2 %collective-permute-done.8.refs_1_ = bf16[400,128]{1,0:T(8,128)(2,1)S(1)} collective-permute-done((bf16[400,128]{1,0:T(8,128)(2,1)S(1)}, bf16[400,128]{1,0:T(8,128)(2,1)S(1)}, u32[]{:S(2)}, u32[]{:S(2)}) %collective-permute-start.8) | collective-permute-done | bytes 102432 | tf_op jit(solution)/shard_map/ppermute | solution.py:94
  39.9 1.3 %collective-permute-done.12.refs_1_ = bf16[400,128]{1,0:T(8,128)(2,1)S(1)} collective-permute-done((bf16[400,128]{1,0:T(8,128)(2,1)S(1)}, bf16[400,128]{1,0:T(8,128)(2,1)S(1)}, u32[]{:S(2)}, u32[]{:S(2)}) %collective-permute-start.12) | collective-permute-done | bytes 102432 | tf_op jit(solution)/shard_map/ppermute | solution.py:94
  42.1 1.6 %weight_grad_1.1 = (f32[1168,128]{1,0:T(8,128)S(1)}, bf16[1168,128]{1,0:T(8,128)(2,1)S(1)}, bf16[1600,384]{1,0:T(8,128)(2,1)S(1)}, f32[8,128]{1,0:T(8,128)S(1)}) custom-call(bf16[800,128]{1,0:T(8,128)(2,1)S(1)} %get-tuple-element.128.refs_0_, bf16[800,128]{1,0:T(8,128)(2,1)S(1)} %collective-permute-done.11.refs_1_, ...), custom_call_target="tpu_custom_call" | custom-call | flops 1150000000 | bytes 1024 | tf_op jit(solution)/shard_map/weight_grad_1/pallas_call | solution.py:39
  45.4 3.7 %collective-permute-start.19 = (bf16[1184,128]{1,0:T(8,128)(2,1)S(1)}, bf16[1184,128]{1,0:T(8,128)(2,1)S(1)}, u32[]{:S(2)}, u32[]{:S(2)}) collective-permute-start(bf16[1184,128]{1,0:T(8,128)(2,1)S(1)} %get-tuple-element.148), channel_id=1, source_target_pairs={{0,8},{4,12},{24,16},{28,20},{1,9},{5,13},{25,17},{29,21},{2,10},{... | collective-permute-start | bytes 909320 | tf_op jit(solution)/shard_map/ppermute | solution.py:571
  49.0 1.9 %weight_grad_0.1 = (f32[1168,128]{1,0:T(8,128)S(1)}, bf16[1168,128]{1,0:T(8,128)(2,1)S(1)}, bf16[1600,384]{1,0:T(8,128)(2,1)S(1)}, f32[8,128]{1,0:T(8,128)S(1)}) custom-call(bf16[800,128]{1,0:T(8,128)(2,1)S(1)} %get-tuple-element.135.refs_0_, bf16[800,128]{1,0:T(8,128)(2,1)S(1)} %collective-permute-done.14.refs_1_, ...), custom_call_target="tpu_custom_call" | custom-call | flops 1150000000 | bytes 1024 | tf_op jit(solution)/shard_map/weight_grad_0/pallas_call | solution.py:39
  52.8 2.0 %collective-permute-start.21 = (bf16[1184,128]{1,0:T(8,128)(2,1)S(1)}, bf16[1184,128]{1,0:T(8,128)(2,1)S(1)}, u32[]{:S(2)}, u32[]{:S(2)}) collective-permute-start(bf16[1184,128]{1,0:T(8,128)(2,1)S(1)} %get-tuple-element.151), channel_id=1, source_target_pairs={{0,8},{4,12},{24,16},{28,20},{1,9},{5,13},{25,17},{29,21},{2,10},{... | collective-permute-start | bytes 909320 | tf_op jit(solution)/shard_map/ppermute | solution.py:571
  56.8 7.4 %collective-permute-start.18 = (bf16[912,128]{1,0:T(8,128)(2,1)S(1)}, bf16[912,128]{1,0:T(8,128)(2,1)S(1)}, u32[]{:S(2)}, u32[]{:S(2)}) collective-permute-start(bf16[912,128]{1,0:T(8,128)(2,1)S(1)} %get-tuple-element.147), channel_id=1, source_target_pairs={{0,8},{4,12},{24,16},{28,20},{1,9},{5,13},{25,17},{29,21},{2,10},{... | collective-permute-start | bytes 700424 | tf_op jit(solution)/shard_map/ppermute | solution.py:571
  64.2 2.9 %input_grad.1 = (f32[1600,256]{1,0:T(8,128)S(1)}, f32[8,128]{1,0:T(8,128)S(1)}) custom-call(bf16[3,9,256,128]{3,2,1,0:T(8,128)(2,1)S(1)} %copy-done, bf16[1600,384]{1,0:T(8,128)(2,1)S(1)} %get-tuple-element.152.refs_1_, bf16[1600,384]{1,0:T(8,128)(2,1)S(1)} %get-tuple-element.153.refs_2_, bf16[1600,384]{1,0:T(8,128)(2,1)S(1)} %get-tuple-element.154.refs_3_, ...), custom_call_target="tpu_custom_call" | custom-call | flops 57500000 | bytes 1024 | tf_op jit(solution)/shard_map/input_grad/pallas_call | solution.py:39
  71.6 1.6 %collective-permute-start.25 = (bf16[400,256]{1,0:T(8,128)(2,1)S(1)}, bf16[400,256]{1,0:T(8,128)(2,1)S(1)}, u32[]{:S(2)}, u32[]{:S(2)}) collective-permute-start(bf16[400,256]{1,0:T(8,128)(2,1)S(1)} %get-tuple-element.170), channel_id=1, source_target_pairs={{0,1},{1,0},{2,3},{3,2},{4,5},{5,4},{6,7},{7,6},{8,9},{9,8},{10,11... | collective-permute-start | bytes 614408 | tf_op jit(solution)/shard_map/ppermute | solution.py:438
  73.9 4.6 %collective-permute-done.23.refs_1_ = bf16[1184,128]{1,0:T(8,128)(2,1)S(1)} collective-permute-done((bf16[1184,128]{1,0:T(8,128)(2,1)S(1)}, bf16[1184,128]{1,0:T(8,128)(2,1)S(1)}, u32[]{:S(2)}, u32[]{:S(2)}) %collective-permute-start.23) | collective-permute-done | bytes 303136 | tf_op jit(solution)/shard_map/ppermute | solution.py:583
  78.6 1.7 %collective-permute-start.27 = (bf16[400,256]{1,0:T(8,128)(2,1)S(1)}, bf16[400,256]{1,0:T(8,128)(2,1)S(1)}, u32[]{:S(2)}, u32[]{:S(2)}) collective-permute-start(bf16[400,256]{1,0:T(8,128)(2,1)S(1)} %get-tuple-element.172), channel_id=1, source_target_pairs={{0,3},{1,2},{2,1},{3,0},{4,7},{5,6},{6,5},{7,4},{8,11},{9,10},{10,... | collective-permute-start | bytes 614408 | tf_op jit(solution)/shard_map/ppermute | solution.py:438
  83.4 1.9 %collective-permute-done.27.refs_3_ = bf16[400,256]{1,0:T(8,128)(2,1)S(1)} collective-permute-done((bf16[400,256]{1,0:T(8,128)(2,1)S(1)}, bf16[400,256]{1,0:T(8,128)(2,1)S(1)}, u32[]{:S(2)}, u32[]{:S(2)}) %collective-permute-start.27) | collective-permute-done | bytes 204832 | tf_op jit(solution)/shard_map/ppermute | solution.py:438
  87.3 1.9 %collective-permute-done.28.refs_1_ = bf16[912,128]{1,0:T(8,128)(2,1)S(1)} collective-permute-done((bf16[912,128]{1,0:T(8,128)(2,1)S(1)}, bf16[912,128]{1,0:T(8,128)(2,1)S(1)}, u32[]{:S(2)}, u32[]{:S(2)}) %collective-permute-start.28) | collective-permute-done | bytes 233504 | tf_op jit(solution)/shard_map/ppermute | solution.py:583
  (86 shorter events, 28.9 us)
Async XLA Ops:
  2.2 8.9 %collective-permute-start = (bf16[400,256]{1,0:T(8,128)(2,1)S(1)}, bf16[400,256]{1,0:T(8,128)(2,1)S(1)}, u32[]{:S(2)}, u32[]{:S(2)}) collective-permute-start(bf16[400,256]{1,0:T(8,128)(2,1)S(1)} %get-tuple-element.98), channel_id=1, source_target_pairs={{0,1},{1,0},{2,3},{3,2},{4,5},{5,4},{6,7},{7,6},{8,9},{9,8},{10,11... | collective-permute-start | bytes 614408 | tf_op jit(solution)/shard_map/ppermute | solution.py:438
  5.2 10.9 %collective-permute-start.1 = (bf16[400,256]{1,0:T(8,128)(2,1)S(1)}, bf16[400,256]{1,0:T(8,128)(2,1)S(1)}, u32[]{:S(2)}, u32[]{:S(2)}) collective-permute-start(bf16[400,256]{1,0:T(8,128)(2,1)S(1)} %get-tuple-element.99), channel_id=1, source_target_pairs={{0,2},{1,3},{2,0},{3,1},{4,6},{5,7},{6,4},{7,5},{8,10},{9,11},{10,... | collective-permute-start | bytes 614408 | tf_op jit(solution)/shard_map/ppermute | solution.py:438
  6.7 9.4 %collective-permute-start.2 = (bf16[400,256]{1,0:T(8,128)(2,1)S(1)}, bf16[400,256]{1,0:T(8,128)(2,1)S(1)}, u32[]{:S(2)}, u32[]{:S(2)}) collective-permute-start(bf16[400,256]{1,0:T(8,128)(2,1)S(1)} %get-tuple-element.100), channel_id=1, source_target_pairs={{0,3},{1,2},{2,1},{3,0},{4,7},{5,6},{6,5},{7,4},{8,11},{9,10},{10,... | collective-permute-start | bytes 614408 | tf_op jit(solution)/shard_map/ppermute | solution.py:438
  21.8 6.0 %collective-permute-start.3 = (bf16[800,128]{1,0:T(8,128)(2,1)S(1)}, bf16[800,128]{1,0:T(8,128)(2,1)S(1)}, u32[]{:S(2)}, u32[]{:S(2)}) collective-permute-start(bf16[800,128]{1,0:T(8,128)(2,1)S(1)} %get-tuple-element.104), channel_id=1, source_target_pairs={{0,1},{1,0},{2,3},{3,2},{4,6},{5,7},{6,4},{7,5},{8,9},{9,8},{10,11... | collective-permute-start | bytes 614408 | tf_op jit(solution)/shard_map/ppermute | solution.py:94
  23.9 5.9 %collective-permute-start.7 = (bf16[400,128]{1,0:T(8,128)(2,1)S(1)}, bf16[400,128]{1,0:T(8,128)(2,1)S(1)}, u32[]{:S(2)}, u32[]{:S(2)}) collective-permute-start(bf16[400,128]{1,0:T(8,128)(2,1)S(1)} %get-tuple-element.115), channel_id=1, source_target_pairs={{0,2},{1,3},{2,0},{3,1},{4,5},{5,4},{6,7},{7,6},{8,10},{9,11},{10,... | collective-permute-start | bytes 307208 | tf_op jit(solution)/shard_map/ppermute | solution.py:94
  27.7 6.1 %collective-permute-start.6 = (bf16[800,128]{1,0:T(8,128)(2,1)S(1)}, bf16[800,128]{1,0:T(8,128)(2,1)S(1)}, u32[]{:S(2)}, u32[]{:S(2)}) collective-permute-start(bf16[800,128]{1,0:T(8,128)(2,1)S(1)} %get-tuple-element.113), channel_id=1, source_target_pairs={{0,1},{1,0},{2,3},{3,2},{4,6},{5,7},{6,4},{7,5},{8,9},{9,8},{10,11... | collective-permute-start | bytes 614408 | tf_op jit(solution)/shard_map/ppermute | solution.py:94
  27.9 6.4 %collective-permute-start.5 = (bf16[400,128]{1,0:T(8,128)(2,1)S(1)}, bf16[400,128]{1,0:T(8,128)(2,1)S(1)}, u32[]{:S(2)}, u32[]{:S(2)}) collective-permute-start(bf16[400,128]{1,0:T(8,128)(2,1)S(1)} %get-tuple-element.111), channel_id=1, source_target_pairs={{0,2},{1,3},{2,0},{3,1},{4,5},{5,4},{6,7},{7,6},{8,10},{9,11},{10,... | collective-permute-start | bytes 307208 | tf_op jit(solution)/shard_map/ppermute | solution.py:94
  30.0 6.2 %collective-permute-start.9 = (bf16[400,128]{1,0:T(8,128)(2,1)S(1)}, bf16[400,128]{1,0:T(8,128)(2,1)S(1)}, u32[]{:S(2)}, u32[]{:S(2)}) collective-permute-start(bf16[400,128]{1,0:T(8,128)(2,1)S(1)} %get-tuple-element.123.refs_0_), channel_id=1, source_target_pairs={{0,2},{1,3},{2,0},{3,1},{4,5},{5,4},{6,7},{7,6},{8,10},{9,11},{10,... | collective-permute-start | bytes 307208 | tf_op jit(solution)/shard_map/ppermute | solution.py:94
  34.4 6.8 %collective-permute-start.12 = (bf16[400,128]{1,0:T(8,128)(2,1)S(1)}, bf16[400,128]{1,0:T(8,128)(2,1)S(1)}, u32[]{:S(2)}, u32[]{:S(2)}) collective-permute-start(bf16[400,128]{1,0:T(8,128)(2,1)S(1)} %get-tuple-element.130.refs_0_), channel_id=1, source_target_pairs={{0,2},{1,3},{2,0},{3,1},{4,5},{5,4},{6,7},{7,6},{8,10},{9,11},{10,... | collective-permute-start | bytes 307208 | tf_op jit(solution)/shard_map/ppermute | solution.py:94
  36.2 5.8 %collective-permute-start.11 = (bf16[800,128]{1,0:T(8,128)(2,1)S(1)}, bf16[800,128]{1,0:T(8,128)(2,1)S(1)}, u32[]{:S(2)}, u32[]{:S(2)}) collective-permute-start(bf16[800,128]{1,0:T(8,128)(2,1)S(1)} %get-tuple-element.128.refs_0_), channel_id=1, source_target_pairs={{0,1},{1,0},{2,3},{3,2},{4,6},{5,7},{6,4},{7,5},{8,9},{9,8},{10,11... | collective-permute-start | bytes 614408 | tf_op jit(solution)/shard_map/ppermute | solution.py:94
  41.2 7.8 %collective-permute-start.14 = (bf16[800,128]{1,0:T(8,128)(2,1)S(1)}, bf16[800,128]{1,0:T(8,128)(2,1)S(1)}, u32[]{:S(2)}, u32[]{:S(2)}) collective-permute-start(bf16[800,128]{1,0:T(8,128)(2,1)S(1)} %get-tuple-element.135.refs_0_), channel_id=1, source_target_pairs={{0,1},{1,0},{2,3},{3,2},{4,6},{5,7},{6,4},{7,5},{8,9},{9,8},{10,11... | collective-permute-start | bytes 614408 | tf_op jit(solution)/shard_map/ppermute | solution.py:94
  43.9 7.1 %collective-permute-start.13 = (bf16[800,128]{1,0:T(8,128)(2,1)S(1)}, bf16[800,128]{1,0:T(8,128)(2,1)S(1)}, u32[]{:S(2)}, u32[]{:S(2)}) collective-permute-start(bf16[800,128]{1,0:T(8,128)(2,1)S(1)} %get-tuple-element.134.refs_0_), channel_id=1, source_target_pairs={{0,1},{1,0},{2,3},{3,2},{4,6},{5,7},{6,4},{7,5},{8,9},{9,8},{10,11... | collective-permute-start | bytes 614408 | tf_op jit(solution)/shard_map/ppermute | solution.py:94
  45.4 10.7 %collective-permute-start.19 = (bf16[1184,128]{1,0:T(8,128)(2,1)S(1)}, bf16[1184,128]{1,0:T(8,128)(2,1)S(1)}, u32[]{:S(2)}, u32[]{:S(2)}) collective-permute-start(bf16[1184,128]{1,0:T(8,128)(2,1)S(1)} %get-tuple-element.148), channel_id=1, source_target_pairs={{0,8},{4,12},{24,16},{28,20},{1,9},{5,13},{25,17},{29,21},{2,10},{... | collective-permute-start | bytes 909320 | tf_op jit(solution)/shard_map/ppermute | solution.py:571
  52.8 14.4 %collective-permute-start.21 = (bf16[1184,128]{1,0:T(8,128)(2,1)S(1)}, bf16[1184,128]{1,0:T(8,128)(2,1)S(1)}, u32[]{:S(2)}, u32[]{:S(2)}) collective-permute-start(bf16[1184,128]{1,0:T(8,128)(2,1)S(1)} %get-tuple-element.151), channel_id=1, source_target_pairs={{0,8},{4,12},{24,16},{28,20},{1,9},{5,13},{25,17},{29,21},{2,10},{... | collective-permute-start | bytes 909320 | tf_op jit(solution)/shard_map/ppermute | solution.py:571
  56.1 11.9 %collective-permute-start.20 = (bf16[1184,128]{1,0:T(8,128)(2,1)S(1)}, bf16[1184,128]{1,0:T(8,128)(2,1)S(1)}, u32[]{:S(2)}, u32[]{:S(2)}) collective-permute-start(bf16[1184,128]{1,0:T(8,128)(2,1)S(1)} %get-tuple-element.150.refs_0_), channel_id=1, source_target_pairs={{8,16},{12,20},{16,8},{20,12},{9,17},{13,21},{17,9},{21,13},{10,18... | collective-permute-start | bytes 909320 | tf_op jit(solution)/shard_map/ppermute | solution.py:576
  56.8 12.6 %collective-permute-start.18 = (bf16[912,128]{1,0:T(8,128)(2,1)S(1)}, bf16[912,128]{1,0:T(8,128)(2,1)S(1)}, u32[]{:S(2)}, u32[]{:S(2)}) collective-permute-start(bf16[912,128]{1,0:T(8,128)(2,1)S(1)} %get-tuple-element.147), channel_id=1, source_target_pairs={{0,8},{4,12},{24,16},{28,20},{1,9},{5,13},{25,17},{29,21},{2,10},{... | collective-permute-start | bytes 700424 | tf_op jit(solution)/shard_map/ppermute | solution.py:571
  68.1 10.5 %collective-permute-start.23 = (bf16[1184,128]{1,0:T(8,128)(2,1)S(1)}, bf16[1184,128]{1,0:T(8,128)(2,1)S(1)}, u32[]{:S(2)}, u32[]{:S(2)}) collective-permute-start(bf16[1184,128]{1,0:T(8,128)(2,1)S(1)} %get-tuple-element.162.refs_0_), channel_id=1, source_target_pairs={{8,0},{12,4},{16,24},{20,28},{9,1},{13,5},{17,25},{21,29},{10,2},{... | collective-permute-start | bytes 909320 | tf_op jit(solution)/shard_map/ppermute | solution.py:583
  69.5 11.7 %collective-permute-start.22 = (bf16[912,128]{1,0:T(8,128)(2,1)S(1)}, bf16[912,128]{1,0:T(8,128)(2,1)S(1)}, u32[]{:S(2)}, u32[]{:S(2)}) collective-permute-start(bf16[912,128]{1,0:T(8,128)(2,1)S(1)} %get-tuple-element.161.refs_0_), channel_id=1, source_target_pairs={{8,16},{12,20},{16,8},{20,12},{9,17},{13,21},{17,9},{21,13},{10,18... | collective-permute-start | bytes 700424 | tf_op jit(solution)/shard_map/ppermute | solution.py:576
  70.3 16.1 %collective-permute-start.29 = (bf16[1184,128]{1,0:T(8,128)(2,1)S(1)}, bf16[1184,128]{1,0:T(8,128)(2,1)S(1)}, u32[]{:S(2)}, u32[]{:S(2)}) collective-permute-start(bf16[1184,128]{1,0:T(8,128)(2,1)S(1)} %get-tuple-element.176.refs_0_), channel_id=1, source_target_pairs={{8,0},{12,4},{16,24},{20,28},{9,1},{13,5},{17,25},{21,29},{10,2},{... | collective-permute-start | bytes 909320 | tf_op jit(solution)/shard_map/ppermute | solution.py:583
  71.6 11.8 %collective-permute-start.25 = (bf16[400,256]{1,0:T(8,128)(2,1)S(1)}, bf16[400,256]{1,0:T(8,128)(2,1)S(1)}, u32[]{:S(2)}, u32[]{:S(2)}) collective-permute-start(bf16[400,256]{1,0:T(8,128)(2,1)S(1)} %get-tuple-element.170), channel_id=1, source_target_pairs={{0,1},{1,0},{2,3},{3,2},{4,5},{5,4},{6,7},{7,6},{8,9},{9,8},{10,11... | collective-permute-start | bytes 614408 | tf_op jit(solution)/shard_map/ppermute | solution.py:438
  73.2 10.1 %collective-permute-start.26 = (bf16[400,256]{1,0:T(8,128)(2,1)S(1)}, bf16[400,256]{1,0:T(8,128)(2,1)S(1)}, u32[]{:S(2)}, u32[]{:S(2)}) collective-permute-start(bf16[400,256]{1,0:T(8,128)(2,1)S(1)} %get-tuple-element.171), channel_id=1, source_target_pairs={{0,2},{1,3},{2,0},{3,1},{4,6},{5,7},{6,4},{7,5},{8,10},{9,11},{10,... | collective-permute-start | bytes 614408 | tf_op jit(solution)/shard_map/ppermute | solution.py:438
  78.6 6.7 %collective-permute-start.27 = (bf16[400,256]{1,0:T(8,128)(2,1)S(1)}, bf16[400,256]{1,0:T(8,128)(2,1)S(1)}, u32[]{:S(2)}, u32[]{:S(2)}) collective-permute-start(bf16[400,256]{1,0:T(8,128)(2,1)S(1)} %get-tuple-element.172), channel_id=1, source_target_pairs={{0,3},{1,2},{2,1},{3,0},{4,7},{5,6},{6,5},{7,4},{8,11},{9,10},{10,... | collective-permute-start | bytes 614408 | tf_op jit(solution)/shard_map/ppermute | solution.py:438
  81.3 8.0 %collective-permute-start.28 = (bf16[912,128]{1,0:T(8,128)(2,1)S(1)}, bf16[912,128]{1,0:T(8,128)(2,1)S(1)}, u32[]{:S(2)}, u32[]{:S(2)}) collective-permute-start(bf16[912,128]{1,0:T(8,128)(2,1)S(1)} %get-tuple-element.175.refs_0_), channel_id=1, source_target_pairs={{8,0},{12,4},{16,24},{20,28},{9,1},{13,5},{17,25},{21,29},{10,2},{... | collective-permute-start | bytes 700424 | tf_op jit(solution)/shard_map/ppermute | solution.py:583
  83.4 6.0 %collective-permute-start.31 = (bf16[1184,128]{1,0:T(8,128)(2,1)S(1)}, bf16[1184,128]{1,0:T(8,128)(2,1)S(1)}, u32[]{:S(2)}, u32[]{:S(2)}) collective-permute-start(bf16[1184,128]{1,0:T(8,128)(2,1)S(1)} %get-tuple-element.182.refs_2_), channel_id=1, source_target_pairs={{0,4},{4,0},{8,12},{12,8},{16,20},{20,16},{24,28},{28,24},{1,5},{5... | collective-permute-start | bytes 909320 | tf_op jit(solution)/shard_map/ppermute | solution.py:612
  (13 other events, 43.9 us)
